TPU v7x, 256 devices: a whole 4x4x8 slice. The times are simulated.
256 devices in a mesh: row: 4 (over x), col: 64 (over z, y, core).
Axes of the slice: x: 4, y: 4, z: 8, core: 2. Of those that a mesh axis runs over, the one named last changes fastest.
Arguments:
- sigma_trail: float32 [16384, 16384], P('row', 'col'), as said below
- panel_one: float32 [16384, 256], P(('row', 'col')), may hold values from -0.046875 to 0.046875
- panel_zero: float32 [16384, 256], P(('row', 'col')), may hold values from -0.046875 to 0.046875
- link: float32 [256, 256], replicated, may hold values from -0.375 to 0.375
- diag_one: float32 [256, 256], replicated, as said below
- diag_zero: float32 [256, 256], replicated, as said below
Outputs:
- sigma_s1: float32 [16384, 256], P(('row', 'col'))
- sigma_11: float32 [256, 256], replicated
- sigma_s0: float32 [16384, 256], P(('row', 'col'))
- sigma_10: float32 [256, 256], replicated
- sigma_00: float32 [256, 256], replicated
Inputs may be any that keep to these rules, and one draw needn't show every extreme that they name: `sigma_trail`: symmetric once its rows and columns are both put back in the global order. `diag_one`: lower triangular, diagonal entries between 1 and 2. `diag_zero`: lower triangular, diagonal entries between 1 and 2.
All inputs are finite; a program needn't handle non-finite values.
Results may differ from a plain program's by a relative error of at most 0.000075.
Values sent between devices are 32-bit elements; how exact they have to be, the bound alone decides.
No kernel may reach another device: no remote copies, remote signals or barrier semaphores. Data moves between devices by JAX's collectives and lax.ppermute only.
A program may use at most 64 MiB of HBM per device.

v0:
```python
import jax
import jax.numpy as jnp
from jax import lax
from jax.sharding import PartitionSpec as P


def from_partner(block, axis, distance):
    count = lax.axis_size(axis)
    route = []
    for low in range(count):
        high = low | 1 << distance
        if high != low and high < count:
            route += [(low, high), (high, low)]
    return lax.ppermute(block, axis, route)


def spread(value, axis, root):
    mine = lax.axis_index(axis) == root
    return lax.psum(jnp.where(mine, value, jnp.zeros_like(value)), axis)


def matmul(left, right):
    return jnp.dot(left, right, precision=lax.Precision.HIGHEST, preferred_element_type=jnp.float32)


def normalize(panel, factor):
    return lax.linalg.triangular_solve(factor, panel, left_side=False, lower=True)


def inverse_block(factor):
    size_here = factor.shape[0]
    inverse = lax.linalg.triangular_solve(
        factor, jnp.eye(size_here, dtype=jnp.float32), left_side=True, lower=True
    )
    return matmul(inverse.T, inverse)


def body(sigma_trail, panel_one, panel_zero, link, diag_one, diag_zero):
    rows_count = lax.axis_size("row")
    col_index = lax.axis_index("col")

    def tile_of(hat):
        current = hat
        for bit in range(rows_count.bit_length() - 1):
            partner = from_partner(current, "col", bit)
            upper = jnp.bitwise_and(jnp.right_shift(col_index, bit), 1)
            current = jnp.where(
                upper == 0,
                jnp.concatenate([current, partner], axis=0),
                jnp.concatenate([partner, current], axis=0),
            )
        return spread(current, "row", col_index % rows_count)

    def reduce_rows(tile):
        return lax.psum_scatter(matmul(sigma_trail, tile), "col", scatter_dimension=0, tiled=True)

    def contract(hat):
        tile = tile_of(hat)
        return (reduce_rows(tile), tile, None)

    hat_one = normalize(panel_one, diag_one)
    hat_zero = normalize(panel_zero, diag_zero)
    hat_link = normalize(link, diag_zero)
    product_one, tile_one, band_one = contract(hat_one)
    sigma_s1 = -product_one
    corner = matmul(hat_one.T, product_one)
    sigma_11 = inverse_block(diag_one) + lax.psum(corner, ("row", "col"))
    product_zero = contract(hat_zero)[0]
    sigma_s0 = -(matmul(sigma_s1, hat_link) + product_zero)
    cross, own = lax.psum(
        (matmul(sigma_s1.T, hat_zero), matmul(hat_zero.T, sigma_s0)), ("row", "col")
    )
    sigma_10 = -(matmul(sigma_11, hat_link) + cross)
    sigma_00 = inverse_block(diag_zero) - matmul(hat_link.T, sigma_10) - own
    return (sigma_s1, sigma_11, sigma_s0, sigma_10, sigma_00)


def solution(mesh):
    in_specs = (P("row", "col"), P(("row", "col"), None), P(("row", "col"), None), P(), P(), P())
    out_specs = (P(("row", "col"), None), P(), P(("row", "col"), None), P(), P())
    return jax.shard_map(body, mesh=mesh, in_specs=in_specs, out_specs=out_specs, check_vma=False)
```

profile of v0, /device:TPU:8, one launch (start us, length us, event | category | flops | bytes accessed | tf_op | source)
XLA Modules:
  0.0 701.2 jit_solution(14444991664241312083)
XLA Ops:
  8.3 4.0 while.9
  8.9 1.4 bitcast_dynamic-update-slice_fusion.4
  10.9 1.4 bitcast_dynamic-update-slice_fusion.4
  12.3 19.7 %custom-call.9 = f32[2,128,128]{1,2,0:T(8,128)S(1)} custom-call(f32[2,128,128]{2,1,0:T(8,128)S(1)} %get-tuple-element.30), custom_call_target="InvertDiagBlocksLowerTriangular" | custom-call | tf_op jit(solution)/shard_map/triangular_solve | solution.py:27
  35.3 4.0 while.10
  35.9 1.4 bitcast_dynamic-update-slice_fusion.5
  37.9 1.4 bitcast_dynamic-update-slice_fusion.5
  39.3 19.7 %custom-call.12 = f32[2,128,128]{1,2,0:T(8,128)S(1)} custom-call(f32[2,128,128]{2,1,0:T(8,128)S(1)} %get-tuple-element.43), custom_call_target="InvertDiagBlocksLowerTriangular" | custom-call | tf_op jit(solution)/shard_map/triangular_solve/custom-call.1 | solution.py:27
  61.8 2.3 collective-permute-start.3
  65.0 3.4 collective-permute-done.3
  69.1 1.5 collective-permute-done.1
  71.6 50.5 %all-reduce.7.cloned.1.call-done = (f32[256,256]{1,0:T(8,128)}, f32[256,256]{1,0:T(8,128)}) async-done(((f32[256,256]{1,0:T(8,128)}, f32[256,256]{1,0:T(8,128)}), (f32[256,256]{1,0:T(8,128)}, f32[256,256]{1,0:T(8,128)})) %all-reduce.7.cloned.1.call-update) | async-done | bytes 524304 | tf_op jit(solution)/shard_map/psum | solution.py:19
  122.1 11.0 %convolution_bitcast_fusion.1 = f32[4096,256]{0,1:T(8,128)} fusion(f32[256,256]{1,0:T(8,128)} %get-tuple-element.76, f32[4096,256]{1,0:T(8,128)} %param.10), kind=kOutput, calls=%fused_computation.5 | convolution fusion | flops 3221225472 | bytes 8650752 | tf_op jit(solution)/shard_map/dot_general | solution.py:23
  133.0 5.6 copy.16
  139.6 7.6 %convolution_bitcast_fusion = f32[4096,256]{1,0:T(8,128)} fusion(f32[256,256]{1,0:T(8,128)S(1)} %copy-done.2, f32[4096,256]{1,0:T(8,128)} %param.10), kind=kOutput, calls=%fused_computation.4 | convolution fusion | flops 3221225472 | bytes 8650752 | tf_op jit(solution)/shard_map/dot_general | solution.py:23
  149.7 132.8 %reduce-scatter.7.cloned.1.call-done = f32[64,256]{1,0:T(8,128)} async-done(((f32[4096,256]{1,0:T(8,128)}), f32[64,256]{1,0:T(8,128)}) %reduce-scatter.7.cloned.1.call-update) | async-done | bytes 65552
  284.5 144.9 %reduce-scatter.5.cloned.1.call-done = f32[64,256]{1,0:T(8,128)} async-done(((f32[4096,256]{1,0:T(8,128)}), f32[64,256]{1,0:T(8,128)}) %reduce-scatter.5.cloned.1.call-update) | async-done | bytes 65552 | tf_op jit(solution)/shard_map/reduce_scatter | solution.py:55
  429.4 1.2 fusion.2
  430.6 1.1 fusion.44
  431.7 2.0 fusion.40
  435.7 253.8 %all-reduce.5.cloned.1.call-done = (f32[256,256]{1,0:T(8,128)}, f32[256,256]{1,0:T(8,128)}, f32[256,256]{1,0:T(8,128)}) async-done(((f32[256,256]{1,0:T(8,128)}, f32[256,256]{1,0:T(8,128)}, f32[256,256]{1,0:T(8,128)}), (f32[256,256]{1,0:T(8,128)}, f32[256,256]{1,0:T(8,128)}, f32[256,256]{1,0:T(8,128)})) %all-reduce.5.cloned.1.call-update) | async-done | bytes 786448 | tf_op jit(solution)/shard_map/psum | solution.py:67
  689.5 1.5 convolution_add_fusion.1
  691.1 1.5 fusion.1
  692.5 2.1 fusion
  (64 shorter events, 19.4 us)
Async XLA Ops:
  7.2 114.9 %all-reduce.7.cloned.1.call-start = ((), (), s32[]{:S(2)}) async-start(), calls=%async_computation.5 | async-start | bytes 1048576 | tf_op jit(solution)/shard_map/psum | solution.py:19
  34.2 27.6 %collective-permute-start.2 = (f32[64,256]{1,0:T(8,128)S(1)}, f32[64,256]{1,0:T(8,128)S(1)}, u32[]{:S(2)}, u32[]{:S(2)}) collective-permute-start(f32[64,256]{1,0:T(8,128)S(1)} %pad_maximum_fusion.5), channel_id=1, source_target_pairs={{0,1},{1,0},{2,3},{3,2},{4,5},{5,4},{6,7},{7,6},{8,9},{9,8},{10,11... | collective-permute-start | bytes 196616 | tf_op jit(solution)/shard_map/ppermute | solution.py:14
  61.2 2.9 collective-permute-start
  61.8 6.6 collective-permute-start.3
  64.1 6.5 collective-permute-start.1
  71.3 211.1 %reduce-scatter.7.cloned.1.call-start = ((), (), s32[]{:S(2)}) async-start(), calls=%async_computation.3 | async-start | bytes 4259840
  138.7 0.9 copy-start.2
  138.7 290.7 %reduce-scatter.5.cloned.1.call-start = ((), (), s32[]{:S(2)}) async-start(), calls=%async_computation.2 | async-start | bytes 4259840 | tf_op jit(solution)/shard_map/reduce_scatter | solution.py:55
  147.2 1.0 copy-start.3
  147.2 542.3 %all-reduce.5.cloned.1.call-start = ((), (), s32[]{:S(2)}) async-start(), calls=%async_computation.4 | async-start | bytes 1572864 | tf_op jit(solution)/shard_map/psum | solution.py:67
  430.6 264.1 %copy-start.4 = (f32[64,256]{1,0:T(8,128)}, f32[64,256]{1,0:T(8,128)S(1)}, u32[]{:S(2)}) copy-start(f32[64,256]{1,0:T(8,128)S(1)} %fusion.2) | copy-start | bytes 196612
  691.1 3.6 copy-start
  692.5 2.2 copy-start.1
Sparse Core Ops, SparseCore 0:
  71.4 50.5 all-reduce.6
  138.8 143.5 reduce-scatter.6
  287.1 142.1 reduce-scatter.4
  435.6 253.8 all-reduce.4
where the time goes:
time: 702 us; the launch traced here: 701 us
  waiting for transfers between devices  587 us (84%)
  other arithmetic  42.8 us (6%)
  matrix products  36.7 us (5%)
  local copies, waits for them, and re-layouts  16.2 us (2%)
  between operations  14.1 us (2%)
    psum x1, waiting for transfers between devices, body(): sigma_11 = inverse_block(diag_one) + lax.psum(corner, ('row', 'col'))  254 us
    reduce_scatter x1, waiting for transfers between devices, reduce_rows(): lax.psum_scatter(matmul(sigma_trail, tile), 'col', scatter_dimension=0, t...  145 us
    unnamed x5, waiting for transfers between devices  133 us
    psum x1, waiting for transfers between devices, spread(): return lax.psum(jnp.where(mine, value, jnp.zeros_like(value)), axis)  50.5 us
    another operation x7, other arithmetic, normalize(): lax.linalg.triangular_solve(factor, panel, left_side=False, lower=True)  41.3 us
    dot_general x10, matrix products, matmul(): jnp.dot(left, right, precision=lax.Precision.HIGHEST, preferred_element_t...  29.7 us
  transfers between devices with their start and end apart: 8, of which 6 were waited for; matrix products, arithmetic and copies ran while one was open for 6% of the time, Pallas kernels for 0%

commit v1 on v0

v1 whole, which is shorter than its diff:
```python
import jax
import jax.numpy as jnp
from jax import lax
from jax.experimental import pallas as pl
from jax.experimental.pallas import tpu as pltpu
from jax.sharding import Mesh, PartitionSpec as P

F32 = jnp.float32
BF16 = jnp.bfloat16
AXES = ("x", "z", "y", "s")
NX, NY, NZ = 4, 4, 8
B = 256
Q = 64
HALF = 128


def device(x, y, z, s):
    return (x % NX) * 64 + (z % NZ) * 8 + (y % NY) * 2 + s


def send(block, move):
    pairs = [
        (device(x, y, z, s), device(*move(x, y, z, s)))
        for x in range(NX)
        for z in range(NZ)
        for y in range(NY)
        for s in range(2)
    ]
    return lax.ppermute(block, AXES, pairs)


def to_core(block):
    return send(block, lambda x, y, z, s: (x, y, z, 1 - s))


def along_y(block):
    return send(block, lambda x, y, z, s: (x, y + 1 - 2 * s, z, s))


def along_z(block):
    return send(block, lambda x, y, z, s: (x, y, z + 1 - 2 * s, s))


SLOTS = ((0, 3, 1, 2), (0, 1, 3, 2))


def swap(block, axis, turn):
    def move(x, y, z, s):
        apart = SLOTS[s][2 - turn]
        return (x ^ apart, y, z, s) if axis == "x" else (x, y ^ apart, z, s)

    return send(block, move)


def gather_four(piece, axis):
    def far(d):
        return send(piece, lambda x, y, z, s: (x ^ d, y, z, s) if axis == "x" else (x, y ^ d, z, s))

    return jnp.stack([piece, far(1), far(2), far(3)])


def after(value, *earlier):
    return lax.optimization_barrier((value, earlier))[0]


def split(value):
    high = value.astype(BF16)
    return high, (value - high.astype(F32)).astype(BF16)


def dot3(left, right, dims):
    lh, ll = split(left)
    rh, rl = split(right)
    d = (dims, ((), ()))
    out = lax.dot_general(lh, rh, d, preferred_element_type=F32)
    out += lax.dot_general(ll, rh, d, preferred_element_type=F32)
    return out + lax.dot_general(lh, rl, d, preferred_element_type=F32)


NN = ((1,), (0,))
TN = ((0,), (0,))


def fill_left(ref, row, place, value):
    deep = ref.shape[1] // 3
    high, low = split(value)
    m, k = value.shape
    ref[row : row + m, place : place + k] = high
    ref[row : row + m, deep + place : deep + place + k] = low
    ref[row : row + m, 2 * deep + place : 2 * deep + place + k] = high


def fill_right(ref, place, column, value):
    deep = ref.shape[0] // 3
    high, low = split(value)
    k, n = value.shape
    ref[place : place + k, column : column + n] = high
    ref[deep + place : deep + place + k, column : column + n] = high
    ref[2 * deep + place : 2 * deep + place + k, column : column + n] = low


def product(left, right):
    return jnp.dot(left, right, preferred_element_type=F32)


def exact(left, right):
    return jnp.dot(left, right, precision=lax.Precision.HIGHEST, preferred_element_type=F32)


def params(limit=16):
    return pltpu.CompilerParams(vmem_limit_bytes=limit * 1024 * 1024)


def cost(flops, moved):
    return pl.CostEstimate(flops=flops, bytes_accessed=moved, transcendentals=0)


VMEM = pl.BlockSpec(memory_space=pltpu.VMEM)
SMEM = pl.BlockSpec(memory_space=pltpu.SMEM)
HBM = pl.BlockSpec(memory_space=pltpu.HBM)
WIDE = 6 * B
SLAB = (NY, 2, Q, B)


def slab_product(at, step, own, other, even, odd, left, right, slabs, sems):
    y, s, slab = at[1], at[3], at[4 + step]
    copies = [
        pltpu.make_async_copy(ref.at[slab], slabs.at[n], sems.at[n]) for n, ref in enumerate((own, other))
    ]
    for copy in copies:
        copy.start()
    depth = even.shape[0] * Q
    for n, ref in enumerate((even, odd)):
        for panel in range(2):
            fill_right(right, n * depth, panel * B, ref[:, panel].reshape(depth, B))
    near = lax.rem(y + 3 + 2 * s, NY)
    for o in range(2):
        copies[o].wait()
        for n, first in enumerate((y, near)):
            blocks = [
                slabs[o, lax.rem(first + 2 * d, NY), core]
                for d in range(2)
                for core in (s, 1 - s)[: depth // 128]
            ]
            fill_left(left, o * B, n * depth, jnp.concatenate(blocks, axis=0).T)
    return product(left[...], right[...])


def slab_scratch(even):
    deep = 6 * even.shape[0] * Q
    return [
        pltpu.VMEM((2 * B, deep), BF16),
        pltpu.VMEM((deep, 2 * B), BF16),
        pltpu.VMEM((2,) + SLAB, F32),
        pltpu.SemaphoreType.DMA((2,)),
    ]


def multiply(place, step, sigma, other, even, odd, total=None):
    totals = [] if total is None else [total]

    def kernel(at, own_ref, other_ref, even_ref, odd_ref, *refs):
        s = at[3]
        out = refs[len(totals)]
        value = slab_product(at, step, own_ref, other_ref, even_ref, odd_ref, *refs[len(totals) + 1 :])
        for o, tile in enumerate((s, 1 - s)):
            part = value[o * B : (o + 1) * B]
            out[tile] = part if total is None else part + refs[0][tile]

    return pl.pallas_call(
        kernel,
        in_specs=[SMEM, HBM, HBM] + [VMEM] * (2 + len(totals)),
        out_specs=VMEM,
        out_shape=jax.ShapeDtypeStruct((2, B, 2 * B), F32),
        scratch_shapes=slab_scratch(even),
        input_output_aliases={5: 0} if totals else {},
        compiler_params=params(30),
        cost_estimate=cost(3 << 28, 2 << 20),
        name="multiply",
    )(place, sigma, other, even, odd, *totals)


N = 3 * B // 32


def last_kernel(at, own, other, even, odd, total, weights, pieces, whole, t_all, t_right, *scratch):
    x, y, s = at[2], at[1], at[3]
    value = slab_product(at, 4, own, other, even, odd, *scratch)
    for o, tile in enumerate((s, 1 - s)):
        t_all[tile] = total[tile] + value[o * B : (o + 1) * B]
    fill_right(t_right, 0, 0, t_all[...].reshape(2 * B, 2 * B))
    top = product(weights[:B], t_right[...])
    whole[:B] = top[:, :B]
    whole[B : 2 * B] = top[:, B:]
    whole[2 * B :] = product(weights[B:], t_right[:, B:])
    for core in range(2):
        for slot, apart in enumerate(SLOTS[core]):
            p = x ^ apart
            for sub, further in enumerate(SLOTS[core]):
                start = (core * NX + p) * (NY * N) + (y ^ further) * N
                pieces[core ^ s, slot, sub * N : (sub + 1) * N] = whole[pl.ds(pl.multiple_of(start, 8), N), :]
            rows = pl.ds(pl.multiple_of((p // 2 * 2 + core) * Q, 8), Q)
            for panel in range(2):
                start = NY * N + panel * Q
                pieces[core ^ s, slot, start : start + Q] = t_all[lax.rem(p, 2), rows, panel * B : (panel + 1) * B]


def last(place, sigma, other, even, odd, total, weights):
    return pl.pallas_call(
        last_kernel,
        in_specs=[SMEM, HBM, HBM] + [VMEM] * 4,
        out_specs=VMEM,
        out_shape=jax.ShapeDtypeStruct((2, NX, NY * N + 2 * Q, B), F32),
        scratch_shapes=[
            pltpu.VMEM((3 * B, B), F32),
            pltpu.VMEM((2, B, 2 * B), F32),
            pltpu.VMEM((WIDE, 2 * B), BF16),
        ]
        + slab_scratch(even),
        compiler_params=params(30),
        cost_estimate=cost(1 << 30, 2 << 20),
        name="last",
    )(place, sigma, other, even, odd, total, weights)


def invert_kernel(_, one_ref, zero_ref, out_one, out_zero, one, zero, sems):
    copies = [pltpu.make_async_copy(one_ref, one, sems.at[0]), pltpu.make_async_copy(zero_ref, zero, sems.at[1])]
    for copy in copies:
        copy.start()
    for copy in copies:
        copy.wait()
    row = lax.broadcasted_iota(jnp.int32, (HALF, HALF), 0)
    col = lax.broadcasted_iota(jnp.int32, (HALF, HALF), 1)
    blocks, inverses = [], []
    for ref in (one, zero):
        for k in range(2):
            block = ref[k * HALF : (k + 1) * HALF, k * HALF : (k + 1) * HALF]
            blocks.append(block)
            inverses.append(jnp.where(row == col, 1.0 / block, 0.0))
    below = jnp.logical_and(row == col + 1, row % 2 == 1)
    scales = [jnp.sum(i, axis=1, keepdims=True) for i in inverses]
    inverses = [
        i - r * jnp.where(below, b, 0.0) * jnp.sum(i, axis=0, keepdims=True)
        for b, i, r in zip(blocks, inverses, scales)
    ]
    size = 2
    while size < HALF:
        below = jnp.logical_and(
            row // (2 * size) == col // (2 * size),
            jnp.logical_and((row // size) % 2 == 1, (col // size) % 2 == 0),
        )
        middles = [exact(jnp.where(below, b, 0.0), i) for b, i in zip(blocks, inverses)]
        inverses = [i - exact(i, m) for i, m in zip(inverses, middles)]
        size *= 2
    for n, (ref, out) in enumerate(((one, out_one), (zero, out_zero))):
        top, bottom = inverses[2 * n], inverses[2 * n + 1]
        out[:HALF, :HALF] = top
        out[HALF:, HALF:] = bottom
        out[:HALF, HALF:] = jnp.zeros((HALF, HALF), F32)
        out[HALF:, :HALF] = -exact(bottom, exact(ref[HALF:, :HALF], top))


def invert(place, one, zero):
    tile = jax.ShapeDtypeStruct((B, B), F32)
    return pl.pallas_call(
        invert_kernel,
        in_specs=[SMEM, HBM, HBM],
        out_specs=[VMEM, VMEM],
        out_shape=[tile, tile],
        scratch_shapes=[pltpu.VMEM((B, B), F32), pltpu.VMEM((B, B), F32), pltpu.SemaphoreType.DMA((2,))],
        compiler_params=params(),
        cost_estimate=cost(1 << 32, 1 << 20),
        name="invert",
    )(place, one, zero)


def constants_kernel(x1_ref, x0_ref, link, z_terms, zt_terms, base):
    x1, x0 = x1_ref[...], x0_ref[...]
    hl = dot3(link[...], x0, NN)
    top = -dot3(x1, hl, NN)
    none = jnp.zeros((B, B), F32)
    for row, column, block in ((0, 0, x1), (0, B, top), (B, 0, none), (B, B, x0)):
        fill_right(z_terms, row, column, block)
        fill_left(zt_terms, column, row, block.T)
    inv1 = dot3(x1, x1, TN)
    cross = dot3(inv1, hl, NN)
    base[:B] = inv1
    base[B : 2 * B] = -cross
    base[2 * B :] = dot3(x0, x0, TN) + dot3(hl, cross, TN)


def constants(x1, x0, link):
    return pl.pallas_call(
        constants_kernel,
        in_specs=[VMEM] * 3,
        out_specs=[VMEM] * 3,
        out_shape=[
            jax.ShapeDtypeStruct((WIDE, 2 * B), BF16),
            jax.ShapeDtypeStruct((2 * B, WIDE), BF16),
            jax.ShapeDtypeStruct((3 * B, B), F32),
        ],
        compiler_params=params(),
        cost_estimate=cost(1 << 29, 3 << 20),
        name="constants",
    )(x1, x0, link)


def weigh_kernel(at, mine, others, weights, rows):
    x, y, s = at[2], at[1], at[3]
    for tile in range(2):
        for g in range(2):
            for core in range(2):
                near = (tile ^ lax.rem(x, 2)) * 2 + (g ^ lax.rem(y, 2))
                start = ((tile * 2 + g) * 2 + core) * Q
                for panel in range(2):
                    block = jnp.where(s == core, mine[near, panel], others[near, panel])
                    rows[start : start + Q, panel * B : (panel + 1) * B] = block
    fill_left(weights, 0, 0, rows[...].T)


def weigh(place, mine, others):
    return pl.pallas_call(
        weigh_kernel,
        in_specs=[SMEM] + [VMEM] * 2,
        out_specs=VMEM,
        out_shape=jax.ShapeDtypeStruct((2 * B, WIDE), BF16),
        scratch_shapes=[pltpu.VMEM((2 * B, 2 * B), F32)],
        compiler_params=params(),
        cost_estimate=cost(1 << 28, 3 << 20),
        name="weigh",
    )(place, mine, others)


def rows_kernel(a, b, z_terms, sigmas, left):
    for panel in range(2):
        rows = slice(NY * N + panel * Q, NY * N + (panel + 1) * Q)
        fill_left(left, 0, panel * B, a[rows] + b[rows])
    both = product(left[...], z_terms[...])
    sigmas[0] = -both[:, :B]
    sigmas[1] = -both[:, B:]


def rows(a, b, z_terms):
    return pl.pallas_call(
        rows_kernel,
        in_specs=[VMEM] * 3,
        out_specs=VMEM,
        out_shape=jax.ShapeDtypeStruct((2, Q, B), F32),
        scratch_shapes=[pltpu.VMEM((Q, WIDE), BF16)],
        compiler_params=params(),
        cost_estimate=cost(1 << 27, 2 << 20),
        name="rows",
    )(a, b, z_terms)


def finish_kernel(at, mine, other, z_terms, zt_terms, base, s11, s10, s00, whole, left, right):
    x, y, s = at[2], at[1], at[3]
    for core in range(2):

        def place_all(ref):
            for slot, apart in enumerate(SLOTS[core]):
                for b in range(NY):
                    start = (core * NX + (x ^ apart)) * (NY * N) + (y ^ b) * N
                    whole[pl.ds(pl.multiple_of(start, 8), N), :] = ref[slot, b]

        @pl.when(s == core)
        def _():
            place_all(mine)

        @pl.when(s != core)
        def _():
            place_all(other)

    crossed = whole[B : 2 * B]
    fill_left(left, 0, 0, whole[:B])
    fill_left(left, 0, B, crossed)
    fill_left(left, B, 0, crossed.T)
    fill_left(left, B, B, whole[2 * B :])
    fill_right(right, 0, 0, product(left[...], z_terms[...]))
    top = product(zt_terms[:B], right[...])
    s11[...] = top[:, :B] + base[:B]
    s10[...] = top[:, B:] + base[B : 2 * B]
    s00[...] = product(zt_terms[B:], right[:, B:]) + base[2 * B :]


def finish(place, mine, other, z_terms, zt_terms, base):
    tile = jax.ShapeDtypeStruct((B, B), F32)
    return pl.pallas_call(
        finish_kernel,
        in_specs=[SMEM] + [VMEM] * 5,
        out_specs=[VMEM] * 3,
        out_shape=[tile, tile, tile],
        scratch_shapes=[
            pltpu.VMEM((3 * B, B), F32),
            pltpu.VMEM((2 * B, WIDE), BF16),
            pltpu.VMEM((WIDE, 2 * B), BF16),
        ],
        compiler_params=params(),
        cost_estimate=cost(1 << 28, 3 << 20),
        name="finish",
    )(place, mine, other, z_terms, zt_terms, base)


def body(sigma, p1, p0, link, diag_one, diag_zero):
    x, y, z, s = (lax.axis_index(name).astype(jnp.int32) for name in ("x", "y", "z", "s"))
    way = 2 * s - 1
    place = jnp.stack([z, y, x, s] + [lax.rem(z + NZ + j * way, NZ) for j in range(5)])

    view = (NZ,) + SLAB
    own = jnp.stack([p1, p0])[None]
    a = jnp.concatenate([own, to_core(own)], axis=0)
    y2 = send(own, lambda x, y, z, s: (x, y + 2, z, s))
    a1 = along_z(a)
    b = jnp.concatenate([after(y2, a), to_core(y2)], axis=0)
    b1 = along_z(b)
    a2 = along_z(after(a1, b))

    sigma_other = to_core(after(sigma, b, a1)).reshape(view)
    sigma = sigma.reshape(view)
    even = jnp.concatenate([own, after(y2, a1)], axis=0)
    odd = along_y(even)
    b1, odd = after((b1, odd), b1, odd)
    b2 = along_z(b1)
    z1 = jnp.concatenate([a1, b1], axis=0)
    e1 = along_y(z1)
    pair = jnp.concatenate([own, jnp.where(y % 2 == s, odd[1:], odd[:1])], axis=0)
    a3 = along_z(after(a2, b1))
    crossed = send(after(pair, a2), lambda x, y, z, s: (x ^ 2, y, z, s))
    total = multiply(place, 0, sigma, sigma_other, even, odd)

    b2 = after(b2, total, a2)
    b3 = along_z(b2)
    z2 = jnp.concatenate([a2, b2], axis=0)
    e2 = along_y(z2)
    a3 = after(a3, b2)
    first = jnp.where(x // 2 == y % 2, pair, after(crossed, b2))
    second = send(first, lambda x, y, z, s: (x ^ 1, y, z, s))
    total = multiply(place, 1, sigma, sigma_other, z1, e1, total)

    b3 = after(b3, total, a3)
    z4 = along_z(jnp.concatenate([a3[:1], b3[:1]], axis=0))
    z3 = jnp.concatenate([a3, b3], axis=0)
    e3 = along_y(z3)
    mine = jnp.concatenate([first, after(second, b3)], axis=0)
    others = to_core(mine)
    total = multiply(place, 2, sigma, sigma_other, z2, e2, total)
    weights = weigh(place, mine, others)

    z4 = after(z4, total, weights)
    e4 = along_y(z4)
    total = multiply(place, 3, sigma, sigma_other, z3, e3, total)
    pieces = last(place, sigma, sigma_other, z4, e4, total, weights)

    part = pieces[0] + to_core(pieces[1])
    came = swap(part[2:], "x", 0)
    x1, x0 = invert(after(place, part), diag_one, diag_zero)
    part = part[:2] + after(came, x1, x0)
    came = swap(part[1], "x", 1)
    z_terms, zt_terms, base = constants(x1, x0, after(link, part))
    parts = (part[0], after(came, base))
    part = (parts[0][: NY * N] + parts[1][: NY * N]).reshape(NY, N, B)
    sigmas = rows(*parts, z_terms)

    part = part[:2] + swap(part[2:], "y", 0)
    part = after(part, sigmas)
    part = part[0] + swap(part[1], "y", 1)
    part = part + send(part, lambda x, y, z, s: (x, y, z ^ 1, s))
    a, b, c = (send(part, lambda x, y, z, s: (x, y, z ^ far, s)) for far in (2, 4, 6))
    part = (part + a) + (b + c)
    sigmas = send(sigmas, lambda x, y, z, s: (y % 2 * 2 + x % 2, y // 2 * 2 + x // 2, z, s))
    mine = gather_four(part, "y")
    pair = jnp.stack([mine, swap(mine, "x", 1)])
    mine = after(jnp.concatenate([pair, swap(pair, "x", 0)], axis=0), sigmas)
    s11, s10, s00 = finish(place, mine, to_core(mine), z_terms, zt_terms, base)
    return sigmas[0], s11, sigmas[1], s10, s00


def solution(mesh):
    mesh = Mesh(mesh.devices.reshape(NX, NZ, NY, 2), AXES)
    in_specs = (P("x", AXES[1:]), P(AXES, None), P(AXES, None), P(), P(), P())
    out_specs = (P(AXES, None), P(), P(AXES, None), P(), P())
    return jax.shard_map(body, mesh=mesh, in_specs=in_specs, out_specs=out_specs, check_vma=False)
```

time: 702 us -> 134 us (0.19)
  waiting for transfers between devices: 587 us -> 58.7 us
  other arithmetic: 42.8 us -> 1.31 us
  starting transfers between devices: 4.39 us -> 45.4 us
  matrix products: 36.7 us -> 0 us
  Pallas kernels: 0 us -> 23.4 us
  between operations: 14.1 us -> 1 us
  local copies, waits for them, and re-layouts: 16.2 us -> 3.24 us
    psum x2 -> x0, waiting for transfers between devices: 304 us -> none  [the longest x1 254 us: body(): sigma_11 = inverse_block(diag_one) + lax.psum(corner, ('row', 'col'))]
    reduce_scatter x1 -> x0, waiting for transfers between devices: 145 us -> none  [reduce_rows(): lax.psum_scatter(matmul(sigma_trail, tile), 'col', scatter_dimension=0, t...]
    unnamed x5 -> x0, waiting for transfers between devices: 133 us -> none
    ppermute x4 -> x35, waiting for transfers between devices: 4.89 us -> 58.7 us  [send(): return lax.ppermute(block, AXES, pairs)]
    ppermute x4 -> x35, starting transfers between devices: 3.82 us -> 45.4 us  [send(): return lax.ppermute(block, AXES, pairs)]
    another operation x7 -> x2, other arithmetic: 41.3 us -> 0.03 us  [body(): pair = jnp.stack([mine, swap(mine, 'x', 1)])]
    dot_general x10 -> x0, matrix products: 29.7 us -> none  [matmul(): jnp.dot(left, right, precision=lax.Precision.HIGHEST, preferred_element_t...]
    pallas_call x0 -> x10, Pallas kernels: none -> 23.4 us  [the longest x4 10.1 us: multiply(): pl.pallas_call(kernel, in_specs=[SMEM, HBM, HBM] + [VMEM] * (2 + len(tota...]
  transfers between devices with their start and end apart: 8 -> 35, of which waited for: 6 -> 24; matrix products, arithmetic and copies ran while one was open for 6% -> 1% of each run, Pallas kernels for 0% -> 13%
where the time goes in v1:
time: 134 us; the launch traced here: 133 us
  waiting for transfers between devices  58.7 us (44%)
  starting transfers between devices  45.4 us (34%)
  Pallas kernels  23.4 us (17%)
  local copies, waits for them, and re-layouts  3.24 us (2%)
    ppermute x35, waiting for transfers between devices, send(): return lax.ppermute(block, AXES, pairs)  58.7 us
    ppermute x35, starting transfers between devices, send(): return lax.ppermute(block, AXES, pairs)  45.4 us
    pallas_call x4, Pallas kernels, multiply(): pl.pallas_call(kernel, in_specs=[SMEM, HBM, HBM] + [VMEM] * (2 + len(tota...  10.1 us
    pallas_call x1, Pallas kernels, invert(): pl.pallas_call(invert_kernel, in_specs=[SMEM, HBM, HBM], out_specs=[VMEM,...  3.94 us
    pallas_call x1, Pallas kernels, last(): pl.pallas_call(last_kernel, in_specs=[SMEM, HBM, HBM] + [VMEM] * 4, out_s...  3.62 us
    pallas_call x1, Pallas kernels, finish(): pl.pallas_call(finish_kernel, in_specs=[SMEM] + [VMEM] * 5, out_specs=[VM...  3.13 us
  transfers between devices with their start and end apart: 35, of which 24 were waited for; matrix products, arithmetic and copies ran while one was open for 1% of the time, Pallas kernels for 13%

profile of v1, /device:TPU:8, one launch (start us, length us, event | category | flops | bytes accessed | tf_op | source)
XLA Modules:
  0.0 133.1 jit_solution(3618591266733239766)
XLA Ops:
  1.6 2.4 %collective-permute-start = (f32[1,2,64,256]{3,2,1,0:T(8,128)S(1)}, f32[1,2,64,256]{3,2,1,0:T(8,128)S(1)}, u32[]{:S(2)}, u32[]{:S(2)}) collective-permute-start(f32[1,2,64,256]{3,2,1,0:T(8,128)S(1)} %maximum_bitcast_fusion), channel_id=1, source_target_pairs={{0,4},{1,5},{2,6},{3,7},{4,0},{5,1},{6,2},{7,3},{8,12},{9,13},{10,... | collective-permute-start | bytes 393224 | tf_op jit(solution)/shard_map/ppermute | solution.py:29
  6.0 3.0 %collective-permute-done = f32[1,2,64,256]{3,2,1,0:T(8,128)S(1)} collective-permute-done((f32[1,2,64,256]{3,2,1,0:T(8,128)S(1)}, f32[1,2,64,256]{3,2,1,0:T(8,128)S(1)}, u32[]{:S(2)}, u32[]{:S(2)}) %collective-permute-start) | collective-permute-done | bytes 131104 | tf_op jit(solution)/shard_map/ppermute | solution.py:29
  10.8 3.5 %collective-permute-done.3 = f32[2,2,64,256]{3,2,1,0:T(8,128)S(1)} collective-permute-done((f32[2,2,64,256]{3,2,1,0:T(8,128)S(1)}, f32[2,2,64,256]{3,2,1,0:T(8,128)S(1)}, u32[]{:S(2)}, u32[]{:S(2)}) %collective-permute-start.3) | collective-permute-done | bytes 262176 | tf_op jit(solution)/shard_map/ppermute | solution.py:29
  16.3 5.6 %collective-permute-done.6 = f32[2,2,64,256]{3,2,1,0:T(8,128)S(1)} collective-permute-done((f32[2,2,64,256]{3,2,1,0:T(8,128)S(1)}, f32[2,2,64,256]{3,2,1,0:T(8,128)S(1)}, u32[]{:S(2)}, u32[]{:S(2)}) %collective-permute-start.6) | collective-permute-done | bytes 262176 | tf_op jit(solution)/shard_map/ppermute | solution.py:29
  22.0 2.8 %collective-permute-done.5 = f32[2,2,64,256]{3,2,1,0:T(8,128)S(1)} collective-permute-done((f32[2,2,64,256]{3,2,1,0:T(8,128)S(1)}, f32[2,2,64,256]{3,2,1,0:T(8,128)S(1)}, u32[]{:S(2)}, u32[]{:S(2)}) %collective-permute-start.5) | collective-permute-done | bytes 262176 | tf_op jit(solution)/shard_map/ppermute | solution.py:29
  24.7 3.0 %collective-permute-start.14 = (f32[2,2,64,256]{3,2,1,0:T(8,128)S(1)}, f32[2,2,64,256]{3,2,1,0:T(8,128)S(1)}, u32[]{:S(2)}, u32[]{:S(2)}) collective-permute-start(f32[2,2,64,256]{3,2,1,0:T(8,128)S(1)} %pad_maximum_fusion.2), channel_id=1, source_target_pairs={{0,128},{1,129},{2,130},{3,131},{4,132},{5,133},{6,134},{7,135},{8... | collective-permute-start | bytes 786440 | tf_op jit(solution)/shard_map/ppermute | solution.py:29
  32.8 2.6 %collective-permute-start.10 = (f32[2,2,64,256]{3,2,1,0:T(8,128)S(1)}, f32[2,2,64,256]{3,2,1,0:T(8,128)S(1)}, u32[]{:S(2)}, u32[]{:S(2)}) collective-permute-start(f32[2,2,64,256]{3,2,1,0:T(8,128)S(1)} %collective-permute-done.9), channel_id=1, source_target_pairs={{0,8},{1,57},{2,10},{3,59},{4,12},{5,61},{6,14},{7,63},{8,16},{9,1... | collective-permute-start | bytes 786440 | tf_op jit(solution)/shard_map/ppermute | solution.py:29
  37.5 2.6 %multiply.5.refs_0_ = f32[2,256,512]{2,1,0:T(8,128)S(1)} custom-call(s32[9]{0:T(128)S(1)} %stack.72.at._, f32[8,4,2,64,256]{4,3,2,1,0:T(8,128)S(1)} %bitcast.47, f32[8,4,2,64,256]{4,3,2,1,0:T(8,128)} %bitcast.13.other_ref.other, f32[4,2,64,256]{3,2,1,0:T(8,128)S(1)} %constant_dynamic-update-slice_fusion.2.even_ref, ...), custom_call_target="tpu_custom_call", output_to_operand_aliasing={{}: (5, {})} | custom-call | flops 805306368 | bytes 2097152 | tf_op jit(solution)/shard_map/multiply/pallas_call | solution.py:170
  45.9 2.6 %multiply.6.refs_0_ = f32[2,256,512]{2,1,0:T(8,128)S(1)} custom-call(s32[9]{0:T(128)S(1)} %stack.72.at._, f32[8,4,2,64,256]{4,3,2,1,0:T(8,128)S(1)} %bitcast.48, f32[8,4,2,64,256]{4,3,2,1,0:T(8,128)} %bitcast.13.other_ref.other, f32[4,2,64,256]{3,2,1,0:T(8,128)S(1)} %constant_dynamic-update-slice_fusion.4.even_ref, ...), custom_call_target="tpu_custom_call", output_to_operand_aliasing={{}: (5, {})} | custom-call | flops 805306368 | bytes 2097152 | tf_op jit(solution)/shard_map/multiply/pallas_call | solution.py:170
  51.7 3.0 %collective-permute-start.17 = (f32[2,2,64,256]{3,2,1,0:T(8,128)S(1)}, f32[2,2,64,256]{3,2,1,0:T(8,128)S(1)}, u32[]{:S(2)}, u32[]{:S(2)}) collective-permute-start(f32[2,2,64,256]{3,2,1,0:T(8,128)S(1)} %collective-permute-done.12.even), channel_id=1, source_target_pairs={{0,2},{1,7},{2,4},{3,1},{4,6},{5,3},{6,0},{7,5},{8,10},{9,15},{10,... | collective-permute-start | bytes 786440 | tf_op jit(solution)/shard_map/ppermute | solution.py:29
  54.7 2.6 %multiply.7.total = f32[2,256,512]{2,1,0:T(8,128)S(1)} custom-call(s32[9]{0:T(128)S(1)} %stack.72.at._, f32[8,4,2,64,256]{4,3,2,1,0:T(8,128)S(1)} %bitcast.49, f32[8,4,2,64,256]{4,3,2,1,0:T(8,128)} %bitcast.13.other_ref.other, f32[4,2,64,256]{3,2,1,0:T(8,128)S(1)} %constant_dynamic-update-slice_fusion.6.even_ref, ...), custom_call_target="tpu_custom_call", output_to_operand_aliasing={{}: (5, {})} | custom-call | flops 805306368 | bytes 2097152 | tf_op jit(solution)/shard_map/multiply/pallas_call | solution.py:170
  58.6 3.6 %last.1 = f32[2,4,224,256]{3,2,1,0:T(8,128)S(1)} custom-call(s32[9]{0:T(128)S(1)} %stack.72.at._, f32[8,4,2,64,256]{4,3,2,1,0:T(8,128)S(1)} %bitcast.50, f32[8,4,2,64,256]{4,3,2,1,0:T(8,128)} %bitcast.13.other_ref.other, f32[2,2,64,256]{3,2,1,0:T(8,128)S(1)} %collective-permute-done.12.even, f32[2,2,64,256]{3,2,1,0:T(8,128)S(1)} %collective-permute-done.17.odd, ...), custom_call_target="tpu_custom_call" | custom-call | flops 1073741824 | bytes 2097152 | tf_op jit(solution)/shard_map/last/pallas_call | solution.py:209
  62.4 2.5 %collective-permute-done.19 = f32[4,224,256]{2,1,0:T(8,128)S(1)} collective-permute-done((f32[4,224,256]{2,1,0:T(8,128)S(1)}, f32[4,224,256]{2,1,0:T(8,128)S(1)}, u32[]{:S(2)}, u32[]{:S(2)}) %collective-permute-start.19) | collective-permute-done | bytes 917536 | tf_op jit(solution)/shard_map/ppermute | solution.py:29
  66.1 3.9 %invert.1 = (f32[256,256]{1,0:T(8,128)S(1)}, f32[256,256]{1,0:T(8,128)S(1)}) custom-call(s32[9]{0:T(128)S(1)} %stack.72.at._, f32[256,256]{1,0:T(8,128)S(1)} %copy-done.1, f32[256,256]{1,0:T(8,128)S(1)} %copy-done.2), custom_call_target="tpu_custom_call" | custom-call | flops 4294967296 | bytes 1048576 | tf_op jit(solution)/shard_map/invert/pallas_call | solution.py:265
  70.1 3.6 %collective-permute-done.20 = f32[2,224,256]{2,1,0:T(8,128)S(1)} collective-permute-done((f32[2,224,256]{2,1,0:T(8,128)S(1)}, f32[2,224,256]{2,1,0:T(8,128)S(1)}, u32[]{:S(2)}, u32[]{:S(2)}) %collective-permute-start.20) | collective-permute-done | bytes 458784 | tf_op jit(solution)/shard_map/ppermute | solution.py:29
  76.5 4.8 %collective-permute-done.21.b = f32[224,256]{1,0:T(8,128)S(1)} collective-permute-done((f32[224,256]{1,0:T(8,128)S(1)}, f32[224,256]{1,0:T(8,128)S(1)}, u32[]{:S(2)}, u32[]{:S(2)}) %collective-permute-start.21) | collective-permute-done | bytes 229408 | tf_op jit(solution)/shard_map/ppermute | solution.py:29
  85.5 2.6 %collective-permute-start.24 = (f32[24,256]{1,0:T(8,128)S(1)}, f32[24,256]{1,0:T(8,128)S(1)}, u32[]{:S(2)}, u32[]{:S(2)}) collective-permute-start(f32[24,256]{1,0:T(8,128)S(1)} %slice_bitcast_fusion.7), channel_id=1, source_target_pairs={{0,6},{1,3},{2,4},{3,1},{4,2},{5,7},{6,0},{7,5},{8,14},{9,11},{10,... | collective-permute-start | bytes 73736 | tf_op jit(solution)/shard_map/ppermute | solution.py:29
  89.9 4.3 %collective-permute-done.25 = f32[24,256]{1,0:T(8,128)S(1)} collective-permute-done((f32[24,256]{1,0:T(8,128)S(1)}, f32[24,256]{1,0:T(8,128)S(1)}, u32[]{:S(2)}, u32[]{:S(2)}) %collective-permute-start.25) | collective-permute-done | bytes 24608 | tf_op jit(solution)/shard_map/ppermute | solution.py:29
  96.4 2.4 %collective-permute-start.28 = (f32[24,256]{1,0:T(8,128)S(1)}, f32[24,256]{1,0:T(8,128)S(1)}, u32[]{:S(2)}, u32[]{:S(2)}) collective-permute-start(f32[24,256]{1,0:T(8,128)S(1)} %add.64), channel_id=1, source_target_pairs={{0,48},{1,49},{2,50},{3,51},{4,52},{5,53},{6,54},{7,55},{8,56},{9,... | collective-permute-start | bytes 73736 | tf_op jit(solution)/shard_map/ppermute | solution.py:29
  105.2 3.9 %collective-permute-start.30 = (f32[24,256]{1,0:T(8,128)S(1)}, f32[24,256]{1,0:T(8,128)S(1)}, u32[]{:S(2)}, u32[]{:S(2)}) collective-permute-start(f32[24,256]{1,0:T(8,128)S(1)} %add_add_fusion), channel_id=1, source_target_pairs={{0,4},{1,5},{2,6},{3,7},{4,0},{5,1},{6,2},{7,3},{8,12},{9,13},{10,... | collective-permute-start | bytes 73736 | tf_op jit(solution)/shard_map/ppermute | solution.py:29
  113.6 5.3 %collective-permute-done.32 = f32[4,24,256]{2,1,0:T(8,128)S(1)} collective-permute-done((f32[4,24,256]{2,1,0:T(8,128)S(1)}, f32[4,24,256]{2,1,0:T(8,128)S(1)}, u32[]{:S(2)}, u32[]{:S(2)}) %collective-permute-start.32) | collective-permute-done | bytes 98336 | tf_op jit(solution)/shard_map/ppermute | solution.py:29
  119.0 4.0 %collective-permute-start.22 = (f32[2,64,256]{2,1,0:T(8,128)S(1)}, f32[2,64,256]{2,1,0:T(8,128)S(1)}, u32[]{:S(2)}, u32[]{:S(2)}) collective-permute-start(f32[2,64,256]{2,1,0:T(8,128)S(1)} %rows.1), channel_id=1, source_target_pairs={{0,0},{1,1},{2,128},{3,129},{4,4},{5,5},{6,132},{7,133},{8,8},{9,9... | collective-permute-start | bytes 393224 | tf_op jit(solution)/shard_map/ppermute | solution.py:29
  124.6 3.6 %collective-permute-done.22 = f32[2,64,256]{2,1,0:T(8,128)S(1)} collective-permute-done((f32[2,64,256]{2,1,0:T(8,128)S(1)}, f32[2,64,256]{2,1,0:T(8,128)S(1)}, u32[]{:S(2)}, u32[]{:S(2)}) %collective-permute-start.22) | collective-permute-done | bytes 131104 | tf_op jit(solution)/shard_map/ppermute | solution.py:29
  129.9 3.1 %finish.1 = (f32[256,256]{1,0:T(8,128)}, f32[256,256]{1,0:T(8,128)}, f32[256,256]{1,0:T(8,128)}) custom-call(s32[9]{0:T(128)S(1)} %stack.72.at._, f32[4,4,24,256]{3,2,1,0:T(8,128)S(1)} %pad_maximum_fusion.1.mine, f32[4,4,24,256]{3,2,1,0:T(8,128)S(1)} %collective-permute-done.34.other, bf16[1536,512]{1,0:T(8,128)(2,1)S(1)} %get-tuple-element.54.z_terms, ...), custom_call_target="tpu_custom_call" | custom-call | flops 268435456 | bytes 3145728 | tf_op jit(solution)/shard_map/finish/pallas_call | solution.py:388
  (99 shorter events, 50.8 us)
Async XLA Ops:
  1.6 7.4 %collective-permute-start = (f32[1,2,64,256]{3,2,1,0:T(8,128)S(1)}, f32[1,2,64,256]{3,2,1,0:T(8,128)S(1)}, u32[]{:S(2)}, u32[]{:S(2)}) collective-permute-start(f32[1,2,64,256]{3,2,1,0:T(8,128)S(1)} %maximum_bitcast_fusion), channel_id=1, source_target_pairs={{0,4},{1,5},{2,6},{3,7},{4,0},{5,1},{6,2},{7,3},{8,12},{9,13},{10,... | collective-permute-start | bytes 393224 | tf_op jit(solution)/shard_map/ppermute | solution.py:29
  4.0 10.3 %collective-permute-start.3 = (f32[2,2,64,256]{3,2,1,0:T(8,128)S(1)}, f32[2,2,64,256]{3,2,1,0:T(8,128)S(1)}, u32[]{:S(2)}, u32[]{:S(2)}) collective-permute-start(f32[2,2,64,256]{3,2,1,0:T(8,128)S(1)} %pad_maximum_fusion.4), channel_id=1, source_target_pairs={{0,8},{1,57},{2,10},{3,59},{4,12},{5,61},{6,14},{7,63},{8,16},{9,1... | collective-permute-start | bytes 786440 | tf_op jit(solution)/shard_map/ppermute | solution.py:29
  14.3 14.1 %collective-permute-start.4 = (f32[4096,256]{1,0:T(8,128)}, f32[4096,256]{1,0:T(8,128)}, u32[]{:S(2)}, u32[]{:S(2)}) collective-permute-start(f32[4096,256]{1,0:T(8,128)} %param.6), channel_id=1, source_target_pairs={{0,1},{1,0},{2,3},{3,2},{4,5},{5,4},{6,7},{7,6},{8,9},{9,8},{10,11... | collective-permute-start | bytes 12582920 | tf_op jit(solution)/shard_map/ppermute | solution.py:29
  14.3 7.6 %collective-permute-start.6 = (f32[2,2,64,256]{3,2,1,0:T(8,128)S(1)}, f32[2,2,64,256]{3,2,1,0:T(8,128)S(1)}, u32[]{:S(2)}, u32[]{:S(2)}) collective-permute-start(f32[2,2,64,256]{3,2,1,0:T(8,128)S(1)} %constant_dynamic-update-slice_fusion), channel_id=1, source_target_pairs={{0,8},{1,57},{2,10},{3,59},{4,12},{5,61},{6,14},{7,63},{8,16},{9,1... | collective-permute-start | bytes 786440 | tf_op jit(solution)/shard_map/ppermute | solution.py:29
  14.3 7.6 %collective-permute-start.7 = (f32[2,2,64,256]{3,2,1,0:T(8,128)S(1)}, f32[2,2,64,256]{3,2,1,0:T(8,128)S(1)}, u32[]{:S(2)}, u32[]{:S(2)}) collective-permute-start(f32[2,2,64,256]{3,2,1,0:T(8,128)S(1)} %pad_maximum_fusion.3.even_ref), channel_id=1, source_target_pairs={{0,2},{1,7},{2,4},{3,1},{4,6},{5,3},{6,0},{7,5},{8,10},{9,15},{10,... | collective-permute-start | bytes 786440 | tf_op jit(solution)/shard_map/ppermute | solution.py:29
  15.0 9.7 %collective-permute-start.5 = (f32[2,2,64,256]{3,2,1,0:T(8,128)S(1)}, f32[2,2,64,256]{3,2,1,0:T(8,128)S(1)}, u32[]{:S(2)}, u32[]{:S(2)}) collective-permute-start(f32[2,2,64,256]{3,2,1,0:T(8,128)S(1)} %collective-permute-done.3), channel_id=1, source_target_pairs={{0,8},{1,57},{2,10},{3,59},{4,12},{5,61},{6,14},{7,63},{8,16},{9,1... | collective-permute-start | bytes 786440 | tf_op jit(solution)/shard_map/ppermute | solution.py:29
  21.9 10.9 %collective-permute-start.9 = (f32[2,2,64,256]{3,2,1,0:T(8,128)S(1)}, f32[2,2,64,256]{3,2,1,0:T(8,128)S(1)}, u32[]{:S(2)}, u32[]{:S(2)}) collective-permute-start(f32[2,2,64,256]{3,2,1,0:T(8,128)S(1)} %collective-permute-done.6), channel_id=1, source_target_pairs={{0,8},{1,57},{2,10},{3,59},{4,12},{5,61},{6,14},{7,63},{8,16},{9,1... | collective-permute-start | bytes 786440 | tf_op jit(solution)/shard_map/ppermute | solution.py:29
  24.7 10.7 %collective-permute-start.14 = (f32[2,2,64,256]{3,2,1,0:T(8,128)S(1)}, f32[2,2,64,256]{3,2,1,0:T(8,128)S(1)}, u32[]{:S(2)}, u32[]{:S(2)}) collective-permute-start(f32[2,2,64,256]{3,2,1,0:T(8,128)S(1)} %pad_maximum_fusion.2), channel_id=1, source_target_pairs={{0,128},{1,129},{2,130},{3,131},{4,132},{5,133},{6,134},{7,135},{8... | collective-permute-start | bytes 786440 | tf_op jit(solution)/shard_map/ppermute | solution.py:29
  27.8 9.7 %collective-permute-start.11 = (f32[4,2,64,256]{3,2,1,0:T(8,128)S(1)}, f32[4,2,64,256]{3,2,1,0:T(8,128)S(1)}, u32[]{:S(2)}, u32[]{:S(2)}) collective-permute-start(f32[4,2,64,256]{3,2,1,0:T(8,128)S(1)} %constant_dynamic-update-slice_fusion.2.even_ref), channel_id=1, source_target_pairs={{0,2},{1,7},{2,4},{3,1},{4,6},{5,3},{6,0},{7,5},{8,10},{9,15},{10,... | collective-permute-start | bytes 1572872 | tf_op jit(solution)/shard_map/ppermute | solution.py:29
  28.4 7.7 %collective-permute-start.8 = (f32[2,2,64,256]{3,2,1,0:T(8,128)S(1)}, f32[2,2,64,256]{3,2,1,0:T(8,128)S(1)}, u32[]{:S(2)}, u32[]{:S(2)}) collective-permute-start(f32[2,2,64,256]{3,2,1,0:T(8,128)S(1)} %collective-permute-done.5), channel_id=1, source_target_pairs={{0,8},{1,57},{2,10},{3,59},{4,12},{5,61},{6,14},{7,63},{8,16},{9,1... | collective-permute-start | bytes 786440 | tf_op jit(solution)/shard_map/ppermute | solution.py:29
  32.8 7.7 %collective-permute-start.10 = (f32[2,2,64,256]{3,2,1,0:T(8,128)S(1)}, f32[2,2,64,256]{3,2,1,0:T(8,128)S(1)}, u32[]{:S(2)}, u32[]{:S(2)}) collective-permute-start(f32[2,2,64,256]{3,2,1,0:T(8,128)S(1)} %collective-permute-done.9), channel_id=1, source_target_pairs={{0,8},{1,57},{2,10},{3,59},{4,12},{5,61},{6,14},{7,63},{8,16},{9,1... | collective-permute-start | bytes 786440 | tf_op jit(solution)/shard_map/ppermute | solution.py:29
  35.4 7.2 %collective-permute-start.15 = (f32[2,2,64,256]{3,2,1,0:T(8,128)S(1)}, f32[2,2,64,256]{3,2,1,0:T(8,128)S(1)}, u32[]{:S(2)}, u32[]{:S(2)}) collective-permute-start(f32[2,2,64,256]{3,2,1,0:T(8,128)S(1)} %broadcast_select_fusion), channel_id=1, source_target_pairs={{0,64},{1,65},{2,66},{3,67},{4,68},{5,69},{6,70},{7,71},{8,72},{9,... | collective-permute-start | bytes 786440 | tf_op jit(solution)/shard_map/ppermute | solution.py:29
  36.2 9.7 %collective-permute-start.13 = (f32[4,2,64,256]{3,2,1,0:T(8,128)S(1)}, f32[4,2,64,256]{3,2,1,0:T(8,128)S(1)}, u32[]{:S(2)}, u32[]{:S(2)}) collective-permute-start(f32[4,2,64,256]{3,2,1,0:T(8,128)S(1)} %constant_dynamic-update-slice_fusion.4.even_ref), channel_id=1, source_target_pairs={{0,2},{1,7},{2,4},{3,1},{4,6},{5,3},{6,0},{7,5},{8,10},{9,15},{10,... | collective-permute-start | bytes 1572872 | tf_op jit(solution)/shard_map/ppermute | solution.py:29
  42.7 5.9 %collective-permute-start.16 = (f32[4,2,64,256]{3,2,1,0:T(8,128)S(1)}, f32[4,2,64,256]{3,2,1,0:T(8,128)S(1)}, u32[]{:S(2)}, u32[]{:S(2)}) collective-permute-start(f32[4,2,64,256]{3,2,1,0:T(8,128)S(1)} %pad_maximum_fusion.mine), channel_id=1, source_target_pairs={{0,1},{1,0},{2,3},{3,2},{4,5},{5,4},{6,7},{7,6},{8,9},{9,8},{10,11... | collective-permute-start | bytes 1572872 | tf_op jit(solution)/shard_map/ppermute | solution.py:29
  43.0 11.7 %collective-permute-start.18 = (f32[4,2,64,256]{3,2,1,0:T(8,128)S(1)}, f32[4,2,64,256]{3,2,1,0:T(8,128)S(1)}, u32[]{:S(2)}, u32[]{:S(2)}) collective-permute-start(f32[4,2,64,256]{3,2,1,0:T(8,128)S(1)} %constant_dynamic-update-slice_fusion.6.even_ref), channel_id=1, source_target_pairs={{0,2},{1,7},{2,4},{3,1},{4,6},{5,3},{6,0},{7,5},{8,10},{9,15},{10,... | collective-permute-start | bytes 1572872 | tf_op jit(solution)/shard_map/ppermute | solution.py:29
  44.1 7.7 %collective-permute-start.12 = (f32[2,2,64,256]{3,2,1,0:T(8,128)S(1)}, f32[2,2,64,256]{3,2,1,0:T(8,128)S(1)}, u32[]{:S(2)}, u32[]{:S(2)}) collective-permute-start(f32[2,2,64,256]{3,2,1,0:T(8,128)S(1)} %pad_maximum_fusion.5), channel_id=1, source_target_pairs={{0,8},{1,57},{2,10},{3,59},{4,12},{5,61},{6,14},{7,63},{8,16},{9,1... | collective-permute-start | bytes 786440 | tf_op jit(solution)/shard_map/ppermute | solution.py:29
  51.7 6.9 %collective-permute-start.17 = (f32[2,2,64,256]{3,2,1,0:T(8,128)S(1)}, f32[2,2,64,256]{3,2,1,0:T(8,128)S(1)}, u32[]{:S(2)}, u32[]{:S(2)}) collective-permute-start(f32[2,2,64,256]{3,2,1,0:T(8,128)S(1)} %collective-permute-done.12.even), channel_id=1, source_target_pairs={{0,2},{1,7},{2,4},{3,1},{4,6},{5,3},{6,0},{7,5},{8,10},{9,15},{10,... | collective-permute-start | bytes 786440 | tf_op jit(solution)/shard_map/ppermute | solution.py:29
  65.0 8.6 %collective-permute-start.20 = (f32[2,224,256]{2,1,0:T(8,128)S(1)}, f32[2,224,256]{2,1,0:T(8,128)S(1)}, u32[]{:S(2)}, u32[]{:S(2)}) collective-permute-start(f32[2,224,256]{2,1,0:T(8,128)S(1)} %slice.88), channel_id=1, source_target_pairs={{0,64},{1,193},{2,66},{3,195},{4,68},{5,197},{6,70},{7,199},{8,72}... | collective-permute-start | bytes 1376264 | tf_op jit(solution)/shard_map/ppermute | solution.py:29
  73.7 7.5 %collective-permute-start.21 = (f32[224,256]{1,0:T(8,128)S(1)}, f32[224,256]{1,0:T(8,128)S(1)}, u32[]{:S(2)}, u32[]{:S(2)}) collective-permute-start(f32[224,256]{1,0:T(8,128)S(1)} %get-tuple-element.61), channel_id=1, source_target_pairs={{0,192},{1,65},{2,194},{3,67},{4,196},{5,69},{6,198},{7,71},{8,200... | collective-permute-start | bytes 688136 | tf_op jit(solution)/shard_map/ppermute | solution.py:29
  94.2 7.7 %collective-permute-start.27 = (f32[24,256]{1,0:T(8,128)S(1)}, f32[24,256]{1,0:T(8,128)S(1)}, u32[]{:S(2)}, u32[]{:S(2)}) collective-permute-start(f32[24,256]{1,0:T(8,128)S(1)} %add.64), channel_id=1, source_target_pairs={{0,32},{1,33},{2,34},{3,35},{4,36},{5,37},{6,38},{7,39},{8,40},{9,... | collective-permute-start | bytes 73736 | tf_op jit(solution)/shard_map/ppermute | solution.py:29
  96.4 5.9 %collective-permute-start.28 = (f32[24,256]{1,0:T(8,128)S(1)}, f32[24,256]{1,0:T(8,128)S(1)}, u32[]{:S(2)}, u32[]{:S(2)}) collective-permute-start(f32[24,256]{1,0:T(8,128)S(1)} %add.64), channel_id=1, source_target_pairs={{0,48},{1,49},{2,50},{3,51},{4,52},{5,53},{6,54},{7,55},{8,56},{9,... | collective-permute-start | bytes 73736 | tf_op jit(solution)/shard_map/ppermute | solution.py:29
  112.9 5.9 %collective-permute-start.32 = (f32[4,24,256]{2,1,0:T(8,128)S(1)}, f32[4,24,256]{2,1,0:T(8,128)S(1)}, u32[]{:S(2)}, u32[]{:S(2)}) collective-permute-start(f32[4,24,256]{2,1,0:T(8,128)S(1)} %get-tuple-element.66), channel_id=1, source_target_pairs={{0,192},{1,65},{2,194},{3,67},{4,196},{5,69},{6,198},{7,71},{8,200... | collective-permute-start | bytes 294920 | tf_op jit(solution)/shard_map/ppermute | solution.py:29
  118.9 5.8 %collective-permute-start.33 = (f32[2,4,24,256]{3,2,1,0:T(8,128)S(1)}, f32[2,4,24,256]{3,2,1,0:T(8,128)S(1)}, u32[]{:S(2)}, u32[]{:S(2)}) collective-permute-start(f32[2,4,24,256]{3,2,1,0:T(8,128)S(1)} %pad_maximum_fusion.6), channel_id=1, source_target_pairs={{0,64},{1,193},{2,66},{3,195},{4,68},{5,197},{6,70},{7,199},{8,72}... | collective-permute-start | bytes 589832 | tf_op jit(solution)/shard_map/ppermute | solution.py:29
  119.0 9.3 %collective-permute-start.22 = (f32[2,64,256]{2,1,0:T(8,128)S(1)}, f32[2,64,256]{2,1,0:T(8,128)S(1)}, u32[]{:S(2)}, u32[]{:S(2)}) collective-permute-start(f32[2,64,256]{2,1,0:T(8,128)S(1)} %rows.1), channel_id=1, source_target_pairs={{0,0},{1,1},{2,128},{3,129},{4,4},{5,5},{6,132},{7,133},{8,8},{9,9... | collective-permute-start | bytes 393224 | tf_op jit(solution)/shard_map/ppermute | solution.py:29
  (15 other events, 56.1 us)

commit v2 on v1

--- a/solution.py
+++ b/solution.py
@@ -52,11 +52,12 @@
     return send(block, move)
 
 
-def gather_four(piece, axis):
-    def far(d):
-        return send(piece, lambda x, y, z, s: (x ^ d, y, z, s) if axis == "x" else (x, y ^ d, z, s))
-
-    return jnp.stack([piece, far(1), far(2), far(3)])
+def to_pair(block, far):
+    return send(block, lambda x, y, z, s: (x, y, ((z + NZ - s) % NZ ^ far) + s, s))
+
+
+def to_near(block):
+    return to_pair(block, 1)
 
 
 def after(value, *earlier):
@@ -183,7 +184,13 @@
 N = 3 * B // 32
 
 
-def last_kernel(at, own, other, even, odd, total, weights, pieces, whole, t_all, t_right, *scratch):
+def along(y, core, sub):
+    base = y if sub < 2 else y ^ SLOTS[core][2]
+    other = base ^ SLOTS[core][1]
+    return jnp.maximum(base, other) if sub % 2 else jnp.minimum(base, other)
+
+
+def last_kernel(at, own, other, even, odd, total, weights, corner, pieces, whole, t_all, t_right, *scratch):
     x, y, s = at[2], at[1], at[3]
     value = slab_product(at, 4, own, other, even, odd, *scratch)
     for o, tile in enumerate((s, 1 - s)):
@@ -196,21 +203,22 @@
     for core in range(2):
         for slot, apart in enumerate(SLOTS[core]):
             p = x ^ apart
-            for sub, further in enumerate(SLOTS[core]):
-                start = (core * NX + p) * (NY * N) + (y ^ further) * N
-                pieces[core ^ s, slot, sub * N : (sub + 1) * N] = whole[pl.ds(pl.multiple_of(start, 8), N), :]
+            for sub in range(NY):
+                start = (core * NX + p) * (NY * N) + along(y, core, sub) * N
+                corner[core ^ s, slot, sub] = whole[pl.ds(pl.multiple_of(start, 8), N), :]
             rows = pl.ds(pl.multiple_of((p // 2 * 2 + core) * Q, 8), Q)
-            for panel in range(2):
-                start = NY * N + panel * Q
-                pieces[core ^ s, slot, start : start + Q] = t_all[lax.rem(p, 2), rows, panel * B : (panel + 1) * B]
+            pieces[core ^ s, slot] = t_all[lax.rem(p, 2), rows, :]
 
 
 def last(place, sigma, other, even, odd, total, weights):
     return pl.pallas_call(
         last_kernel,
         in_specs=[SMEM, HBM, HBM] + [VMEM] * 4,
-        out_specs=VMEM,
-        out_shape=jax.ShapeDtypeStruct((2, NX, NY * N + 2 * Q, B), F32),
+        out_specs=[VMEM, VMEM],
+        out_shape=[
+            jax.ShapeDtypeStruct((2, NX, NY, N, B), F32),
+            jax.ShapeDtypeStruct((2, NX, Q, 2 * B), F32),
+        ],
         scratch_shapes=[
             pltpu.VMEM((3 * B, B), F32),
             pltpu.VMEM((2, B, 2 * B), F32),
@@ -332,9 +340,7 @@
 
 
 def rows_kernel(a, b, z_terms, sigmas, left):
-    for panel in range(2):
-        rows = slice(NY * N + panel * Q, NY * N + (panel + 1) * Q)
-        fill_left(left, 0, panel * B, a[rows] + b[rows])
+    fill_left(left, 0, 0, a[...] + b[...])
     both = product(left[...], z_terms[...])
     sigmas[0] = -both[:, :B]
     sigmas[1] = -both[:, B:]
@@ -359,9 +365,9 @@
 
         def place_all(ref):
             for slot, apart in enumerate(SLOTS[core]):
-                for b in range(NY):
-                    start = (core * NX + (x ^ apart)) * (NY * N) + (y ^ b) * N
-                    whole[pl.ds(pl.multiple_of(start, 8), N), :] = ref[slot, b]
+                for sub in range(NY):
+                    start = (core * NX + (x ^ apart)) * (NY * N) + along(y, core, sub) * N
+                    whole[pl.ds(pl.multiple_of(start, 8), N), :] = ref[slot, sub // 2, sub % 2]
 
         @pl.when(s == core)
         def _():
@@ -428,49 +434,50 @@
     crossed = send(after(pair, a2), lambda x, y, z, s: (x ^ 2, y, z, s))
     total = multiply(place, 0, sigma, sigma_other, even, odd)
 
-    b2 = after(b2, total, a2)
+    b2 = after(b2, a2)
     b3 = along_z(b2)
     z2 = jnp.concatenate([a2, b2], axis=0)
     e2 = along_y(z2)
     a3 = after(a3, b2)
     first = jnp.where(x // 2 == y % 2, pair, after(crossed, b2))
     second = send(first, lambda x, y, z, s: (x ^ 1, y, z, s))
-    total = multiply(place, 1, sigma, sigma_other, z1, e1, total)
-
-    b3 = after(b3, total, a3)
+
+    b3 = after(b3, a3, total)
     z4 = along_z(jnp.concatenate([a3[:1], b3[:1]], axis=0))
     z3 = jnp.concatenate([a3, b3], axis=0)
     e3 = along_y(z3)
     mine = jnp.concatenate([first, after(second, b3)], axis=0)
     others = to_core(mine)
+    total = multiply(place, 1, sigma, sigma_other, z1, e1, total)
+
+    z4, others, e2 = after((z4, others, e2), z4, others, total, e2)
+    e4 = along_y(z4)
     total = multiply(place, 2, sigma, sigma_other, z2, e2, total)
     weights = weigh(place, mine, others)
-
-    z4 = after(z4, total, weights)
-    e4 = along_y(z4)
     total = multiply(place, 3, sigma, sigma_other, z3, e3, total)
-    pieces = last(place, sigma, sigma_other, z4, e4, total, weights)
-
-    part = pieces[0] + to_core(pieces[1])
+    corner, pieces = last(place, sigma, sigma_other, z4, e4, total, weights)
+
+    part = corner[0] + to_core(corner[1])
     came = swap(part[2:], "x", 0)
+    q = pieces[0] + to_core(pieces[1])
     x1, x0 = invert(after(place, part), diag_one, diag_zero)
-    part = part[:2] + after(came, x1, x0)
+    part = part[:2] + after(came, x1, x0, q)
     came = swap(part[1], "x", 1)
     z_terms, zt_terms, base = constants(x1, x0, after(link, part))
-    parts = (part[0], after(came, base))
-    part = (parts[0][: NY * N] + parts[1][: NY * N]).reshape(NY, N, B)
-    sigmas = rows(*parts, z_terms)
-
+    part = part[0] + after(came, base)
+    q = q[:2] + swap(q[2:], "x", 0)
     part = part[:2] + swap(part[2:], "y", 0)
-    part = after(part, sigmas)
-    part = part[0] + swap(part[1], "y", 1)
-    part = part + send(part, lambda x, y, z, s: (x, y, z ^ 1, s))
-    a, b, c = (send(part, lambda x, y, z, s: (x, y, z ^ far, s)) for far in (2, 4, 6))
-    part = (part + a) + (b + c)
+    part = part + swap(part, "y", 1)
+    part = after(part, q)
+    part = part + to_near(part)
+    came = swap(q[1], "x", 1)
+    a, b, c = (to_pair(part, far) for far in (2, 4, 6))
+    part = after((part + a) + (b + c), came)
+    sigmas = rows(q[0], came, z_terms)
+    part = jnp.stack([part, after(swap(part, "y", 0), sigmas)])
     sigmas = send(sigmas, lambda x, y, z, s: (y % 2 * 2 + x % 2, y // 2 * 2 + x // 2, z, s))
-    mine = gather_four(part, "y")
-    pair = jnp.stack([mine, swap(mine, "x", 1)])
-    mine = after(jnp.concatenate([pair, swap(pair, "x", 0)], axis=0), sigmas)
+    part = jnp.stack([part, swap(part, "x", 1)])
+    mine = after(jnp.concatenate([part, swap(part, "x", 0)], axis=0), sigmas)
     s11, s10, s00 = finish(place, mine, to_core(mine), z_terms, zt_terms, base)
     return sigmas[0], s11, sigmas[1], s10, s00
 

time: 134 us -> 129 us (0.963)
  waiting for transfers between devices: 58.7 us -> 49.7 us
  starting transfers between devices: 45.4 us -> 48.1 us
    ppermute x35 -> x36, waiting for transfers between devices: 58.7 us -> 49.7 us  [send(): return lax.ppermute(block, AXES, pairs)]
    ppermute x35 -> x36, starting transfers between devices: 45.4 us -> 48.1 us  [send(): return lax.ppermute(block, AXES, pairs)]
  transfers between devices with their start and end apart: 35 -> 36, of which waited for: 24 -> 22; matrix products, arithmetic and copies ran while one was open for 1% -> 1% of each run, Pallas kernels for 13% -> 13%
where the time goes in v2:
time: 129 us; the launch traced here: 127 us
  waiting for transfers between devices  49.7 us (39%)
  starting transfers between devices  48.1 us (37%)
  Pallas kernels  23.4 us (18%)
  local copies, waits for them, and re-layouts  3.23 us (3%)
  other arithmetic  1.34 us (1%)
    ppermute x36, waiting for transfers between devices, send(): return lax.ppermute(block, AXES, pairs)  49.7 us
    ppermute x36, starting transfers between devices, send(): return lax.ppermute(block, AXES, pairs)  48.1 us
    pallas_call x4, Pallas kernels, multiply(): pl.pallas_call(kernel, in_specs=[SMEM, HBM, HBM] + [VMEM] * (2 + len(tota...  10.1 us
    pallas_call x1, Pallas kernels, invert(): pl.pallas_call(invert_kernel, in_specs=[SMEM, HBM, HBM], out_specs=[VMEM,...  3.94 us
    pallas_call x1, Pallas kernels, last(): pl.pallas_call(last_kernel, in_specs=[SMEM, HBM, HBM] + [VMEM] * 4, out_s...  3.58 us
    pallas_call x1, Pallas kernels, finish(): pl.pallas_call(finish_kernel, in_specs=[SMEM] + [VMEM] * 5, out_specs=[VM...  3.14 us
  transfers between devices with their start and end apart: 36, of which 22 were waited for; matrix products, arithmetic and copies ran while one was open for 1% of the time, Pallas kernels for 13%

profile of v2, /device:TPU:8, one launch (start us, length us, event | category | flops | bytes accessed | tf_op | source)
XLA Modules:
  0.0 126.7 jit_solution(478231429927252889)
XLA Ops:
  1.6 2.4 %collective-permute-start = (f32[1,2,64,256]{3,2,1,0:T(8,128)S(1)}, f32[1,2,64,256]{3,2,1,0:T(8,128)S(1)}, u32[]{:S(2)}, u32[]{:S(2)}) collective-permute-start(f32[1,2,64,256]{3,2,1,0:T(8,128)S(1)} %maximum_bitcast_fusion), channel_id=1, source_target_pairs={{0,4},{1,5},{2,6},{3,7},{4,0},{5,1},{6,2},{7,3},{8,12},{9,13},{10,... | collective-permute-start | bytes 393224 | tf_op jit(solution)/shard_map/ppermute | solution.py:29
  6.0 3.0 %collective-permute-done = f32[1,2,64,256]{3,2,1,0:T(8,128)S(1)} collective-permute-done((f32[1,2,64,256]{3,2,1,0:T(8,128)S(1)}, f32[1,2,64,256]{3,2,1,0:T(8,128)S(1)}, u32[]{:S(2)}, u32[]{:S(2)}) %collective-permute-start) | collective-permute-done | bytes 131104 | tf_op jit(solution)/shard_map/ppermute | solution.py:29
  10.8 3.5 %collective-permute-done.3 = f32[2,2,64,256]{3,2,1,0:T(8,128)S(1)} collective-permute-done((f32[2,2,64,256]{3,2,1,0:T(8,128)S(1)}, f32[2,2,64,256]{3,2,1,0:T(8,128)S(1)}, u32[]{:S(2)}, u32[]{:S(2)}) %collective-permute-start.3) | collective-permute-done | bytes 262176 | tf_op jit(solution)/shard_map/ppermute | solution.py:29
  16.2 5.7 %collective-permute-done.6 = f32[2,2,64,256]{3,2,1,0:T(8,128)S(1)} collective-permute-done((f32[2,2,64,256]{3,2,1,0:T(8,128)S(1)}, f32[2,2,64,256]{3,2,1,0:T(8,128)S(1)}, u32[]{:S(2)}, u32[]{:S(2)}) %collective-permute-start.6) | collective-permute-done | bytes 262176 | tf_op jit(solution)/shard_map/ppermute | solution.py:29
  22.0 2.8 %collective-permute-done.5 = f32[2,2,64,256]{3,2,1,0:T(8,128)S(1)} collective-permute-done((f32[2,2,64,256]{3,2,1,0:T(8,128)S(1)}, f32[2,2,64,256]{3,2,1,0:T(8,128)S(1)}, u32[]{:S(2)}, u32[]{:S(2)}) %collective-permute-start.5) | collective-permute-done | bytes 262176 | tf_op jit(solution)/shard_map/ppermute | solution.py:29
  24.7 3.0 %collective-permute-start.12 = (f32[2,2,64,256]{3,2,1,0:T(8,128)S(1)}, f32[2,2,64,256]{3,2,1,0:T(8,128)S(1)}, u32[]{:S(2)}, u32[]{:S(2)}) collective-permute-start(f32[2,2,64,256]{3,2,1,0:T(8,128)S(1)} %pad_maximum_fusion.2), channel_id=1, source_target_pairs={{0,128},{1,129},{2,130},{3,131},{4,132},{5,133},{6,134},{7,135},{8... | collective-permute-start | bytes 786440 | tf_op jit(solution)/shard_map/ppermute | solution.py:29
  40.9 2.4 %collective-permute-start.18 = (f32[4,2,64,256]{3,2,1,0:T(8,128)S(1)}, f32[4,2,64,256]{3,2,1,0:T(8,128)S(1)}, u32[]{:S(2)}, u32[]{:S(2)}) collective-permute-start(f32[4,2,64,256]{3,2,1,0:T(8,128)S(1)} %constant_dynamic-update-slice_fusion.6.even_ref), channel_id=1, source_target_pairs={{0,2},{1,7},{2,4},{3,1},{4,6},{5,3},{6,0},{7,5},{8,10},{9,15},{10,... | collective-permute-start | bytes 1572872 | tf_op jit(solution)/shard_map/ppermute | solution.py:29
  44.2 2.6 %multiply.5.refs_0_ = f32[2,256,512]{2,1,0:T(8,128)S(1)} custom-call(s32[9]{0:T(128)S(1)} %stack.66.at._, f32[8,4,2,64,256]{4,3,2,1,0:T(8,128)S(1)} %bitcast.43, f32[8,4,2,64,256]{4,3,2,1,0:T(8,128)} %bitcast.13.other_ref.other, f32[4,2,64,256]{3,2,1,0:T(8,128)S(1)} %constant_dynamic-update-slice_fusion.4.even_ref, ...), custom_call_target="tpu_custom_call", output_to_operand_aliasing={{}: (5, {})} | custom-call | flops 805306368 | bytes 2097152 | tf_op jit(solution)/shard_map/multiply/pallas_call | solution.py:171
  46.9 4.1 %collective-permute-done.11.even = f32[2,2,64,256]{3,2,1,0:T(8,128)S(1)} collective-permute-done((f32[2,2,64,256]{3,2,1,0:T(8,128)S(1)}, f32[2,2,64,256]{3,2,1,0:T(8,128)S(1)}, u32[]{:S(2)}, u32[]{:S(2)}) %collective-permute-start.11) | collective-permute-done | bytes 262176 | tf_op jit(solution)/shard_map/ppermute | solution.py:29
  53.5 2.6 %multiply.6.refs_0_ = f32[2,256,512]{2,1,0:T(8,128)S(1)} custom-call(s32[9]{0:T(128)S(1)} %stack.66.at._, f32[8,4,2,64,256]{4,3,2,1,0:T(8,128)S(1)} %bitcast.44, f32[8,4,2,64,256]{4,3,2,1,0:T(8,128)} %bitcast.13.other_ref.other, f32[4,2,64,256]{3,2,1,0:T(8,128)S(1)} %constant_dynamic-update-slice_fusion.2.even_ref, ...), custom_call_target="tpu_custom_call", output_to_operand_aliasing={{}: (5, {})} | custom-call | flops 805306368 | bytes 2097152 | tf_op jit(solution)/shard_map/multiply/pallas_call | solution.py:171
  56.2 2.6 %multiply.7.total = f32[2,256,512]{2,1,0:T(8,128)S(1)} custom-call(s32[9]{0:T(128)S(1)} %stack.66.at._, f32[8,4,2,64,256]{4,3,2,1,0:T(8,128)S(1)} %bitcast.45, f32[8,4,2,64,256]{4,3,2,1,0:T(8,128)} %bitcast.13.other_ref.other, f32[4,2,64,256]{3,2,1,0:T(8,128)S(1)} %constant_dynamic-update-slice_fusion.6.even_ref, ...), custom_call_target="tpu_custom_call", output_to_operand_aliasing={{}: (5, {})} | custom-call | flops 805306368 | bytes 2097152 | tf_op jit(solution)/shard_map/multiply/pallas_call | solution.py:171
  58.8 3.6 %last.1 = (f32[2,4,4,24,256]{4,3,2,1,0:T(8,128)S(1)}, f32[2,4,64,512]{3,2,1,0:T(8,128)S(1)}) custom-call(s32[9]{0:T(128)S(1)} %stack.66.at._, f32[8,4,2,64,256]{4,3,2,1,0:T(8,128)S(1)} %bitcast.46, f32[8,4,2,64,256]{4,3,2,1,0:T(8,128)} %bitcast.13.other_ref.other, f32[2,2,64,256]{3,2,1,0:T(8,128)S(1)} %collective-permute-done.11.even, ...), custom_call_target="tpu_custom_call" | custom-call | flops 1073741824 | bytes 2097152 | tf_op jit(solution)/shard_map/last/pallas_call | solution.py:214
  65.9 3.9 %invert.1 = (f32[256,256]{1,0:T(8,128)S(1)}, f32[256,256]{1,0:T(8,128)S(1)}) custom-call(s32[9]{0:T(128)S(1)} %stack.66.at._, f32[256,256]{1,0:T(8,128)S(1)} %copy-done.1, f32[256,256]{1,0:T(8,128)S(1)} %copy-done.2), custom_call_target="tpu_custom_call" | custom-call | flops 4294967296 | bytes 1048576 | tf_op jit(solution)/shard_map/invert/pallas_call | solution.py:273
  70.2 3.1 %collective-permute-start.25 = (f32[4,24,256]{2,1,0:T(8,128)S(1)}, f32[4,24,256]{2,1,0:T(8,128)S(1)}, u32[]{:S(2)}, u32[]{:S(2)}) collective-permute-start(f32[4,24,256]{2,1,0:T(8,128)S(1)} %slice_bitcast_fusion.4), channel_id=1, source_target_pairs={{0,192},{1,65},{2,194},{3,67},{4,196},{5,69},{6,198},{7,71},{8,200... | collective-permute-start | bytes 294920 | tf_op jit(solution)/shard_map/ppermute | solution.py:29
  76.9 3.6 %collective-permute-done.26 = f32[2,24,256]{2,1,0:T(8,128)S(1)} collective-permute-done((f32[2,24,256]{2,1,0:T(8,128)S(1)}, f32[2,24,256]{2,1,0:T(8,128)S(1)}, u32[]{:S(2)}, u32[]{:S(2)}) %collective-permute-start.26) | collective-permute-done | bytes 49184 | tf_op jit(solution)/shard_map/ppermute | solution.py:29
  81.1 3.6 %collective-permute-done.27 = f32[2,24,256]{2,1,0:T(8,128)S(1)} collective-permute-done((f32[2,24,256]{2,1,0:T(8,128)S(1)}, f32[2,24,256]{2,1,0:T(8,128)S(1)}, u32[]{:S(2)}, u32[]{:S(2)}) %collective-permute-start.27) | collective-permute-done | bytes 49184 | tf_op jit(solution)/shard_map/ppermute | solution.py:29
  85.1 3.9 %collective-permute-done.28 = f32[2,24,256]{2,1,0:T(8,128)S(1)} collective-permute-done((f32[2,24,256]{2,1,0:T(8,128)S(1)}, f32[2,24,256]{2,1,0:T(8,128)S(1)}, u32[]{:S(2)}, u32[]{:S(2)}) %collective-permute-start.28) | collective-permute-done | bytes 49184 | tf_op jit(solution)/shard_map/ppermute | solution.py:29
  91.3 2.4 %collective-permute-start.30 = (f32[2,24,256]{2,1,0:T(8,128)S(1)}, f32[2,24,256]{2,1,0:T(8,128)S(1)}, u32[]{:S(2)}, u32[]{:S(2)}) collective-permute-start(f32[2,24,256]{2,1,0:T(8,128)S(1)} %add.72), channel_id=1, source_target_pairs={{0,32},{1,33},{2,34},{3,35},{4,36},{5,37},{6,38},{7,39},{8,40},{9,... | collective-permute-start | bytes 147464 | tf_op jit(solution)/shard_map/ppermute | solution.py:29
  95.6 3.3 %collective-permute-start.21 = (f32[64,512]{1,0:T(8,128)S(1)}, f32[64,512]{1,0:T(8,128)S(1)}, u32[]{:S(2)}, u32[]{:S(2)}) collective-permute-start(f32[64,512]{1,0:T(8,128)S(1)} %get-tuple-element.73), channel_id=1, source_target_pairs={{0,192},{1,65},{2,194},{3,67},{4,196},{5,69},{6,198},{7,71},{8,200... | collective-permute-start | bytes 393224 | tf_op jit(solution)/shard_map/ppermute | solution.py:29
  105.9 3.3 %collective-permute-start.33 = (f32[2,2,24,256]{3,2,1,0:T(8,128)S(1)}, f32[2,2,24,256]{3,2,1,0:T(8,128)S(1)}, u32[]{:S(2)}, u32[]{:S(2)}) collective-permute-start(f32[2,2,24,256]{3,2,1,0:T(8,128)S(1)} %get-tuple-element.78), channel_id=1, source_target_pairs={{0,192},{1,65},{2,194},{3,67},{4,196},{5,69},{6,198},{7,71},{8,200... | collective-permute-start | bytes 294920 | tf_op jit(solution)/shard_map/ppermute | solution.py:29
  109.2 2.6 %collective-permute-done.33 = f32[2,2,24,256]{3,2,1,0:T(8,128)S(1)} collective-permute-done((f32[2,2,24,256]{3,2,1,0:T(8,128)S(1)}, f32[2,2,24,256]{3,2,1,0:T(8,128)S(1)}, u32[]{:S(2)}, u32[]{:S(2)}) %collective-permute-start.33) | collective-permute-done | bytes 98336 | tf_op jit(solution)/shard_map/ppermute | solution.py:29
  112.0 6.8 %collective-permute-start.24 = (f32[2,64,256]{2,1,0:T(8,128)S(1)}, f32[2,64,256]{2,1,0:T(8,128)S(1)}, u32[]{:S(2)}, u32[]{:S(2)}) collective-permute-start(f32[2,64,256]{2,1,0:T(8,128)S(1)} %rows.1), channel_id=1, source_target_pairs={{0,0},{1,1},{2,128},{3,129},{4,4},{5,5},{6,132},{7,133},{8,8},{9,9... | collective-permute-start | bytes 393224 | tf_op jit(solution)/shard_map/ppermute | solution.py:29
  118.8 3.1 %collective-permute-done.24 = f32[2,64,256]{2,1,0:T(8,128)S(1)} collective-permute-done((f32[2,64,256]{2,1,0:T(8,128)S(1)}, f32[2,64,256]{2,1,0:T(8,128)S(1)}, u32[]{:S(2)}, u32[]{:S(2)}) %collective-permute-start.24) | collective-permute-done | bytes 131104 | tf_op jit(solution)/shard_map/ppermute | solution.py:29
  123.6 3.1 %finish.1 = (f32[256,256]{1,0:T(8,128)}, f32[256,256]{1,0:T(8,128)}, f32[256,256]{1,0:T(8,128)}) custom-call(s32[9]{0:T(128)S(1)} %stack.66.at._, f32[4,2,2,24,256]{4,3,2,1,0:T(8,128)S(1)} %pad_maximum_fusion.1.mine, f32[4,2,2,24,256]{4,3,2,1,0:T(8,128)S(1)} %collective-permute-done.35.other, bf16[1536,512]{1,0:T(8,128)(2,1)S(1)} %get-tuple-element.62.z_terms, ...), custom_call_target="tpu_custom_call" | custom-call | flops 268435456 | bytes 3145728 | tf_op jit(solution)/shard_map/finish/pallas_call | solution.py:394
  (105 shorter events, 44.6 us)
Async XLA Ops:
  1.6 7.4 %collective-permute-start = (f32[1,2,64,256]{3,2,1,0:T(8,128)S(1)}, f32[1,2,64,256]{3,2,1,0:T(8,128)S(1)}, u32[]{:S(2)}, u32[]{:S(2)}) collective-permute-start(f32[1,2,64,256]{3,2,1,0:T(8,128)S(1)} %maximum_bitcast_fusion), channel_id=1, source_target_pairs={{0,4},{1,5},{2,6},{3,7},{4,0},{5,1},{6,2},{7,3},{8,12},{9,13},{10,... | collective-permute-start | bytes 393224 | tf_op jit(solution)/shard_map/ppermute | solution.py:29
  4.0 10.3 %collective-permute-start.3 = (f32[2,2,64,256]{3,2,1,0:T(8,128)S(1)}, f32[2,2,64,256]{3,2,1,0:T(8,128)S(1)}, u32[]{:S(2)}, u32[]{:S(2)}) collective-permute-start(f32[2,2,64,256]{3,2,1,0:T(8,128)S(1)} %pad_maximum_fusion.4), channel_id=1, source_target_pairs={{0,8},{1,57},{2,10},{3,59},{4,12},{5,61},{6,14},{7,63},{8,16},{9,1... | collective-permute-start | bytes 786440 | tf_op jit(solution)/shard_map/ppermute | solution.py:29
  14.3 21.9 %collective-permute-start.4 = (f32[4096,256]{1,0:T(8,128)}, f32[4096,256]{1,0:T(8,128)}, u32[]{:S(2)}, u32[]{:S(2)}) collective-permute-start(f32[4096,256]{1,0:T(8,128)} %param.6), channel_id=1, source_target_pairs={{0,1},{1,0},{2,3},{3,2},{4,5},{5,4},{6,7},{7,6},{8,9},{9,8},{10,11... | collective-permute-start | bytes 12582920 | tf_op jit(solution)/shard_map/ppermute | solution.py:29
  14.3 7.6 %collective-permute-start.6 = (f32[2,2,64,256]{3,2,1,0:T(8,128)S(1)}, f32[2,2,64,256]{3,2,1,0:T(8,128)S(1)}, u32[]{:S(2)}, u32[]{:S(2)}) collective-permute-start(f32[2,2,64,256]{3,2,1,0:T(8,128)S(1)} %constant_dynamic-update-slice_fusion), channel_id=1, source_target_pairs={{0,8},{1,57},{2,10},{3,59},{4,12},{5,61},{6,14},{7,63},{8,16},{9,1... | collective-permute-start | bytes 786440 | tf_op jit(solution)/shard_map/ppermute | solution.py:29
  14.3 7.6 %collective-permute-start.7 = (f32[2,2,64,256]{3,2,1,0:T(8,128)S(1)}, f32[2,2,64,256]{3,2,1,0:T(8,128)S(1)}, u32[]{:S(2)}, u32[]{:S(2)}) collective-permute-start(f32[2,2,64,256]{3,2,1,0:T(8,128)S(1)} %pad_maximum_fusion.3.even_ref), channel_id=1, source_target_pairs={{0,2},{1,7},{2,4},{3,1},{4,6},{5,3},{6,0},{7,5},{8,10},{9,15},{10,... | collective-permute-start | bytes 786440 | tf_op jit(solution)/shard_map/ppermute | solution.py:29
  14.9 9.8 %collective-permute-start.5 = (f32[2,2,64,256]{3,2,1,0:T(8,128)S(1)}, f32[2,2,64,256]{3,2,1,0:T(8,128)S(1)}, u32[]{:S(2)}, u32[]{:S(2)}) collective-permute-start(f32[2,2,64,256]{3,2,1,0:T(8,128)S(1)} %collective-permute-done.3), channel_id=1, source_target_pairs={{0,8},{1,57},{2,10},{3,59},{4,12},{5,61},{6,14},{7,63},{8,16},{9,1... | collective-permute-start | bytes 786440 | tf_op jit(solution)/shard_map/ppermute | solution.py:29
  21.9 7.6 %collective-permute-start.9 = (f32[2,2,64,256]{3,2,1,0:T(8,128)S(1)}, f32[2,2,64,256]{3,2,1,0:T(8,128)S(1)}, u32[]{:S(2)}, u32[]{:S(2)}) collective-permute-start(f32[2,2,64,256]{3,2,1,0:T(8,128)S(1)} %collective-permute-done.6), channel_id=1, source_target_pairs={{0,8},{1,57},{2,10},{3,59},{4,12},{5,61},{6,14},{7,63},{8,16},{9,1... | collective-permute-start | bytes 786440 | tf_op jit(solution)/shard_map/ppermute | solution.py:29
  24.7 8.3 %collective-permute-start.12 = (f32[2,2,64,256]{3,2,1,0:T(8,128)S(1)}, f32[2,2,64,256]{3,2,1,0:T(8,128)S(1)}, u32[]{:S(2)}, u32[]{:S(2)}) collective-permute-start(f32[2,2,64,256]{3,2,1,0:T(8,128)S(1)} %pad_maximum_fusion.2), channel_id=1, source_target_pairs={{0,128},{1,129},{2,130},{3,131},{4,132},{5,133},{6,134},{7,135},{8... | collective-permute-start | bytes 786440 | tf_op jit(solution)/shard_map/ppermute | solution.py:29
  27.8 7.7 %collective-permute-start.8 = (f32[2,2,64,256]{3,2,1,0:T(8,128)S(1)}, f32[2,2,64,256]{3,2,1,0:T(8,128)S(1)}, u32[]{:S(2)}, u32[]{:S(2)}) collective-permute-start(f32[2,2,64,256]{3,2,1,0:T(8,128)S(1)} %collective-permute-done.5), channel_id=1, source_target_pairs={{0,8},{1,57},{2,10},{3,59},{4,12},{5,61},{6,14},{7,63},{8,16},{9,1... | collective-permute-start | bytes 786440 | tf_op jit(solution)/shard_map/ppermute | solution.py:29
  28.0 16.2 %collective-permute-start.16 = (f32[4,2,64,256]{3,2,1,0:T(8,128)S(1)}, f32[4,2,64,256]{3,2,1,0:T(8,128)S(1)}, u32[]{:S(2)}, u32[]{:S(2)}) collective-permute-start(f32[4,2,64,256]{3,2,1,0:T(8,128)S(1)} %constant_dynamic-update-slice_fusion.4.even_ref), channel_id=1, source_target_pairs={{0,2},{1,7},{2,4},{3,1},{4,6},{5,3},{6,0},{7,5},{8,10},{9,15},{10,... | collective-permute-start | bytes 1572872 | tf_op jit(solution)/shard_map/ppermute | solution.py:29
  29.5 11.2 %collective-permute-start.10 = (f32[2,2,64,256]{3,2,1,0:T(8,128)S(1)}, f32[2,2,64,256]{3,2,1,0:T(8,128)S(1)}, u32[]{:S(2)}, u32[]{:S(2)}) collective-permute-start(f32[2,2,64,256]{3,2,1,0:T(8,128)S(1)} %collective-permute-done.9), channel_id=1, source_target_pairs={{0,8},{1,57},{2,10},{3,59},{4,12},{5,61},{6,14},{7,63},{8,16},{9,1... | collective-permute-start | bytes 786440 | tf_op jit(solution)/shard_map/ppermute | solution.py:29
  33.0 7.7 %collective-permute-start.13 = (f32[2,2,64,256]{3,2,1,0:T(8,128)S(1)}, f32[2,2,64,256]{3,2,1,0:T(8,128)S(1)}, u32[]{:S(2)}, u32[]{:S(2)}) collective-permute-start(f32[2,2,64,256]{3,2,1,0:T(8,128)S(1)} %broadcast_select_fusion), channel_id=1, source_target_pairs={{0,64},{1,65},{2,66},{3,67},{4,68},{5,69},{6,70},{7,71},{8,72},{9,... | collective-permute-start | bytes 786440 | tf_op jit(solution)/shard_map/ppermute | solution.py:29
  35.5 11.3 %collective-permute-start.15 = (f32[4,2,64,256]{3,2,1,0:T(8,128)S(1)}, f32[4,2,64,256]{3,2,1,0:T(8,128)S(1)}, u32[]{:S(2)}, u32[]{:S(2)}) collective-permute-start(f32[4,2,64,256]{3,2,1,0:T(8,128)S(1)} %constant_dynamic-update-slice_fusion.2.even_ref), channel_id=1, source_target_pairs={{0,2},{1,7},{2,4},{3,1},{4,6},{5,3},{6,0},{7,5},{8,10},{9,15},{10,... | collective-permute-start | bytes 1572872 | tf_op jit(solution)/shard_map/ppermute | solution.py:29
  40.7 10.2 %collective-permute-start.14 = (f32[4,2,64,256]{3,2,1,0:T(8,128)S(1)}, f32[4,2,64,256]{3,2,1,0:T(8,128)S(1)}, u32[]{:S(2)}, u32[]{:S(2)}) collective-permute-start(f32[4,2,64,256]{3,2,1,0:T(8,128)S(1)} %pad_maximum_fusion.mine), channel_id=1, source_target_pairs={{0,1},{1,0},{2,3},{3,2},{4,5},{5,4},{6,7},{7,6},{8,9},{9,8},{10,11... | collective-permute-start | bytes 1572872 | tf_op jit(solution)/shard_map/ppermute | solution.py:29
  40.9 15.3 %collective-permute-start.18 = (f32[4,2,64,256]{3,2,1,0:T(8,128)S(1)}, f32[4,2,64,256]{3,2,1,0:T(8,128)S(1)}, u32[]{:S(2)}, u32[]{:S(2)}) collective-permute-start(f32[4,2,64,256]{3,2,1,0:T(8,128)S(1)} %constant_dynamic-update-slice_fusion.6.even_ref), channel_id=1, source_target_pairs={{0,2},{1,7},{2,4},{3,1},{4,6},{5,3},{6,0},{7,5},{8,10},{9,15},{10,... | collective-permute-start | bytes 1572872 | tf_op jit(solution)/shard_map/ppermute | solution.py:29
  43.3 7.7 %collective-permute-start.11 = (f32[2,2,64,256]{3,2,1,0:T(8,128)S(1)}, f32[2,2,64,256]{3,2,1,0:T(8,128)S(1)}, u32[]{:S(2)}, u32[]{:S(2)}) collective-permute-start(f32[2,2,64,256]{3,2,1,0:T(8,128)S(1)} %pad_maximum_fusion.5), channel_id=1, source_target_pairs={{0,8},{1,57},{2,10},{3,59},{4,12},{5,61},{6,14},{7,63},{8,16},{9,1... | collective-permute-start | bytes 786440 | tf_op jit(solution)/shard_map/ppermute | solution.py:29
  50.9 7.9 %collective-permute-start.17 = (f32[2,2,64,256]{3,2,1,0:T(8,128)S(1)}, f32[2,2,64,256]{3,2,1,0:T(8,128)S(1)}, u32[]{:S(2)}, u32[]{:S(2)}) collective-permute-start(f32[2,2,64,256]{3,2,1,0:T(8,128)S(1)} %collective-permute-done.11.even), channel_id=1, source_target_pairs={{0,2},{1,7},{2,4},{3,1},{4,6},{5,3},{6,0},{7,5},{8,10},{9,15},{10,... | collective-permute-start | bytes 786440 | tf_op jit(solution)/shard_map/ppermute | solution.py:29
  62.6 7.3 %collective-permute-start.19 = (f32[4,64,512]{2,1,0:T(8,128)S(1)}, f32[4,64,512]{2,1,0:T(8,128)S(1)}, u32[]{:S(2)}, u32[]{:S(2)}) collective-permute-start(f32[4,64,512]{2,1,0:T(8,128)S(1)} %slice_bitcast_fusion), channel_id=1, source_target_pairs={{0,1},{1,0},{2,3},{3,2},{4,5},{5,4},{6,7},{7,6},{8,9},{9,8},{10,11... | collective-permute-start | bytes 1572872 | tf_op jit(solution)/shard_map/ppermute | solution.py:29
  76.8 7.9 %collective-permute-start.20 = (f32[2,64,512]{2,1,0:T(8,128)S(1)}, f32[2,64,512]{2,1,0:T(8,128)S(1)}, u32[]{:S(2)}, u32[]{:S(2)}) collective-permute-start(f32[2,64,512]{2,1,0:T(8,128)S(1)} %slice.81), channel_id=1, source_target_pairs={{0,64},{1,193},{2,66},{3,195},{4,68},{5,197},{6,70},{7,199},{8,72}... | collective-permute-start | bytes 786440 | tf_op jit(solution)/shard_map/ppermute | solution.py:29
  88.9 9.9 %collective-permute-start.29 = (f32[2,24,256]{2,1,0:T(8,128)S(1)}, f32[2,24,256]{2,1,0:T(8,128)S(1)}, u32[]{:S(2)}, u32[]{:S(2)}) collective-permute-start(f32[2,24,256]{2,1,0:T(8,128)S(1)} %add.72), channel_id=1, source_target_pairs={{0,16},{1,49},{2,18},{3,51},{4,20},{5,53},{6,22},{7,55},{8,24},{9,... | collective-permute-start | bytes 147464 | tf_op jit(solution)/shard_map/ppermute | solution.py:29
  91.3 8.1 %collective-permute-start.30 = (f32[2,24,256]{2,1,0:T(8,128)S(1)}, f32[2,24,256]{2,1,0:T(8,128)S(1)}, u32[]{:S(2)}, u32[]{:S(2)}) collective-permute-start(f32[2,24,256]{2,1,0:T(8,128)S(1)} %add.72), channel_id=1, source_target_pairs={{0,32},{1,33},{2,34},{3,35},{4,36},{5,37},{6,38},{7,39},{8,40},{9,... | collective-permute-start | bytes 147464 | tf_op jit(solution)/shard_map/ppermute | solution.py:29
  95.6 6.3 %collective-permute-start.21 = (f32[64,512]{1,0:T(8,128)S(1)}, f32[64,512]{1,0:T(8,128)S(1)}, u32[]{:S(2)}, u32[]{:S(2)}) collective-permute-start(f32[64,512]{1,0:T(8,128)S(1)} %get-tuple-element.73), channel_id=1, source_target_pairs={{0,192},{1,65},{2,194},{3,67},{4,196},{5,69},{6,198},{7,71},{8,200... | collective-permute-start | bytes 393224 | tf_op jit(solution)/shard_map/ppermute | solution.py:29
  111.9 6.9 %collective-permute-start.34 = (f32[2,2,2,24,256]{4,3,2,1,0:T(8,128)S(1)}, f32[2,2,2,24,256]{4,3,2,1,0:T(8,128)S(1)}, u32[]{:S(2)}, u32[]{:S(2)}) collective-permute-start(f32[2,2,2,24,256]{4,3,2,1,0:T(8,128)S(1)} %pad_maximum_fusion.6), channel_id=1, source_target_pairs={{0,64},{1,193},{2,66},{3,195},{4,68},{5,197},{6,70},{7,199},{8,72}... | collective-permute-start | bytes 589832 | tf_op jit(solution)/shard_map/ppermute | solution.py:29
  112.0 9.9 %collective-permute-start.24 = (f32[2,64,256]{2,1,0:T(8,128)S(1)}, f32[2,64,256]{2,1,0:T(8,128)S(1)}, u32[]{:S(2)}, u32[]{:S(2)}) collective-permute-start(f32[2,64,256]{2,1,0:T(8,128)S(1)} %rows.1), channel_id=1, source_target_pairs={{0,0},{1,1},{2,128},{3,129},{4,4},{5,5},{6,132},{7,133},{8,8},{9,9... | collective-permute-start | bytes 393224 | tf_op jit(solution)/shard_map/ppermute | solution.py:29
  (16 other events, 61.0 us)

commit v3 on v2

--- a/solution.py
+++ b/solution.py
@@ -123,23 +123,41 @@
 SLAB = (NY, 2, Q, B)
 
 
+def stage(place, sigma):
+    def kernel(at, ref, out, sems):
+        copies = [pltpu.make_async_copy(ref.at[at[4 + n]], out.at[n], sems.at[n]) for n in range(5)]
+        for copy in copies:
+            copy.start()
+        for copy in copies:
+            copy.wait()
+
+    return pl.pallas_call(
+        kernel,
+        in_specs=[SMEM, HBM],
+        out_specs=VMEM,
+        out_shape=jax.ShapeDtypeStruct((5,) + SLAB, F32),
+        scratch_shapes=[pltpu.SemaphoreType.DMA((5,))],
+        compiler_params=params(),
+        cost_estimate=cost(0, 5 << 20),
+        name="stage",
+    )(place, sigma)
+
+
 def slab_product(at, step, own, other, even, odd, left, right, slabs, sems):
     y, s, slab = at[1], at[3], at[4 + step]
-    copies = [
-        pltpu.make_async_copy(ref.at[slab], slabs.at[n], sems.at[n]) for n, ref in enumerate((own, other))
-    ]
-    for copy in copies:
-        copy.start()
+    copy = pltpu.make_async_copy(other.at[slab], slabs, sems.at[0])
+    copy.start()
     depth = even.shape[0] * Q
     for n, ref in enumerate((even, odd)):
         for panel in range(2):
             fill_right(right, n * depth, panel * B, ref[:, panel].reshape(depth, B))
     near = lax.rem(y + 3 + 2 * s, NY)
     for o in range(2):
-        copies[o].wait()
+        if o == 1:
+            copy.wait()
         for n, first in enumerate((y, near)):
             blocks = [
-                slabs[o, lax.rem(first + 2 * d, NY), core]
+                (slabs if o else own.at[step])[lax.rem(first + 2 * d, NY), core]
                 for d in range(2)
                 for core in (s, 1 - s)[: depth // 128]
             ]
@@ -152,8 +170,8 @@
     return [
         pltpu.VMEM((2 * B, deep), BF16),
         pltpu.VMEM((deep, 2 * B), BF16),
-        pltpu.VMEM((2,) + SLAB, F32),
-        pltpu.SemaphoreType.DMA((2,)),
+        pltpu.VMEM(SLAB, F32),
+        pltpu.SemaphoreType.DMA((1,)),
     ]
 
 
@@ -170,7 +188,7 @@
 
     return pl.pallas_call(
         kernel,
-        in_specs=[SMEM, HBM, HBM] + [VMEM] * (2 + len(totals)),
+        in_specs=[SMEM, VMEM, HBM] + [VMEM] * (2 + len(totals)),
         out_specs=VMEM,
         out_shape=jax.ShapeDtypeStruct((2, B, 2 * B), F32),
         scratch_shapes=slab_scratch(even),
@@ -213,7 +231,7 @@
 def last(place, sigma, other, even, odd, total, weights):
     return pl.pallas_call(
         last_kernel,
-        in_specs=[SMEM, HBM, HBM] + [VMEM] * 4,
+        in_specs=[SMEM, VMEM, HBM] + [VMEM] * 4,
         out_specs=[VMEM, VMEM],
         out_shape=[
             jax.ShapeDtypeStruct((2, NX, NY, N, B), F32),
@@ -339,19 +357,20 @@
     )(place, mine, others)
 
 
-def rows_kernel(a, b, z_terms, sigmas, left):
+def rows_kernel(a, b, z_terms, s1, s0, left):
     fill_left(left, 0, 0, a[...] + b[...])
     both = product(left[...], z_terms[...])
-    sigmas[0] = -both[:, :B]
-    sigmas[1] = -both[:, B:]
+    s1[...] = -both[:, :B]
+    s0[...] = -both[:, B:]
 
 
 def rows(a, b, z_terms):
+    out = jax.ShapeDtypeStruct((Q, B), F32)
     return pl.pallas_call(
         rows_kernel,
         in_specs=[VMEM] * 3,
-        out_specs=VMEM,
-        out_shape=jax.ShapeDtypeStruct((2, Q, B), F32),
+        out_specs=[VMEM] * 2,
+        out_shape=[out, out],
         scratch_shapes=[pltpu.VMEM((Q, WIDE), BF16)],
         compiler_params=params(),
         cost_estimate=cost(1 << 27, 2 << 20),
@@ -417,12 +436,13 @@
     a = jnp.concatenate([own, to_core(own)], axis=0)
     y2 = send(own, lambda x, y, z, s: (x, y + 2, z, s))
     a1 = along_z(a)
-    b = jnp.concatenate([after(y2, a), to_core(y2)], axis=0)
+    staged = stage(after(place, a), sigma.reshape(view))
+    y2 = after(y2, a, staged)
+    b = jnp.concatenate([y2, to_core(y2)], axis=0)
     b1 = along_z(b)
     a2 = along_z(after(a1, b))
 
     sigma_other = to_core(after(sigma, b, a1)).reshape(view)
-    sigma = sigma.reshape(view)
     even = jnp.concatenate([own, after(y2, a1)], axis=0)
     odd = along_y(even)
     b1, odd = after((b1, odd), b1, odd)
@@ -432,30 +452,30 @@
     pair = jnp.concatenate([own, jnp.where(y % 2 == s, odd[1:], odd[:1])], axis=0)
     a3 = along_z(after(a2, b1))
     crossed = send(after(pair, a2), lambda x, y, z, s: (x ^ 2, y, z, s))
-    total = multiply(place, 0, sigma, sigma_other, even, odd)
 
     b2 = after(b2, a2)
     b3 = along_z(b2)
     z2 = jnp.concatenate([a2, b2], axis=0)
     e2 = along_y(z2)
     a3 = after(a3, b2)
-    first = jnp.where(x // 2 == y % 2, pair, after(crossed, b2))
-    second = send(first, lambda x, y, z, s: (x ^ 1, y, z, s))
-
-    b3 = after(b3, a3, total)
+    total = multiply(place, 0, staged, sigma_other, even, odd)
+
+    b3, crossed = after((b3, crossed), b3, crossed, a3, total)
     z4 = along_z(jnp.concatenate([a3[:1], b3[:1]], axis=0))
     z3 = jnp.concatenate([a3, b3], axis=0)
     e3 = along_y(z3)
-    mine = jnp.concatenate([first, after(second, b3)], axis=0)
+    first = jnp.where(x // 2 == y % 2, pair, crossed)
+    second = send(first, lambda x, y, z, s: (x ^ 1, y, z, s))
+    total = multiply(place, 1, staged, sigma_other, z1, e1, total)
+
+    z4, second, e2 = after((z4, second, e2), z4, second, e2, total)
+    e4 = along_y(z4)
+    mine = jnp.concatenate([first, second], axis=0)
     others = to_core(mine)
-    total = multiply(place, 1, sigma, sigma_other, z1, e1, total)
-
-    z4, others, e2 = after((z4, others, e2), z4, others, total, e2)
-    e4 = along_y(z4)
-    total = multiply(place, 2, sigma, sigma_other, z2, e2, total)
+    total = multiply(place, 2, staged, sigma_other, z2, e2, total)
     weights = weigh(place, mine, others)
-    total = multiply(place, 3, sigma, sigma_other, z3, e3, total)
-    corner, pieces = last(place, sigma, sigma_other, z4, e4, total, weights)
+    total = multiply(place, 3, staged, sigma_other, z3, e3, total)
+    corner, pieces = last(place, staged, sigma_other, z4, e4, total, weights)
 
     part = corner[0] + to_core(corner[1])
     came = swap(part[2:], "x", 0)
@@ -473,13 +493,19 @@
     came = swap(q[1], "x", 1)
     a, b, c = (to_pair(part, far) for far in (2, 4, 6))
     part = after((part + a) + (b + c), came)
-    sigmas = rows(q[0], came, z_terms)
-    part = jnp.stack([part, after(swap(part, "y", 0), sigmas)])
-    sigmas = send(sigmas, lambda x, y, z, s: (y % 2 * 2 + x % 2, y // 2 * 2 + x // 2, z, s))
+    s1, s0 = rows(q[0], came, z_terms)
+    part = jnp.stack([part, after(swap(part, "y", 0), s1, s0)])
+
+    def home(block):
+        return send(block, lambda x, y, z, s: (y % 2 * 2 + x % 2, y // 2 * 2 + x // 2, z, s))
+
+    sigmas = home(jnp.stack([s1, s0]))
     part = jnp.stack([part, swap(part, "x", 1)])
-    mine = after(jnp.concatenate([part, swap(part, "x", 0)], axis=0), sigmas)
+    mine = jnp.concatenate([part, swap(part, "x", 0)], axis=0)
     s11, s10, s00 = finish(place, mine, to_core(mine), z_terms, zt_terms, base)
-    return sigmas[0], s11, sigmas[1], s10, s00
+    sigmas = after(sigmas, s11)
+    s1, s0 = sigmas[0], sigmas[1]
+    return s1, s11, s0, s10, s00
 
 
 def solution(mesh):

time: 129 us -> 127 us (0.984)
  waiting for transfers between devices: 49.7 us -> 44.1 us
  Pallas kernels: 23.4 us -> 25.7 us
  starting transfers between devices: 48.1 us -> 49.5 us
    ppermute x36, waiting for transfers between devices: 49.7 us -> 44.1 us  [send(): return lax.ppermute(block, AXES, pairs)]
    pallas_call x6 -> x7, Pallas kernels: 14.1 us -> 16.5 us  [the longest x4 10.3 us: multiply(): pl.pallas_call(kernel, in_specs=[SMEM, VMEM, HBM] + [VMEM] * (2 + len(tot...]
    ppermute x36, starting transfers between devices: 48.1 us -> 49.5 us  [send(): return lax.ppermute(block, AXES, pairs)]
  transfers between devices with their start and end apart: 36 -> 36, of which waited for: 22 -> 23; matrix products, arithmetic and copies ran while one was open for 1% -> 3% of each run, Pallas kernels for 13% -> 18%
where the time goes in v3:
time: 127 us; the launch traced here: 126 us
  starting transfers between devices  49.5 us (39%)
  waiting for transfers between devices  44.1 us (35%)
  Pallas kernels  25.7 us (20%)
  local copies, waits for them, and re-layouts  4.25 us (3%)
  other arithmetic  1.35 us (1%)
    ppermute x36, starting transfers between devices, send(): return lax.ppermute(block, AXES, pairs)  49.5 us
    ppermute x36, waiting for transfers between devices, send(): return lax.ppermute(block, AXES, pairs)  44.1 us
    pallas_call x4, Pallas kernels, multiply(): pl.pallas_call(kernel, in_specs=[SMEM, VMEM, HBM] + [VMEM] * (2 + len(tot...  10.3 us
    pallas_call x1, Pallas kernels, invert(): pl.pallas_call(invert_kernel, in_specs=[SMEM, HBM, HBM], out_specs=[VMEM,...  3.94 us
    pallas_call x1, Pallas kernels, last(): pl.pallas_call(last_kernel, in_specs=[SMEM, VMEM, HBM] + [VMEM] * 4, out_...  3.55 us
    pallas_call x1, Pallas kernels, finish(): pl.pallas_call(finish_kernel, in_specs=[SMEM] + [VMEM] * 5, out_specs=[VM...  3.15 us
  transfers between devices with their start and end apart: 36, of which 23 were waited for; matrix products, arithmetic and copies ran while one was open for 3% of the time, Pallas kernels for 18%

profile of v3, /device:TPU:8, one launch (start us, length us, event | category | flops | bytes accessed | tf_op | source)
XLA Modules:
  0.0 125.9 jit_solution(13644804249228616850)
XLA Ops:
  1.6 2.4 %collective-permute-start.1 = (f32[1,2,64,256]{3,2,1,0:T(8,128)S(1)}, f32[1,2,64,256]{3,2,1,0:T(8,128)S(1)}, u32[]{:S(2)}, u32[]{:S(2)}) collective-permute-start(f32[1,2,64,256]{3,2,1,0:T(8,128)S(1)} %maximum_bitcast_fusion), channel_id=1, source_target_pairs={{0,4},{1,5},{2,6},{3,7},{4,0},{5,1},{6,2},{7,3},{8,12},{9,13},{10,... | collective-permute-start | bytes 393224 | tf_op jit(solution)/shard_map/ppermute | solution.py:29
  6.1 2.3 %stage.1.own_ref.own = f32[5,4,2,64,256]{4,3,2,1,0:T(8,128)S(1)} custom-call(s32[9]{0:T(128)S(1)} %stack.75.at._, f32[8,4,2,64,256]{4,3,2,1,0:T(8,128)} %bitcast.12.ref), custom_call_target="tpu_custom_call" | custom-call | bytes 5242880 | tf_op jit(solution)/shard_map/stage/pallas_call | solution.py:134
  9.0 3.2 %collective-permute-start.2 = (f32[1,2,64,256]{3,2,1,0:T(8,128)S(1)}, f32[1,2,64,256]{3,2,1,0:T(8,128)S(1)}, u32[]{:S(2)}, u32[]{:S(2)}) collective-permute-start(f32[1,2,64,256]{3,2,1,0:T(8,128)S(1)} %collective-permute-done.1), channel_id=1, source_target_pairs={{0,1},{1,0},{2,3},{3,2},{4,5},{5,4},{6,7},{7,6},{8,9},{9,8},{10,11... | collective-permute-start | bytes 393224 | tf_op jit(solution)/shard_map/ppermute | solution.py:29
  16.7 5.5 %collective-permute-done.6 = f32[2,2,64,256]{3,2,1,0:T(8,128)} collective-permute-done((f32[2,2,64,256]{3,2,1,0:T(8,128)}, f32[2,2,64,256]{3,2,1,0:T(8,128)}, u32[]{:S(2)}, u32[]{:S(2)}) %collective-permute-start.6) | collective-permute-done | bytes 262176 | tf_op jit(solution)/shard_map/ppermute | solution.py:29
  22.2 2.8 %collective-permute-done.5 = f32[2,2,64,256]{3,2,1,0:T(8,128)} collective-permute-done((f32[2,2,64,256]{3,2,1,0:T(8,128)S(1)}, f32[2,2,64,256]{3,2,1,0:T(8,128)}, u32[]{:S(2)}, u32[]{:S(2)}) %collective-permute-start.5) | collective-permute-done | bytes 262176 | tf_op jit(solution)/shard_map/ppermute | solution.py:29
  25.1 3.1 %collective-permute-start.11 = (f32[2,2,64,256]{3,2,1,0:T(8,128)S(1)}, f32[2,2,64,256]{3,2,1,0:T(8,128)S(1)}, u32[]{:S(2)}, u32[]{:S(2)}) collective-permute-start(f32[2,2,64,256]{3,2,1,0:T(8,128)S(1)} %pad_maximum_fusion.2), channel_id=1, source_target_pairs={{0,128},{1,129},{2,130},{3,131},{4,132},{5,133},{6,134},{7,135},{8... | collective-permute-start | bytes 786440 | tf_op jit(solution)/shard_map/ppermute | solution.py:29
  41.2 2.7 %multiply.5.refs_0_ = f32[2,256,512]{2,1,0:T(8,128)S(1)} custom-call(s32[9]{0:T(128)S(1)} %stack.75.at._, f32[5,4,2,64,256]{4,3,2,1,0:T(8,128)S(1)} %stage.1.own_ref.own, f32[8,4,2,64,256]{4,3,2,1,0:T(8,128)} %bitcast.13.other_ref.other, f32[4,2,64,256]{3,2,1,0:T(8,128)S(1)} %constant_dynamic-update-slice_fusion.4.even_ref, ...), custom_call_target="tpu_custom_call", output_to_operand_aliasing={{}: (5, {})} | custom-call | flops 805306368 | bytes 2097152 | tf_op jit(solution)/shard_map/multiply/pallas_call | solution.py:189
  47.7 2.7 %multiply.6.refs_0_ = f32[2,256,512]{2,1,0:T(8,128)S(1)} custom-call(s32[9]{0:T(128)S(1)} %stack.75.at._, f32[5,4,2,64,256]{4,3,2,1,0:T(8,128)S(1)} %stage.1.own_ref.own, f32[8,4,2,64,256]{4,3,2,1,0:T(8,128)} %bitcast.13.other_ref.other, f32[4,2,64,256]{3,2,1,0:T(8,128)S(1)} %constant_dynamic-update-slice_fusion.2.even_ref, ...), custom_call_target="tpu_custom_call", output_to_operand_aliasing={{}: (5, {})} | custom-call | flops 805306368 | bytes 2097152 | tf_op jit(solution)/shard_map/multiply/pallas_call | solution.py:189
  50.4 2.7 %multiply.7.total = f32[2,256,512]{2,1,0:T(8,128)S(1)} custom-call(s32[9]{0:T(128)S(1)} %stack.75.at._, f32[5,4,2,64,256]{4,3,2,1,0:T(8,128)S(1)} %stage.1.own_ref.own, f32[8,4,2,64,256]{4,3,2,1,0:T(8,128)} %bitcast.13.other_ref.other, f32[4,2,64,256]{3,2,1,0:T(8,128)S(1)} %constant_dynamic-update-slice_fusion.6.even_ref, ...), custom_call_target="tpu_custom_call", output_to_operand_aliasing={{}: (5, {})} | custom-call | flops 805306368 | bytes 2097152 | tf_op jit(solution)/shard_map/multiply/pallas_call | solution.py:189
  54.0 3.5 %last.1 = (f32[2,4,4,24,256]{4,3,2,1,0:T(8,128)S(1)}, f32[2,4,64,512]{3,2,1,0:T(8,128)S(1)}) custom-call(s32[9]{0:T(128)S(1)} %stack.75.at._, f32[5,4,2,64,256]{4,3,2,1,0:T(8,128)S(1)} %stage.1.own_ref.own, f32[8,4,2,64,256]{4,3,2,1,0:T(8,128)} %bitcast.13.other_ref.other, f32[2,2,64,256]{3,2,1,0:T(8,128)S(1)} %collective-permute-done.12.even, ...), custom_call_target="tpu_custom_call" | custom-call | flops 1073741824 | bytes 2097152 | tf_op jit(solution)/shard_map/last/pallas_call | solution.py:232
  61.5 3.9 %invert.1 = (f32[256,256]{1,0:T(8,128)S(1)}, f32[256,256]{1,0:T(8,128)S(1)}) custom-call(s32[9]{0:T(128)S(1)} %stack.75.at._, f32[256,256]{1,0:T(8,128)S(1)} %copy-done, f32[256,256]{1,0:T(8,128)S(1)} %copy-done.1), custom_call_target="tpu_custom_call" | custom-call | flops 4294967296 | bytes 1048576 | tf_op jit(solution)/shard_map/invert/pallas_call | solution.py:291
  66.6 2.2 %collective-permute-start.25 = (f32[4,24,256]{2,1,0:T(8,128)S(1)}, f32[4,24,256]{2,1,0:T(8,128)S(1)}, u32[]{:S(2)}, u32[]{:S(2)}) collective-permute-start(f32[4,24,256]{2,1,0:T(8,128)S(1)} %slice_bitcast_fusion.4), channel_id=1, source_target_pairs={{0,192},{1,65},{2,194},{3,67},{4,196},{5,69},{6,198},{7,71},{8,200... | collective-permute-start | bytes 294920 | tf_op jit(solution)/shard_map/ppermute | solution.py:29
  70.1 2.6 %collective-permute-done.25 = f32[4,24,256]{2,1,0:T(8,128)S(1)} collective-permute-done((f32[4,24,256]{2,1,0:T(8,128)S(1)}, f32[4,24,256]{2,1,0:T(8,128)S(1)}, u32[]{:S(2)}, u32[]{:S(2)}) %collective-permute-start.25) | collective-permute-done | bytes 98336 | tf_op jit(solution)/shard_map/ppermute | solution.py:29
  74.5 2.5 %collective-permute-done.26 = f32[2,24,256]{2,1,0:T(8,128)S(1)} collective-permute-done((f32[2,24,256]{2,1,0:T(8,128)S(1)}, f32[2,24,256]{2,1,0:T(8,128)S(1)}, u32[]{:S(2)}, u32[]{:S(2)}) %collective-permute-start.26) | collective-permute-done | bytes 49184 | tf_op jit(solution)/shard_map/ppermute | solution.py:29
  77.9 2.9 %collective-permute-done.20 = f32[2,64,512]{2,1,0:T(8,128)S(1)} collective-permute-done((f32[2,64,512]{2,1,0:T(8,128)S(1)}, f32[2,64,512]{2,1,0:T(8,128)S(1)}, u32[]{:S(2)}, u32[]{:S(2)}) %collective-permute-start.20) | collective-permute-done | bytes 262176 | tf_op jit(solution)/shard_map/ppermute | solution.py:29
  83.3 2.3 %collective-permute-done.28 = f32[2,24,256]{2,1,0:T(8,128)S(1)} collective-permute-done((f32[2,24,256]{2,1,0:T(8,128)S(1)}, f32[2,24,256]{2,1,0:T(8,128)S(1)}, u32[]{:S(2)}, u32[]{:S(2)}) %collective-permute-start.28) | collective-permute-done | bytes 49184 | tf_op jit(solution)/shard_map/ppermute | solution.py:29
  85.6 3.2 %collective-permute-start.30 = (f32[2,24,256]{2,1,0:T(8,128)S(1)}, f32[2,24,256]{2,1,0:T(8,128)S(1)}, u32[]{:S(2)}, u32[]{:S(2)}) collective-permute-start(f32[2,24,256]{2,1,0:T(8,128)S(1)} %add.72), channel_id=1, source_target_pairs={{0,32},{1,33},{2,34},{3,35},{4,36},{5,37},{6,38},{7,39},{8,40},{9,... | collective-permute-start | bytes 147464 | tf_op jit(solution)/shard_map/ppermute | solution.py:29
  88.8 2.7 %collective-permute-start.31 = (f32[2,24,256]{2,1,0:T(8,128)S(1)}, f32[2,24,256]{2,1,0:T(8,128)S(1)}, u32[]{:S(2)}, u32[]{:S(2)}) collective-permute-start(f32[2,24,256]{2,1,0:T(8,128)S(1)} %add.72), channel_id=1, source_target_pairs={{0,48},{1,17},{2,50},{3,19},{4,52},{5,21},{6,54},{7,23},{8,56},{9,... | collective-permute-start | bytes 147464 | tf_op jit(solution)/shard_map/ppermute | solution.py:29
  98.4 2.7 %collective-permute-start.32 = (f32[2,24,256]{2,1,0:T(8,128)S(1)}, f32[2,24,256]{2,1,0:T(8,128)S(1)}, u32[]{:S(2)}, u32[]{:S(2)}) collective-permute-start(f32[2,24,256]{2,1,0:T(8,128)S(1)} %add_add_fusion), channel_id=1, source_target_pairs={{0,2},{1,7},{2,0},{3,5},{4,6},{5,3},{6,4},{7,1},{8,10},{9,15},{10,... | collective-permute-start | bytes 147464 | tf_op jit(solution)/shard_map/ppermute | solution.py:29
  105.0 4.2 %collective-permute-done.33 = f32[2,2,24,256]{3,2,1,0:T(8,128)S(1)} collective-permute-done((f32[2,2,24,256]{3,2,1,0:T(8,128)S(1)}, f32[2,2,24,256]{3,2,1,0:T(8,128)S(1)}, u32[]{:S(2)}, u32[]{:S(2)}) %collective-permute-start.33) | collective-permute-done | bytes 98336 | tf_op jit(solution)/shard_map/ppermute | solution.py:29
  109.3 5.7 %collective-permute-done.34 = f32[2,2,2,24,256]{4,3,2,1,0:T(8,128)S(1)} collective-permute-done((f32[2,2,2,24,256]{4,3,2,1,0:T(8,128)S(1)}, f32[2,2,2,24,256]{4,3,2,1,0:T(8,128)S(1)}, u32[]{:S(2)}, u32[]{:S(2)}) %collective-permute-start.34) | collective-permute-done | bytes 196640 | tf_op jit(solution)/shard_map/ppermute | solution.py:29
  115.1 4.5 %collective-permute-start.24 = (f32[2,64,256]{2,1,0:T(8,128)S(1)}, f32[2,64,256]{2,1,0:T(8,128)S(1)}, u32[]{:S(2)}, u32[]{:S(2)}) collective-permute-start(f32[2,64,256]{2,1,0:T(8,128)S(1)} %pad_maximum_fusion.7), channel_id=1, source_target_pairs={{0,0},{1,1},{2,128},{3,129},{4,4},{5,5},{6,132},{7,133},{8,8},{9,9... | collective-permute-start | bytes 393224 | tf_op jit(solution)/shard_map/ppermute | solution.py:29
  119.6 3.1 %finish.1 = (f32[256,256]{1,0:T(8,128)}, f32[256,256]{1,0:T(8,128)}, f32[256,256]{1,0:T(8,128)}) custom-call(s32[9]{0:T(128)S(1)} %stack.75.at._, f32[4,2,2,24,256]{4,3,2,1,0:T(8,128)S(1)} %pad_maximum_fusion.1.mine, f32[4,2,2,24,256]{4,3,2,1,0:T(8,128)S(1)} %collective-permute-done.35.other, bf16[1536,512]{1,0:T(8,128)(2,1)S(1)} %get-tuple-element.64.z_terms, ...), custom_call_target="tpu_custom_call" | custom-call | flops 268435456 | bytes 3145728 | tf_op jit(solution)/shard_map/finish/pallas_call | solution.py:413
  122.7 2.6 %collective-permute-done.24 = f32[2,64,256]{2,1,0:T(8,128)S(1)} collective-permute-done((f32[2,64,256]{2,1,0:T(8,128)S(1)}, f32[2,64,256]{2,1,0:T(8,128)S(1)}, u32[]{:S(2)}, u32[]{:S(2)}) %collective-permute-start.24) | collective-permute-done | bytes 131104 | tf_op jit(solution)/shard_map/ppermute | solution.py:29
  (105 shorter events, 48.9 us)
Async XLA Ops:
  1.6 7.4 %collective-permute-start.1 = (f32[1,2,64,256]{3,2,1,0:T(8,128)S(1)}, f32[1,2,64,256]{3,2,1,0:T(8,128)S(1)}, u32[]{:S(2)}, u32[]{:S(2)}) collective-permute-start(f32[1,2,64,256]{3,2,1,0:T(8,128)S(1)} %maximum_bitcast_fusion), channel_id=1, source_target_pairs={{0,4},{1,5},{2,6},{3,7},{4,0},{5,1},{6,2},{7,3},{8,12},{9,13},{10,... | collective-permute-start | bytes 393224 | tf_op jit(solution)/shard_map/ppermute | solution.py:29
  4.0 10.3 %collective-permute-start.3 = (f32[2,2,64,256]{3,2,1,0:T(8,128)S(1)}, f32[2,2,64,256]{3,2,1,0:T(8,128)S(1)}, u32[]{:S(2)}, u32[]{:S(2)}) collective-permute-start(f32[2,2,64,256]{3,2,1,0:T(8,128)S(1)} %pad_maximum_fusion.4), channel_id=1, source_target_pairs={{0,8},{1,57},{2,10},{3,59},{4,12},{5,61},{6,14},{7,63},{8,16},{9,1... | collective-permute-start | bytes 786440 | tf_op jit(solution)/shard_map/ppermute | solution.py:29
  14.3 20.4 %collective-permute-start.4 = (f32[4096,256]{1,0:T(8,128)}, f32[4096,256]{1,0:T(8,128)}, u32[]{:S(2)}, u32[]{:S(2)}) collective-permute-start(f32[4096,256]{1,0:T(8,128)} %param.6), channel_id=1, source_target_pairs={{0,1},{1,0},{2,3},{3,2},{4,5},{5,4},{6,7},{7,6},{8,9},{9,8},{10,11... | collective-permute-start | bytes 12582920 | tf_op jit(solution)/shard_map/ppermute | solution.py:29
  14.3 7.9 %collective-permute-start.6 = (f32[2,2,64,256]{3,2,1,0:T(8,128)}, f32[2,2,64,256]{3,2,1,0:T(8,128)}, u32[]{:S(2)}, u32[]{:S(2)}) collective-permute-start(f32[2,2,64,256]{3,2,1,0:T(8,128)} %constant_dynamic-update-slice_fusion), channel_id=1, source_target_pairs={{0,8},{1,57},{2,10},{3,59},{4,12},{5,61},{6,14},{7,63},{8,16},{9,1... | collective-permute-start | bytes 786440 | tf_op jit(solution)/shard_map/ppermute | solution.py:29
  14.3 7.9 %collective-permute-start.7 = (f32[2,2,64,256]{3,2,1,0:T(8,128)S(1)}, f32[2,2,64,256]{3,2,1,0:T(8,128)S(1)}, u32[]{:S(2)}, u32[]{:S(2)}) collective-permute-start(f32[2,2,64,256]{3,2,1,0:T(8,128)S(1)} %pad_maximum_fusion.3.even_ref), channel_id=1, source_target_pairs={{0,2},{1,7},{2,4},{3,1},{4,6},{5,3},{6,0},{7,5},{8,10},{9,15},{10,... | collective-permute-start | bytes 786440 | tf_op jit(solution)/shard_map/ppermute | solution.py:29
  14.9 10.1 %collective-permute-start.5 = (f32[2,2,64,256]{3,2,1,0:T(8,128)S(1)}, f32[2,2,64,256]{3,2,1,0:T(8,128)}, u32[]{:S(2)}, u32[]{:S(2)}) collective-permute-start(f32[2,2,64,256]{3,2,1,0:T(8,128)S(1)} %collective-permute-done.3), channel_id=1, source_target_pairs={{0,8},{1,57},{2,10},{3,59},{4,12},{5,61},{6,14},{7,63},{8,16},{9,1... | collective-permute-start | bytes 786440 | tf_op jit(solution)/shard_map/ppermute | solution.py:29
  22.2 8.1 %collective-permute-start.9 = (f32[2,2,64,256]{3,2,1,0:T(8,128)}, f32[2,2,64,256]{3,2,1,0:T(8,128)S(1)}, u32[]{:S(2)}, u32[]{:S(2)}) collective-permute-start(f32[2,2,64,256]{3,2,1,0:T(8,128)} %collective-permute-done.6), channel_id=1, source_target_pairs={{0,8},{1,57},{2,10},{3,59},{4,12},{5,61},{6,14},{7,63},{8,16},{9,1... | collective-permute-start | bytes 786440 | tf_op jit(solution)/shard_map/ppermute | solution.py:29
  25.0 8.3 %collective-permute-start.8 = (f32[2,2,64,256]{3,2,1,0:T(8,128)}, f32[2,2,64,256]{3,2,1,0:T(8,128)S(1)}, u32[]{:S(2)}, u32[]{:S(2)}) collective-permute-start(f32[2,2,64,256]{3,2,1,0:T(8,128)} %collective-permute-done.5), channel_id=1, source_target_pairs={{0,8},{1,57},{2,10},{3,59},{4,12},{5,61},{6,14},{7,63},{8,16},{9,1... | collective-permute-start | bytes 786440 | tf_op jit(solution)/shard_map/ppermute | solution.py:29
  25.1 11.9 %collective-permute-start.11 = (f32[2,2,64,256]{3,2,1,0:T(8,128)S(1)}, f32[2,2,64,256]{3,2,1,0:T(8,128)S(1)}, u32[]{:S(2)}, u32[]{:S(2)}) collective-permute-start(f32[2,2,64,256]{3,2,1,0:T(8,128)S(1)} %pad_maximum_fusion.2), channel_id=1, source_target_pairs={{0,128},{1,129},{2,130},{3,131},{4,132},{5,133},{6,134},{7,135},{8... | collective-permute-start | bytes 786440 | tf_op jit(solution)/shard_map/ppermute | solution.py:29
  29.2 12.0 %collective-permute-start.15 = (f32[4,2,64,256]{3,2,1,0:T(8,128)S(1)}, f32[4,2,64,256]{3,2,1,0:T(8,128)S(1)}, u32[]{:S(2)}, u32[]{:S(2)}) collective-permute-start(f32[4,2,64,256]{3,2,1,0:T(8,128)S(1)} %constant_dynamic-update-slice_fusion.4.even_ref), channel_id=1, source_target_pairs={{0,2},{1,7},{2,4},{3,1},{4,6},{5,3},{6,0},{7,5},{8,10},{9,15},{10,... | collective-permute-start | bytes 1572872 | tf_op jit(solution)/shard_map/ppermute | solution.py:29
  30.3 7.6 %collective-permute-start.10 = (f32[2,2,64,256]{3,2,1,0:T(8,128)S(1)}, f32[2,2,64,256]{3,2,1,0:T(8,128)S(1)}, u32[]{:S(2)}, u32[]{:S(2)}) collective-permute-start(f32[2,2,64,256]{3,2,1,0:T(8,128)S(1)} %collective-permute-done.9), channel_id=1, source_target_pairs={{0,8},{1,57},{2,10},{3,59},{4,12},{5,61},{6,14},{7,63},{8,16},{9,1... | collective-permute-start | bytes 786440 | tf_op jit(solution)/shard_map/ppermute | solution.py:29
  33.4 10.7 %collective-permute-start.14 = (f32[4,2,64,256]{3,2,1,0:T(8,128)S(1)}, f32[4,2,64,256]{3,2,1,0:T(8,128)S(1)}, u32[]{:S(2)}, u32[]{:S(2)}) collective-permute-start(f32[4,2,64,256]{3,2,1,0:T(8,128)S(1)} %constant_dynamic-update-slice_fusion.2.even_ref), channel_id=1, source_target_pairs={{0,2},{1,7},{2,4},{3,1},{4,6},{5,3},{6,0},{7,5},{8,10},{9,15},{10,... | collective-permute-start | bytes 1572872 | tf_op jit(solution)/shard_map/ppermute | solution.py:29
  37.9 7.7 %collective-permute-start.12 = (f32[2,2,64,256]{3,2,1,0:T(8,128)S(1)}, f32[2,2,64,256]{3,2,1,0:T(8,128)S(1)}, u32[]{:S(2)}, u32[]{:S(2)}) collective-permute-start(f32[2,2,64,256]{3,2,1,0:T(8,128)S(1)} %pad_maximum_fusion.5), channel_id=1, source_target_pairs={{0,8},{1,57},{2,10},{3,59},{4,12},{5,61},{6,14},{7,63},{8,16},{9,1... | collective-permute-start | bytes 786440 | tf_op jit(solution)/shard_map/ppermute | solution.py:29
  38.9 7.4 %collective-permute-start.13 = (f32[2,2,64,256]{3,2,1,0:T(8,128)S(1)}, f32[2,2,64,256]{3,2,1,0:T(8,128)S(1)}, u32[]{:S(2)}, u32[]{:S(2)}) collective-permute-start(f32[2,2,64,256]{3,2,1,0:T(8,128)S(1)} %broadcast_select_fusion), channel_id=1, source_target_pairs={{0,64},{1,65},{2,66},{3,67},{4,68},{5,69},{6,70},{7,71},{8,72},{9,... | collective-permute-start | bytes 786440 | tf_op jit(solution)/shard_map/ppermute | solution.py:29
  39.6 10.8 %collective-permute-start.17 = (f32[4,2,64,256]{3,2,1,0:T(8,128)S(1)}, f32[4,2,64,256]{3,2,1,0:T(8,128)S(1)}, u32[]{:S(2)}, u32[]{:S(2)}) collective-permute-start(f32[4,2,64,256]{3,2,1,0:T(8,128)S(1)} %constant_dynamic-update-slice_fusion.6.even_ref), channel_id=1, source_target_pairs={{0,2},{1,7},{2,4},{3,1},{4,6},{5,3},{6,0},{7,5},{8,10},{9,15},{10,... | collective-permute-start | bytes 1572872 | tf_op jit(solution)/shard_map/ppermute | solution.py:29
  46.3 6.8 %collective-permute-start.18 = (f32[4,2,64,256]{3,2,1,0:T(8,128)S(1)}, f32[4,2,64,256]{3,2,1,0:T(8,128)S(1)}, u32[]{:S(2)}, u32[]{:S(2)}) collective-permute-start(f32[4,2,64,256]{3,2,1,0:T(8,128)S(1)} %pad_maximum_fusion.mine), channel_id=1, source_target_pairs={{0,1},{1,0},{2,3},{3,2},{4,5},{5,4},{6,7},{7,6},{8,9},{9,8},{10,11... | collective-permute-start | bytes 1572872 | tf_op jit(solution)/shard_map/ppermute | solution.py:29
  46.4 7.7 %collective-permute-start.16 = (f32[2,2,64,256]{3,2,1,0:T(8,128)S(1)}, f32[2,2,64,256]{3,2,1,0:T(8,128)S(1)}, u32[]{:S(2)}, u32[]{:S(2)}) collective-permute-start(f32[2,2,64,256]{3,2,1,0:T(8,128)S(1)} %collective-permute-done.12.even), channel_id=1, source_target_pairs={{0,2},{1,7},{2,4},{3,1},{4,6},{5,3},{6,0},{7,5},{8,10},{9,15},{10,... | collective-permute-start | bytes 786440 | tf_op jit(solution)/shard_map/ppermute | solution.py:29
  59.4 6.0 %collective-permute-start.19 = (f32[4,64,512]{2,1,0:T(8,128)S(1)}, f32[4,64,512]{2,1,0:T(8,128)S(1)}, u32[]{:S(2)}, u32[]{:S(2)}) collective-permute-start(f32[4,64,512]{2,1,0:T(8,128)S(1)} %slice_bitcast_fusion), channel_id=1, source_target_pairs={{0,1},{1,0},{2,3},{3,2},{4,5},{5,4},{6,7},{7,6},{8,9},{9,8},{10,11... | collective-permute-start | bytes 1572872 | tf_op jit(solution)/shard_map/ppermute | solution.py:29
  66.6 6.1 %collective-permute-start.25 = (f32[4,24,256]{2,1,0:T(8,128)S(1)}, f32[4,24,256]{2,1,0:T(8,128)S(1)}, u32[]{:S(2)}, u32[]{:S(2)}) collective-permute-start(f32[4,24,256]{2,1,0:T(8,128)S(1)} %slice_bitcast_fusion.4), channel_id=1, source_target_pairs={{0,192},{1,65},{2,194},{3,67},{4,196},{5,69},{6,198},{7,71},{8,200... | collective-permute-start | bytes 294920 | tf_op jit(solution)/shard_map/ppermute | solution.py:29
  74.4 6.5 %collective-permute-start.20 = (f32[2,64,512]{2,1,0:T(8,128)S(1)}, f32[2,64,512]{2,1,0:T(8,128)S(1)}, u32[]{:S(2)}, u32[]{:S(2)}) collective-permute-start(f32[2,64,512]{2,1,0:T(8,128)S(1)} %slice.81), channel_id=1, source_target_pairs={{0,64},{1,193},{2,66},{3,195},{4,68},{5,197},{6,70},{7,199},{8,72}... | collective-permute-start | bytes 786440 | tf_op jit(solution)/shard_map/ppermute | solution.py:29
  85.6 8.7 %collective-permute-start.30 = (f32[2,24,256]{2,1,0:T(8,128)S(1)}, f32[2,24,256]{2,1,0:T(8,128)S(1)}, u32[]{:S(2)}, u32[]{:S(2)}) collective-permute-start(f32[2,24,256]{2,1,0:T(8,128)S(1)} %add.72), channel_id=1, source_target_pairs={{0,32},{1,33},{2,34},{3,35},{4,36},{5,37},{6,38},{7,39},{8,40},{9,... | collective-permute-start | bytes 147464 | tf_op jit(solution)/shard_map/ppermute | solution.py:29
  88.8 6.2 %collective-permute-start.31 = (f32[2,24,256]{2,1,0:T(8,128)S(1)}, f32[2,24,256]{2,1,0:T(8,128)S(1)}, u32[]{:S(2)}, u32[]{:S(2)}) collective-permute-start(f32[2,24,256]{2,1,0:T(8,128)S(1)} %add.72), channel_id=1, source_target_pairs={{0,48},{1,17},{2,50},{3,19},{4,52},{5,21},{6,54},{7,23},{8,56},{9,... | collective-permute-start | bytes 147464 | tf_op jit(solution)/shard_map/ppermute | solution.py:29
  92.2 6.3 %collective-permute-start.21 = (f32[64,512]{1,0:T(8,128)S(1)}, f32[64,512]{1,0:T(8,128)S(1)}, u32[]{:S(2)}, u32[]{:S(2)}) collective-permute-start(f32[64,512]{1,0:T(8,128)S(1)} %get-tuple-element.77), channel_id=1, source_target_pairs={{0,192},{1,65},{2,194},{3,67},{4,196},{5,69},{6,198},{7,71},{8,200... | collective-permute-start | bytes 393224 | tf_op jit(solution)/shard_map/ppermute | solution.py:29
  115.1 10.2 %collective-permute-start.24 = (f32[2,64,256]{2,1,0:T(8,128)S(1)}, f32[2,64,256]{2,1,0:T(8,128)S(1)}, u32[]{:S(2)}, u32[]{:S(2)}) collective-permute-start(f32[2,64,256]{2,1,0:T(8,128)S(1)} %pad_maximum_fusion.7), channel_id=1, source_target_pairs={{0,0},{1,1},{2,128},{3,129},{4,4},{5,5},{6,132},{7,133},{8,8},{9,9... | collective-permute-start | bytes 393224 | tf_op jit(solution)/shard_map/ppermute | solution.py:29
  (15 other events, 70.2 us)

commit v4 on v3

--- a/solution.py
+++ b/solution.py
@@ -56,8 +56,20 @@
     return send(block, lambda x, y, z, s: (x, y, ((z + NZ - s) % NZ ^ far) + s, s))
 
 
-def to_near(block):
-    return to_pair(block, 1)
+def to_pair_y(block):
+    return send(block, lambda x, y, z, s: (x, y ^ SLOTS[s][1], ((z + NZ - s) % NZ ^ 1) + s, s))
+
+
+def to_second_x(block):
+    return swap(block, "x", 1)
+
+
+def to_first_y(block):
+    return swap(block, "y", 0)
+
+
+def to_both(block):
+    return send(block, lambda x, y, z, s: (x ^ SLOTS[s][1], y ^ SLOTS[s][2], z, s))
 
 
 def after(value, *earlier):
@@ -482,30 +494,23 @@
     q = pieces[0] + to_core(pieces[1])
     x1, x0 = invert(after(place, part), diag_one, diag_zero)
     part = part[:2] + after(came, x1, x0, q)
-    came = swap(part[1], "x", 1)
+    part = part.reshape(2, 2, 2, N, B)
+    a, b, c = to_second_x(part[1, 0]), to_first_y(part[0, 1]), to_both(part[1, 1])
     z_terms, zt_terms, base = constants(x1, x0, after(link, part))
-    part = part[0] + after(came, base)
+    part = (part[0, 0] + after(a, base)) + (b + c)
+    a, b, c = swap(part, "y", 1), to_pair(part, 1), to_pair_y(part)
     q = q[:2] + swap(q[2:], "x", 0)
-    part = part[:2] + swap(part[2:], "y", 0)
-    part = part + swap(part, "y", 1)
-    part = after(part, q)
-    part = part + to_near(part)
+    part = after((part + a) + (b + c), q)
+    a, b, c = (to_pair(part, far) for far in (2, 4, 6))
     came = swap(q[1], "x", 1)
-    a, b, c = (to_pair(part, far) for far in (2, 4, 6))
     part = after((part + a) + (b + c), came)
     s1, s0 = rows(q[0], came, z_terms)
-    part = jnp.stack([part, after(swap(part, "y", 0), s1, s0)])
-
-    def home(block):
-        return send(block, lambda x, y, z, s: (y % 2 * 2 + x % 2, y // 2 * 2 + x // 2, z, s))
-
-    sigmas = home(jnp.stack([s1, s0]))
-    part = jnp.stack([part, swap(part, "x", 1)])
-    mine = jnp.concatenate([part, swap(part, "x", 0)], axis=0)
+    a, b, c = to_second_x(part), to_first_y(part), to_both(part)
+    part = jnp.stack([jnp.stack([part, after(b, s1, s0)]), jnp.stack([a, c])])
+    sigmas = send(jnp.stack([s1, s0]), lambda x, y, z, s: (y % 2 * 2 + x % 2, y // 2 * 2 + x // 2, z, s))
+    mine = after(jnp.concatenate([part, swap(part, "x", 0)], axis=0), sigmas)
     s11, s10, s00 = finish(place, mine, to_core(mine), z_terms, zt_terms, base)
-    sigmas = after(sigmas, s11)
-    s1, s0 = sigmas[0], sigmas[1]
-    return s1, s11, s0, s10, s00
+    return sigmas[0], s11, sigmas[1], s10, s00
 
 
 def solution(mesh):

time: 127 us -> 125 us (0.984)
  waiting for transfers between devices: 44.1 us -> 40.2 us
  starting transfers between devices: 49.5 us -> 51.2 us
    ppermute x36 -> x39, waiting for transfers between devices: 44.1 us -> 40.2 us  [send(): return lax.ppermute(block, AXES, pairs)]
    ppermute x36 -> x39, starting transfers between devices: 49.5 us -> 51.2 us  [send(): return lax.ppermute(block, AXES, pairs)]
  transfers between devices with their start and end apart: 36 -> 39, of which waited for: 23 -> 23; matrix products, arithmetic and copies ran while one was open for 3% -> 4% of each run, Pallas kernels for 18% -> 15%
where the time goes in v4:
time: 125 us; the launch traced here: 124 us
  starting transfers between devices  51.2 us (41%)
  waiting for transfers between devices  40.2 us (32%)
  Pallas kernels  25.7 us (21%)
  local copies, waits for them, and re-layouts  4.24 us (3%)
  other arithmetic  1.35 us (1%)
    ppermute x39, starting transfers between devices, send(): return lax.ppermute(block, AXES, pairs)  51.2 us
    ppermute x39, waiting for transfers between devices, send(): return lax.ppermute(block, AXES, pairs)  40.2 us
    pallas_call x4, Pallas kernels, multiply(): pl.pallas_call(kernel, in_specs=[SMEM, VMEM, HBM] + [VMEM] * (2 + len(tot...  10.3 us
    pallas_call x1, Pallas kernels, invert(): pl.pallas_call(invert_kernel, in_specs=[SMEM, HBM, HBM], out_specs=[VMEM,...  3.94 us
    pallas_call x1, Pallas kernels, last(): pl.pallas_call(last_kernel, in_specs=[SMEM, VMEM, HBM] + [VMEM] * 4, out_...  3.55 us
    pallas_call x1, Pallas kernels, finish(): pl.pallas_call(finish_kernel, in_specs=[SMEM] + [VMEM] * 5, out_specs=[VM...  3.14 us
  transfers between devices with their start and end apart: 39, of which 23 were waited for; matrix products, arithmetic and copies ran while one was open for 4% of the time, Pallas kernels for 15%

profile of v4, /device:TPU:8, one launch (start us, length us, event | category | flops | bytes accessed | tf_op | source)
XLA Modules:
  0.0 123.8 jit_solution(3157470397078212856)
XLA Ops:
  1.6 2.4 %collective-permute-start.1 = (f32[1,2,64,256]{3,2,1,0:T(8,128)S(1)}, f32[1,2,64,256]{3,2,1,0:T(8,128)S(1)}, u32[]{:S(2)}, u32[]{:S(2)}) collective-permute-start(f32[1,2,64,256]{3,2,1,0:T(8,128)S(1)} %maximum_bitcast_fusion), channel_id=1, source_target_pairs={{0,4},{1,5},{2,6},{3,7},{4,0},{5,1},{6,2},{7,3},{8,12},{9,13},{10,... | collective-permute-start | bytes 393224 | tf_op jit(solution)/shard_map/ppermute | solution.py:29
  6.1 2.3 %stage.1.own_ref.own = f32[5,4,2,64,256]{4,3,2,1,0:T(8,128)S(1)} custom-call(s32[9]{0:T(128)S(1)} %stack.84.at._, f32[8,4,2,64,256]{4,3,2,1,0:T(8,128)} %bitcast.12.ref), custom_call_target="tpu_custom_call" | custom-call | bytes 5242880 | tf_op jit(solution)/shard_map/stage/pallas_call | solution.py:146
  9.0 3.2 %collective-permute-start.2 = (f32[1,2,64,256]{3,2,1,0:T(8,128)S(1)}, f32[1,2,64,256]{3,2,1,0:T(8,128)S(1)}, u32[]{:S(2)}, u32[]{:S(2)}) collective-permute-start(f32[1,2,64,256]{3,2,1,0:T(8,128)S(1)} %collective-permute-done.1), channel_id=1, source_target_pairs={{0,1},{1,0},{2,3},{3,2},{4,5},{5,4},{6,7},{7,6},{8,9},{9,8},{10,11... | collective-permute-start | bytes 393224 | tf_op jit(solution)/shard_map/ppermute | solution.py:29
  16.7 5.5 %collective-permute-done.6 = f32[2,2,64,256]{3,2,1,0:T(8,128)} collective-permute-done((f32[2,2,64,256]{3,2,1,0:T(8,128)}, f32[2,2,64,256]{3,2,1,0:T(8,128)}, u32[]{:S(2)}, u32[]{:S(2)}) %collective-permute-start.6) | collective-permute-done | bytes 262176 | tf_op jit(solution)/shard_map/ppermute | solution.py:29
  22.2 2.8 %collective-permute-done.5 = f32[2,2,64,256]{3,2,1,0:T(8,128)} collective-permute-done((f32[2,2,64,256]{3,2,1,0:T(8,128)S(1)}, f32[2,2,64,256]{3,2,1,0:T(8,128)}, u32[]{:S(2)}, u32[]{:S(2)}) %collective-permute-start.5) | collective-permute-done | bytes 262176 | tf_op jit(solution)/shard_map/ppermute | solution.py:29
  25.1 3.1 %collective-permute-start.11 = (f32[2,2,64,256]{3,2,1,0:T(8,128)S(1)}, f32[2,2,64,256]{3,2,1,0:T(8,128)S(1)}, u32[]{:S(2)}, u32[]{:S(2)}) collective-permute-start(f32[2,2,64,256]{3,2,1,0:T(8,128)S(1)} %pad_maximum_fusion.2), channel_id=1, source_target_pairs={{0,128},{1,129},{2,130},{3,131},{4,132},{5,133},{6,134},{7,135},{8... | collective-permute-start | bytes 786440 | tf_op jit(solution)/shard_map/ppermute | solution.py:29
  30.3 2.0 %collective-permute-start.10 = (f32[2,2,64,256]{3,2,1,0:T(8,128)S(1)}, f32[2,2,64,256]{3,2,1,0:T(8,128)S(1)}, u32[]{:S(2)}, u32[]{:S(2)}) collective-permute-start(f32[2,2,64,256]{3,2,1,0:T(8,128)S(1)} %collective-permute-done.9), channel_id=1, source_target_pairs={{0,8},{1,57},{2,10},{3,59},{4,12},{5,61},{6,14},{7,63},{8,16},{9,1... | collective-permute-start | bytes 786440 | tf_op jit(solution)/shard_map/ppermute | solution.py:29
  34.7 2.2 %multiply.4.refs_0_ = f32[2,256,512]{2,1,0:T(8,128)S(1)} custom-call(s32[9]{0:T(128)S(1)} %stack.84.at._, f32[5,4,2,64,256]{4,3,2,1,0:T(8,128)S(1)} %stage.1.own_ref.own, f32[8,4,2,64,256]{4,3,2,1,0:T(8,128)} %bitcast.13.other_ref.other, f32[2,2,64,256]{3,2,1,0:T(8,128)S(1)} %pad_maximum_fusion.3.even_ref, f32[2,2,64,256]{3,2,1,0:T(8,128)S(1)} %collective-permute-done.7.odd_ref), custom_call_target="tpu_custom_call" | custom-call | flops 805306368 | bytes 2097152 | tf_op jit(solution)/shard_map/multiply/pallas_call | solution.py:201
  41.2 2.7 %multiply.5.refs_0_ = f32[2,256,512]{2,1,0:T(8,128)S(1)} custom-call(s32[9]{0:T(128)S(1)} %stack.84.at._, f32[5,4,2,64,256]{4,3,2,1,0:T(8,128)S(1)} %stage.1.own_ref.own, f32[8,4,2,64,256]{4,3,2,1,0:T(8,128)} %bitcast.13.other_ref.other, f32[4,2,64,256]{3,2,1,0:T(8,128)S(1)} %constant_dynamic-update-slice_fusion.4.even_ref, ...), custom_call_target="tpu_custom_call", output_to_operand_aliasing={{}: (5, {})} | custom-call | flops 805306368 | bytes 2097152 | tf_op jit(solution)/shard_map/multiply/pallas_call | solution.py:201
  47.7 2.7 %multiply.6.refs_0_ = f32[2,256,512]{2,1,0:T(8,128)S(1)} custom-call(s32[9]{0:T(128)S(1)} %stack.84.at._, f32[5,4,2,64,256]{4,3,2,1,0:T(8,128)S(1)} %stage.1.own_ref.own, f32[8,4,2,64,256]{4,3,2,1,0:T(8,128)} %bitcast.13.other_ref.other, f32[4,2,64,256]{3,2,1,0:T(8,128)S(1)} %constant_dynamic-update-slice_fusion.2.even_ref, ...), custom_call_target="tpu_custom_call", output_to_operand_aliasing={{}: (5, {})} | custom-call | flops 805306368 | bytes 2097152 | tf_op jit(solution)/shard_map/multiply/pallas_call | solution.py:201
  50.4 2.7 %multiply.7.total = f32[2,256,512]{2,1,0:T(8,128)S(1)} custom-call(s32[9]{0:T(128)S(1)} %stack.84.at._, f32[5,4,2,64,256]{4,3,2,1,0:T(8,128)S(1)} %stage.1.own_ref.own, f32[8,4,2,64,256]{4,3,2,1,0:T(8,128)} %bitcast.13.other_ref.other, f32[4,2,64,256]{3,2,1,0:T(8,128)S(1)} %constant_dynamic-update-slice_fusion.6.even_ref, ...), custom_call_target="tpu_custom_call", output_to_operand_aliasing={{}: (5, {})} | custom-call | flops 805306368 | bytes 2097152 | tf_op jit(solution)/shard_map/multiply/pallas_call | solution.py:201
  54.0 3.5 %last.1 = (f32[2,4,4,24,256]{4,3,2,1,0:T(8,128)S(1)}, f32[2,4,64,512]{3,2,1,0:T(8,128)S(1)}) custom-call(s32[9]{0:T(128)S(1)} %stack.84.at._, f32[5,4,2,64,256]{4,3,2,1,0:T(8,128)S(1)} %stage.1.own_ref.own, f32[8,4,2,64,256]{4,3,2,1,0:T(8,128)} %bitcast.13.other_ref.other, f32[2,2,64,256]{3,2,1,0:T(8,128)S(1)} %collective-permute-done.12.even, ...), custom_call_target="tpu_custom_call" | custom-call | flops 1073741824 | bytes 2097152 | tf_op jit(solution)/shard_map/last/pallas_call | solution.py:244
  61.5 3.9 %invert.1 = (f32[256,256]{1,0:T(8,128)S(1)}, f32[256,256]{1,0:T(8,128)S(1)}) custom-call(s32[9]{0:T(128)S(1)} %stack.84.at._, f32[256,256]{1,0:T(8,128)S(1)} %copy-done, f32[256,256]{1,0:T(8,128)S(1)} %copy-done.1), custom_call_target="tpu_custom_call" | custom-call | flops 4294967296 | bytes 1048576 | tf_op jit(solution)/shard_map/invert/pallas_call | solution.py:303
  66.7 2.2 %collective-permute-start.25 = (f32[2,24,256]{2,1,0:T(8,128)S(1)}, f32[2,24,256]{2,1,0:T(8,128)S(1)}, u32[]{:S(2)}, u32[]{:S(2)}) collective-permute-start(f32[2,24,256]{2,1,0:T(8,128)S(1)} %get-tuple-element.81), channel_id=1, source_target_pairs={{0,192},{1,65},{2,194},{3,67},{4,196},{5,69},{6,198},{7,71},{8,200... | collective-permute-start | bytes 147464 | tf_op jit(solution)/shard_map/ppermute | solution.py:29
  73.0 3.6 %collective-permute-done.27 = f32[2,24,256]{2,1,0:T(8,128)S(1)} collective-permute-done((f32[2,24,256]{2,1,0:T(8,128)S(1)}, f32[2,24,256]{2,1,0:T(8,128)S(1)}, u32[]{:S(2)}, u32[]{:S(2)}) %collective-permute-start.27) | collective-permute-done | bytes 49184 | tf_op jit(solution)/shard_map/ppermute | solution.py:29
  80.7 2.4 %collective-permute-done.30 = f32[2,24,256]{2,1,0:T(8,128)S(1)} collective-permute-done((f32[2,24,256]{2,1,0:T(8,128)S(1)}, f32[2,24,256]{2,1,0:T(8,128)S(1)}, u32[]{:S(2)}, u32[]{:S(2)}) %collective-permute-start.30) | collective-permute-done | bytes 49184 | tf_op jit(solution)/shard_map/ppermute | solution.py:29
  83.7 2.9 %collective-permute-done.20 = f32[2,64,512]{2,1,0:T(8,128)S(1)} collective-permute-done((f32[2,64,512]{2,1,0:T(8,128)S(1)}, f32[2,64,512]{2,1,0:T(8,128)S(1)}, u32[]{:S(2)}, u32[]{:S(2)}) %collective-permute-start.20) | collective-permute-done | bytes 262176 | tf_op jit(solution)/shard_map/ppermute | solution.py:29
  86.6 3.3 %collective-permute-start.32 = (f32[2,24,256]{2,1,0:T(8,128)S(1)}, f32[2,24,256]{2,1,0:T(8,128)S(1)}, u32[]{:S(2)}, u32[]{:S(2)}) collective-permute-start(f32[2,24,256]{2,1,0:T(8,128)S(1)} %add_add_fusion.1), channel_id=1, source_target_pairs={{0,32},{1,33},{2,34},{3,35},{4,36},{5,37},{6,38},{7,39},{8,40},{9,... | collective-permute-start | bytes 147464 | tf_op jit(solution)/shard_map/ppermute | solution.py:29
  90.0 2.5 %collective-permute-start.33 = (f32[2,24,256]{2,1,0:T(8,128)S(1)}, f32[2,24,256]{2,1,0:T(8,128)S(1)}, u32[]{:S(2)}, u32[]{:S(2)}) collective-permute-start(f32[2,24,256]{2,1,0:T(8,128)S(1)} %add_add_fusion.1), channel_id=1, source_target_pairs={{0,48},{1,17},{2,50},{3,19},{4,52},{5,21},{6,54},{7,23},{8,56},{9,... | collective-permute-start | bytes 147464 | tf_op jit(solution)/shard_map/ppermute | solution.py:29
  97.5 2.0 %collective-permute-done.21.b = f32[64,512]{1,0:T(8,128)S(1)} collective-permute-done((f32[64,512]{1,0:T(8,128)S(1)}, f32[64,512]{1,0:T(8,128)S(1)}, u32[]{:S(2)}, u32[]{:S(2)}) %collective-permute-start.21) | collective-permute-done | bytes 131104 | tf_op jit(solution)/shard_map/ppermute | solution.py:29
  104.6 4.8 %collective-permute-done.36 = f32[2,24,256]{2,1,0:T(8,128)S(1)} collective-permute-done((f32[2,24,256]{2,1,0:T(8,128)S(1)}, f32[2,24,256]{2,1,0:T(8,128)S(1)}, u32[]{:S(2)}, u32[]{:S(2)}) %collective-permute-start.36) | collective-permute-done | bytes 49184 | tf_op jit(solution)/shard_map/ppermute | solution.py:29
  109.6 4.6 %collective-permute-start.24 = (f32[2,64,256]{2,1,0:T(8,128)S(1)}, f32[2,64,256]{2,1,0:T(8,128)S(1)}, u32[]{:S(2)}, u32[]{:S(2)}) collective-permute-start(f32[2,64,256]{2,1,0:T(8,128)S(1)} %pad_maximum_fusion.7), channel_id=1, source_target_pairs={{0,0},{1,1},{2,128},{3,129},{4,4},{5,5},{6,132},{7,133},{8,8},{9,9... | collective-permute-start | bytes 393224 | tf_op jit(solution)/shard_map/ppermute | solution.py:29
  115.3 3.6 %collective-permute-done.24 = f32[2,64,256]{2,1,0:T(8,128)S(1)} collective-permute-done((f32[2,64,256]{2,1,0:T(8,128)S(1)}, f32[2,64,256]{2,1,0:T(8,128)S(1)}, u32[]{:S(2)}, u32[]{:S(2)}) %collective-permute-start.24) | collective-permute-done | bytes 131104 | tf_op jit(solution)/shard_map/ppermute | solution.py:29
  120.6 3.1 %finish.1 = (f32[256,256]{1,0:T(8,128)}, f32[256,256]{1,0:T(8,128)}, f32[256,256]{1,0:T(8,128)}) custom-call(s32[9]{0:T(128)S(1)} %stack.84.at._, f32[4,2,2,24,256]{4,3,2,1,0:T(8,128)S(1)} %pad_maximum_fusion.1.mine, f32[4,2,2,24,256]{4,3,2,1,0:T(8,128)S(1)} %collective-permute-done.38.other, bf16[1536,512]{1,0:T(8,128)(2,1)S(1)} %get-tuple-element.64.z_terms, ...), custom_call_target="tpu_custom_call" | custom-call | flops 268435456 | bytes 3145728 | tf_op jit(solution)/shard_map/finish/pallas_call | solution.py:425
  (109 shorter events, 48.5 us)
Async XLA Ops:
  1.6 7.4 %collective-permute-start.1 = (f32[1,2,64,256]{3,2,1,0:T(8,128)S(1)}, f32[1,2,64,256]{3,2,1,0:T(8,128)S(1)}, u32[]{:S(2)}, u32[]{:S(2)}) collective-permute-start(f32[1,2,64,256]{3,2,1,0:T(8,128)S(1)} %maximum_bitcast_fusion), channel_id=1, source_target_pairs={{0,4},{1,5},{2,6},{3,7},{4,0},{5,1},{6,2},{7,3},{8,12},{9,13},{10,... | collective-permute-start | bytes 393224 | tf_op jit(solution)/shard_map/ppermute | solution.py:29
  4.0 10.3 %collective-permute-start.3 = (f32[2,2,64,256]{3,2,1,0:T(8,128)S(1)}, f32[2,2,64,256]{3,2,1,0:T(8,128)S(1)}, u32[]{:S(2)}, u32[]{:S(2)}) collective-permute-start(f32[2,2,64,256]{3,2,1,0:T(8,128)S(1)} %pad_maximum_fusion.4), channel_id=1, source_target_pairs={{0,8},{1,57},{2,10},{3,59},{4,12},{5,61},{6,14},{7,63},{8,16},{9,1... | collective-permute-start | bytes 786440 | tf_op jit(solution)/shard_map/ppermute | solution.py:29
  14.3 20.4 %collective-permute-start.4 = (f32[4096,256]{1,0:T(8,128)}, f32[4096,256]{1,0:T(8,128)}, u32[]{:S(2)}, u32[]{:S(2)}) collective-permute-start(f32[4096,256]{1,0:T(8,128)} %param.6), channel_id=1, source_target_pairs={{0,1},{1,0},{2,3},{3,2},{4,5},{5,4},{6,7},{7,6},{8,9},{9,8},{10,11... | collective-permute-start | bytes 12582920 | tf_op jit(solution)/shard_map/ppermute | solution.py:29
  14.3 7.9 %collective-permute-start.6 = (f32[2,2,64,256]{3,2,1,0:T(8,128)}, f32[2,2,64,256]{3,2,1,0:T(8,128)}, u32[]{:S(2)}, u32[]{:S(2)}) collective-permute-start(f32[2,2,64,256]{3,2,1,0:T(8,128)} %constant_dynamic-update-slice_fusion), channel_id=1, source_target_pairs={{0,8},{1,57},{2,10},{3,59},{4,12},{5,61},{6,14},{7,63},{8,16},{9,1... | collective-permute-start | bytes 786440 | tf_op jit(solution)/shard_map/ppermute | solution.py:29
  14.3 7.9 %collective-permute-start.7 = (f32[2,2,64,256]{3,2,1,0:T(8,128)S(1)}, f32[2,2,64,256]{3,2,1,0:T(8,128)S(1)}, u32[]{:S(2)}, u32[]{:S(2)}) collective-permute-start(f32[2,2,64,256]{3,2,1,0:T(8,128)S(1)} %pad_maximum_fusion.3.even_ref), channel_id=1, source_target_pairs={{0,2},{1,7},{2,4},{3,1},{4,6},{5,3},{6,0},{7,5},{8,10},{9,15},{10,... | collective-permute-start | bytes 786440 | tf_op jit(solution)/shard_map/ppermute | solution.py:29
  14.9 10.1 %collective-permute-start.5 = (f32[2,2,64,256]{3,2,1,0:T(8,128)S(1)}, f32[2,2,64,256]{3,2,1,0:T(8,128)}, u32[]{:S(2)}, u32[]{:S(2)}) collective-permute-start(f32[2,2,64,256]{3,2,1,0:T(8,128)S(1)} %collective-permute-done.3), channel_id=1, source_target_pairs={{0,8},{1,57},{2,10},{3,59},{4,12},{5,61},{6,14},{7,63},{8,16},{9,1... | collective-permute-start | bytes 786440 | tf_op jit(solution)/shard_map/ppermute | solution.py:29
  22.2 8.1 %collective-permute-start.9 = (f32[2,2,64,256]{3,2,1,0:T(8,128)}, f32[2,2,64,256]{3,2,1,0:T(8,128)S(1)}, u32[]{:S(2)}, u32[]{:S(2)}) collective-permute-start(f32[2,2,64,256]{3,2,1,0:T(8,128)} %collective-permute-done.6), channel_id=1, source_target_pairs={{0,8},{1,57},{2,10},{3,59},{4,12},{5,61},{6,14},{7,63},{8,16},{9,1... | collective-permute-start | bytes 786440 | tf_op jit(solution)/shard_map/ppermute | solution.py:29
  25.0 8.3 %collective-permute-start.8 = (f32[2,2,64,256]{3,2,1,0:T(8,128)}, f32[2,2,64,256]{3,2,1,0:T(8,128)S(1)}, u32[]{:S(2)}, u32[]{:S(2)}) collective-permute-start(f32[2,2,64,256]{3,2,1,0:T(8,128)} %collective-permute-done.5), channel_id=1, source_target_pairs={{0,8},{1,57},{2,10},{3,59},{4,12},{5,61},{6,14},{7,63},{8,16},{9,1... | collective-permute-start | bytes 786440 | tf_op jit(solution)/shard_map/ppermute | solution.py:29
  25.1 11.9 %collective-permute-start.11 = (f32[2,2,64,256]{3,2,1,0:T(8,128)S(1)}, f32[2,2,64,256]{3,2,1,0:T(8,128)S(1)}, u32[]{:S(2)}, u32[]{:S(2)}) collective-permute-start(f32[2,2,64,256]{3,2,1,0:T(8,128)S(1)} %pad_maximum_fusion.2), channel_id=1, source_target_pairs={{0,128},{1,129},{2,130},{3,131},{4,132},{5,133},{6,134},{7,135},{8... | collective-permute-start | bytes 786440 | tf_op jit(solution)/shard_map/ppermute | solution.py:29
  29.2 12.0 %collective-permute-start.15 = (f32[4,2,64,256]{3,2,1,0:T(8,128)S(1)}, f32[4,2,64,256]{3,2,1,0:T(8,128)S(1)}, u32[]{:S(2)}, u32[]{:S(2)}) collective-permute-start(f32[4,2,64,256]{3,2,1,0:T(8,128)S(1)} %constant_dynamic-update-slice_fusion.4.even_ref), channel_id=1, source_target_pairs={{0,2},{1,7},{2,4},{3,1},{4,6},{5,3},{6,0},{7,5},{8,10},{9,15},{10,... | collective-permute-start | bytes 1572872 | tf_op jit(solution)/shard_map/ppermute | solution.py:29
  30.3 7.6 %collective-permute-start.10 = (f32[2,2,64,256]{3,2,1,0:T(8,128)S(1)}, f32[2,2,64,256]{3,2,1,0:T(8,128)S(1)}, u32[]{:S(2)}, u32[]{:S(2)}) collective-permute-start(f32[2,2,64,256]{3,2,1,0:T(8,128)S(1)} %collective-permute-done.9), channel_id=1, source_target_pairs={{0,8},{1,57},{2,10},{3,59},{4,12},{5,61},{6,14},{7,63},{8,16},{9,1... | collective-permute-start | bytes 786440 | tf_op jit(solution)/shard_map/ppermute | solution.py:29
  33.4 10.7 %collective-permute-start.14 = (f32[4,2,64,256]{3,2,1,0:T(8,128)S(1)}, f32[4,2,64,256]{3,2,1,0:T(8,128)S(1)}, u32[]{:S(2)}, u32[]{:S(2)}) collective-permute-start(f32[4,2,64,256]{3,2,1,0:T(8,128)S(1)} %constant_dynamic-update-slice_fusion.2.even_ref), channel_id=1, source_target_pairs={{0,2},{1,7},{2,4},{3,1},{4,6},{5,3},{6,0},{7,5},{8,10},{9,15},{10,... | collective-permute-start | bytes 1572872 | tf_op jit(solution)/shard_map/ppermute | solution.py:29
  37.9 7.7 %collective-permute-start.12 = (f32[2,2,64,256]{3,2,1,0:T(8,128)S(1)}, f32[2,2,64,256]{3,2,1,0:T(8,128)S(1)}, u32[]{:S(2)}, u32[]{:S(2)}) collective-permute-start(f32[2,2,64,256]{3,2,1,0:T(8,128)S(1)} %pad_maximum_fusion.5), channel_id=1, source_target_pairs={{0,8},{1,57},{2,10},{3,59},{4,12},{5,61},{6,14},{7,63},{8,16},{9,1... | collective-permute-start | bytes 786440 | tf_op jit(solution)/shard_map/ppermute | solution.py:29
  38.9 7.4 %collective-permute-start.13 = (f32[2,2,64,256]{3,2,1,0:T(8,128)S(1)}, f32[2,2,64,256]{3,2,1,0:T(8,128)S(1)}, u32[]{:S(2)}, u32[]{:S(2)}) collective-permute-start(f32[2,2,64,256]{3,2,1,0:T(8,128)S(1)} %broadcast_select_fusion), channel_id=1, source_target_pairs={{0,64},{1,65},{2,66},{3,67},{4,68},{5,69},{6,70},{7,71},{8,72},{9,... | collective-permute-start | bytes 786440 | tf_op jit(solution)/shard_map/ppermute | solution.py:29
  39.6 10.8 %collective-permute-start.17 = (f32[4,2,64,256]{3,2,1,0:T(8,128)S(1)}, f32[4,2,64,256]{3,2,1,0:T(8,128)S(1)}, u32[]{:S(2)}, u32[]{:S(2)}) collective-permute-start(f32[4,2,64,256]{3,2,1,0:T(8,128)S(1)} %constant_dynamic-update-slice_fusion.6.even_ref), channel_id=1, source_target_pairs={{0,2},{1,7},{2,4},{3,1},{4,6},{5,3},{6,0},{7,5},{8,10},{9,15},{10,... | collective-permute-start | bytes 1572872 | tf_op jit(solution)/shard_map/ppermute | solution.py:29
  46.3 6.8 %collective-permute-start.18 = (f32[4,2,64,256]{3,2,1,0:T(8,128)S(1)}, f32[4,2,64,256]{3,2,1,0:T(8,128)S(1)}, u32[]{:S(2)}, u32[]{:S(2)}) collective-permute-start(f32[4,2,64,256]{3,2,1,0:T(8,128)S(1)} %pad_maximum_fusion.mine), channel_id=1, source_target_pairs={{0,1},{1,0},{2,3},{3,2},{4,5},{5,4},{6,7},{7,6},{8,9},{9,8},{10,11... | collective-permute-start | bytes 1572872 | tf_op jit(solution)/shard_map/ppermute | solution.py:29
  46.4 7.7 %collective-permute-start.16 = (f32[2,2,64,256]{3,2,1,0:T(8,128)S(1)}, f32[2,2,64,256]{3,2,1,0:T(8,128)S(1)}, u32[]{:S(2)}, u32[]{:S(2)}) collective-permute-start(f32[2,2,64,256]{3,2,1,0:T(8,128)S(1)} %collective-permute-done.12.even), channel_id=1, source_target_pairs={{0,2},{1,7},{2,4},{3,1},{4,6},{5,3},{6,0},{7,5},{8,10},{9,15},{10,... | collective-permute-start | bytes 786440 | tf_op jit(solution)/shard_map/ppermute | solution.py:29
  66.7 6.3 %collective-permute-start.25 = (f32[2,24,256]{2,1,0:T(8,128)S(1)}, f32[2,24,256]{2,1,0:T(8,128)S(1)}, u32[]{:S(2)}, u32[]{:S(2)}) collective-permute-start(f32[2,24,256]{2,1,0:T(8,128)S(1)} %get-tuple-element.81), channel_id=1, source_target_pairs={{0,192},{1,65},{2,194},{3,67},{4,196},{5,69},{6,198},{7,71},{8,200... | collective-permute-start | bytes 147464 | tf_op jit(solution)/shard_map/ppermute | solution.py:29
  80.1 6.5 %collective-permute-start.20 = (f32[2,64,512]{2,1,0:T(8,128)S(1)}, f32[2,64,512]{2,1,0:T(8,128)S(1)}, u32[]{:S(2)}, u32[]{:S(2)}) collective-permute-start(f32[2,64,512]{2,1,0:T(8,128)S(1)} %slice.81), channel_id=1, source_target_pairs={{0,64},{1,193},{2,66},{3,195},{4,68},{5,197},{6,70},{7,199},{8,72}... | collective-permute-start | bytes 786440 | tf_op jit(solution)/shard_map/ppermute | solution.py:29
  86.6 8.4 %collective-permute-start.32 = (f32[2,24,256]{2,1,0:T(8,128)S(1)}, f32[2,24,256]{2,1,0:T(8,128)S(1)}, u32[]{:S(2)}, u32[]{:S(2)}) collective-permute-start(f32[2,24,256]{2,1,0:T(8,128)S(1)} %add_add_fusion.1), channel_id=1, source_target_pairs={{0,32},{1,33},{2,34},{3,35},{4,36},{5,37},{6,38},{7,39},{8,40},{9,... | collective-permute-start | bytes 147464 | tf_op jit(solution)/shard_map/ppermute | solution.py:29
  93.2 6.3 %collective-permute-start.21 = (f32[64,512]{1,0:T(8,128)S(1)}, f32[64,512]{1,0:T(8,128)S(1)}, u32[]{:S(2)}, u32[]{:S(2)}) collective-permute-start(f32[64,512]{1,0:T(8,128)S(1)} %get-tuple-element.77), channel_id=1, source_target_pairs={{0,192},{1,65},{2,194},{3,67},{4,196},{5,69},{6,198},{7,71},{8,200... | collective-permute-start | bytes 393224 | tf_op jit(solution)/shard_map/ppermute | solution.py:29
  101.3 8.2 %collective-permute-start.36 = (f32[2,24,256]{2,1,0:T(8,128)S(1)}, f32[2,24,256]{2,1,0:T(8,128)S(1)}, u32[]{:S(2)}, u32[]{:S(2)}) collective-permute-start(f32[2,24,256]{2,1,0:T(8,128)S(1)} %add_add_fusion), channel_id=1, source_target_pairs={{0,194},{1,71},{2,192},{3,69},{4,198},{5,67},{6,196},{7,65},{8,202... | collective-permute-start | bytes 147464 | tf_op jit(solution)/shard_map/ppermute | solution.py:29
  102.7 6.8 %collective-permute-start.35 = (f32[2,24,256]{2,1,0:T(8,128)S(1)}, f32[2,24,256]{2,1,0:T(8,128)S(1)}, u32[]{:S(2)}, u32[]{:S(2)}) collective-permute-start(f32[2,24,256]{2,1,0:T(8,128)S(1)} %add_add_fusion), channel_id=1, source_target_pairs={{0,192},{1,65},{2,194},{3,67},{4,196},{5,69},{6,198},{7,71},{8,200... | collective-permute-start | bytes 147464 | tf_op jit(solution)/shard_map/ppermute | solution.py:29
  109.6 9.3 %collective-permute-start.24 = (f32[2,64,256]{2,1,0:T(8,128)S(1)}, f32[2,64,256]{2,1,0:T(8,128)S(1)}, u32[]{:S(2)}, u32[]{:S(2)}) collective-permute-start(f32[2,64,256]{2,1,0:T(8,128)S(1)} %pad_maximum_fusion.7), channel_id=1, source_target_pairs={{0,0},{1,1},{2,128},{3,129},{4,4},{5,5},{6,132},{7,133},{8,8},{9,9... | collective-permute-start | bytes 393224 | tf_op jit(solution)/shard_map/ppermute | solution.py:29
  (18 other events, 87.7 us)

commit v5 on v4

--- a/solution.py
+++ b/solution.py
@@ -498,17 +498,18 @@
     a, b, c = to_second_x(part[1, 0]), to_first_y(part[0, 1]), to_both(part[1, 1])
     z_terms, zt_terms, base = constants(x1, x0, after(link, part))
     part = (part[0, 0] + after(a, base)) + (b + c)
-    a, b, c = swap(part, "y", 1), to_pair(part, 1), to_pair_y(part)
-    q = q[:2] + swap(q[2:], "x", 0)
-    part = after((part + a) + (b + c), q)
-    a, b, c = (to_pair(part, far) for far in (2, 4, 6))
-    came = swap(q[1], "x", 1)
-    part = after((part + a) + (b + c), came)
-    s1, s0 = rows(q[0], came, z_terms)
-    a, b, c = to_second_x(part), to_first_y(part), to_both(part)
-    part = jnp.stack([jnp.stack([part, after(b, s1, s0)]), jnp.stack([a, c])])
+    got = swap(q[2:], "x", 0)
+    a, b, c = swap(part, "y", 1), to_pair(part, 1), to_pair_y(after(part, got))
+    q = q[:2] + got
+    part = (part + a) + (b + c)
+    got = swap(q[1], "x", 1)
+    a, b, c = to_pair(part, 2), to_pair(part, 4), to_pair(after(part, got), 6)
+    part = (part + a) + (b + c)
+    s1, s0 = rows(q[0], got, z_terms)
     sigmas = send(jnp.stack([s1, s0]), lambda x, y, z, s: (y % 2 * 2 + x % 2, y // 2 * 2 + x // 2, z, s))
-    mine = after(jnp.concatenate([part, swap(part, "x", 0)], axis=0), sigmas)
+    a, b, c = to_second_x(part), to_first_y(part), to_both(after(part, sigmas))
+    part = jnp.stack([jnp.stack([part, b]), jnp.stack([a, c])])
+    mine = jnp.concatenate([part, swap(part, "x", 0)], axis=0)
     s11, s10, s00 = finish(place, mine, to_core(mine), z_terms, zt_terms, base)
     return sigmas[0], s11, sigmas[1], s10, s00
 

time: 125 us -> 120 us (0.960)
  waiting for transfers between devices: 40.2 us -> 30.5 us
  starting transfers between devices: 51.2 us -> 54.9 us
    ppermute x39, waiting for transfers between devices: 40.2 us -> 30.5 us  [send(): return lax.ppermute(block, AXES, pairs)]
    ppermute x39, starting transfers between devices: 51.2 us -> 54.9 us  [send(): return lax.ppermute(block, AXES, pairs)]
  transfers between devices with their start and end apart: 39 -> 39, of which waited for: 23 -> 17; matrix products, arithmetic and copies ran while one was open for 4% -> 4% of each run, Pallas kernels for 15% -> 16%
where the time goes in v5:
time: 120 us; the launch traced here: 118 us
  starting transfers between devices  54.9 us (46%)
  waiting for transfers between devices  30.5 us (25%)
  Pallas kernels  25.7 us (21%)
  local copies, waits for them, and re-layouts  4.25 us (4%)
  other arithmetic  1.35 us (1%)
    ppermute x39, starting transfers between devices, send(): return lax.ppermute(block, AXES, pairs)  54.9 us
    ppermute x39, waiting for transfers between devices, send(): return lax.ppermute(block, AXES, pairs)  30.5 us
    pallas_call x4, Pallas kernels, multiply(): pl.pallas_call(kernel, in_specs=[SMEM, VMEM, HBM] + [VMEM] * (2 + len(tot...  10.3 us
    pallas_call x1, Pallas kernels, invert(): pl.pallas_call(invert_kernel, in_specs=[SMEM, HBM, HBM], out_specs=[VMEM,...  3.94 us
    pallas_call x1, Pallas kernels, last(): pl.pallas_call(last_kernel, in_specs=[SMEM, VMEM, HBM] + [VMEM] * 4, out_...  3.55 us
    pallas_call x1, Pallas kernels, finish(): pl.pallas_call(finish_kernel, in_specs=[SMEM] + [VMEM] * 5, out_specs=[VM...  3.14 us
  transfers between devices with their start and end apart: 39, of which 17 were waited for; matrix products, arithmetic and copies ran while one was open for 4% of the time, Pallas kernels for 16%

profile of v5, /device:TPU:8, one launch (start us, length us, event | category | flops | bytes accessed | tf_op | source)
XLA Modules:
  0.0 117.8 jit_solution(7657397720889865604)
XLA Ops:
  1.6 2.4 %collective-permute-start.1 = (f32[1,2,64,256]{3,2,1,0:T(8,128)S(1)}, f32[1,2,64,256]{3,2,1,0:T(8,128)S(1)}, u32[]{:S(2)}, u32[]{:S(2)}) collective-permute-start(f32[1,2,64,256]{3,2,1,0:T(8,128)S(1)} %maximum_bitcast_fusion), channel_id=1, source_target_pairs={{0,4},{1,5},{2,6},{3,7},{4,0},{5,1},{6,2},{7,3},{8,12},{9,13},{10,... | collective-permute-start | bytes 393224 | tf_op jit(solution)/shard_map/ppermute | solution.py:29
  4.0 2.0 %collective-permute-start.3 = (f32[2,2,64,256]{3,2,1,0:T(8,128)S(1)}, f32[2,2,64,256]{3,2,1,0:T(8,128)S(1)}, u32[]{:S(2)}, u32[]{:S(2)}) collective-permute-start(f32[2,2,64,256]{3,2,1,0:T(8,128)S(1)} %pad_maximum_fusion.4), channel_id=1, source_target_pairs={{0,8},{1,57},{2,10},{3,59},{4,12},{5,61},{6,14},{7,63},{8,16},{9,1... | collective-permute-start | bytes 786440 | tf_op jit(solution)/shard_map/ppermute | solution.py:29
  6.1 2.3 %stage.1.own_ref.own = f32[5,4,2,64,256]{4,3,2,1,0:T(8,128)S(1)} custom-call(s32[9]{0:T(128)S(1)} %stack.84.at._, f32[8,4,2,64,256]{4,3,2,1,0:T(8,128)} %bitcast.12.ref), custom_call_target="tpu_custom_call" | custom-call | bytes 5242880 | tf_op jit(solution)/shard_map/stage/pallas_call | solution.py:146
  9.0 3.2 %collective-permute-start.2 = (f32[1,2,64,256]{3,2,1,0:T(8,128)S(1)}, f32[1,2,64,256]{3,2,1,0:T(8,128)S(1)}, u32[]{:S(2)}, u32[]{:S(2)}) collective-permute-start(f32[1,2,64,256]{3,2,1,0:T(8,128)S(1)} %collective-permute-done.1), channel_id=1, source_target_pairs={{0,1},{1,0},{2,3},{3,2},{4,5},{5,4},{6,7},{7,6},{8,9},{9,8},{10,11... | collective-permute-start | bytes 393224 | tf_op jit(solution)/shard_map/ppermute | solution.py:29
  16.7 5.5 %collective-permute-done.6 = f32[2,2,64,256]{3,2,1,0:T(8,128)} collective-permute-done((f32[2,2,64,256]{3,2,1,0:T(8,128)}, f32[2,2,64,256]{3,2,1,0:T(8,128)}, u32[]{:S(2)}, u32[]{:S(2)}) %collective-permute-start.6) | collective-permute-done | bytes 262176 | tf_op jit(solution)/shard_map/ppermute | solution.py:29
  22.2 2.8 %collective-permute-done.5 = f32[2,2,64,256]{3,2,1,0:T(8,128)} collective-permute-done((f32[2,2,64,256]{3,2,1,0:T(8,128)S(1)}, f32[2,2,64,256]{3,2,1,0:T(8,128)}, u32[]{:S(2)}, u32[]{:S(2)}) %collective-permute-start.5) | collective-permute-done | bytes 262176 | tf_op jit(solution)/shard_map/ppermute | solution.py:29
  25.1 3.1 %collective-permute-start.11 = (f32[2,2,64,256]{3,2,1,0:T(8,128)S(1)}, f32[2,2,64,256]{3,2,1,0:T(8,128)S(1)}, u32[]{:S(2)}, u32[]{:S(2)}) collective-permute-start(f32[2,2,64,256]{3,2,1,0:T(8,128)S(1)} %pad_maximum_fusion.2), channel_id=1, source_target_pairs={{0,128},{1,129},{2,130},{3,131},{4,132},{5,133},{6,134},{7,135},{8... | collective-permute-start | bytes 786440 | tf_op jit(solution)/shard_map/ppermute | solution.py:29
  30.3 2.0 %collective-permute-start.10 = (f32[2,2,64,256]{3,2,1,0:T(8,128)S(1)}, f32[2,2,64,256]{3,2,1,0:T(8,128)S(1)}, u32[]{:S(2)}, u32[]{:S(2)}) collective-permute-start(f32[2,2,64,256]{3,2,1,0:T(8,128)S(1)} %collective-permute-done.9), channel_id=1, source_target_pairs={{0,8},{1,57},{2,10},{3,59},{4,12},{5,61},{6,14},{7,63},{8,16},{9,1... | collective-permute-start | bytes 786440 | tf_op jit(solution)/shard_map/ppermute | solution.py:29
  34.7 2.2 %multiply.4.refs_0_ = f32[2,256,512]{2,1,0:T(8,128)S(1)} custom-call(s32[9]{0:T(128)S(1)} %stack.84.at._, f32[5,4,2,64,256]{4,3,2,1,0:T(8,128)S(1)} %stage.1.own_ref.own, f32[8,4,2,64,256]{4,3,2,1,0:T(8,128)} %bitcast.13.other_ref.other, f32[2,2,64,256]{3,2,1,0:T(8,128)S(1)} %pad_maximum_fusion.3.even_ref, f32[2,2,64,256]{3,2,1,0:T(8,128)S(1)} %collective-permute-done.7.odd_ref), custom_call_target="tpu_custom_call" | custom-call | flops 805306368 | bytes 2097152 | tf_op jit(solution)/shard_map/multiply/pallas_call | solution.py:201
  41.2 2.7 %multiply.5.refs_0_ = f32[2,256,512]{2,1,0:T(8,128)S(1)} custom-call(s32[9]{0:T(128)S(1)} %stack.84.at._, f32[5,4,2,64,256]{4,3,2,1,0:T(8,128)S(1)} %stage.1.own_ref.own, f32[8,4,2,64,256]{4,3,2,1,0:T(8,128)} %bitcast.13.other_ref.other, f32[4,2,64,256]{3,2,1,0:T(8,128)S(1)} %constant_dynamic-update-slice_fusion.4.even_ref, ...), custom_call_target="tpu_custom_call", output_to_operand_aliasing={{}: (5, {})} | custom-call | flops 805306368 | bytes 2097152 | tf_op jit(solution)/shard_map/multiply/pallas_call | solution.py:201
  47.7 2.7 %multiply.6.refs_0_ = f32[2,256,512]{2,1,0:T(8,128)S(1)} custom-call(s32[9]{0:T(128)S(1)} %stack.84.at._, f32[5,4,2,64,256]{4,3,2,1,0:T(8,128)S(1)} %stage.1.own_ref.own, f32[8,4,2,64,256]{4,3,2,1,0:T(8,128)} %bitcast.13.other_ref.other, f32[4,2,64,256]{3,2,1,0:T(8,128)S(1)} %constant_dynamic-update-slice_fusion.2.even_ref, ...), custom_call_target="tpu_custom_call", output_to_operand_aliasing={{}: (5, {})} | custom-call | flops 805306368 | bytes 2097152 | tf_op jit(solution)/shard_map/multiply/pallas_call | solution.py:201
  50.4 2.7 %multiply.7.total = f32[2,256,512]{2,1,0:T(8,128)S(1)} custom-call(s32[9]{0:T(128)S(1)} %stack.84.at._, f32[5,4,2,64,256]{4,3,2,1,0:T(8,128)S(1)} %stage.1.own_ref.own, f32[8,4,2,64,256]{4,3,2,1,0:T(8,128)} %bitcast.13.other_ref.other, f32[4,2,64,256]{3,2,1,0:T(8,128)S(1)} %constant_dynamic-update-slice_fusion.6.even_ref, ...), custom_call_target="tpu_custom_call", output_to_operand_aliasing={{}: (5, {})} | custom-call | flops 805306368 | bytes 2097152 | tf_op jit(solution)/shard_map/multiply/pallas_call | solution.py:201
  54.0 3.5 %last.1 = (f32[2,4,4,24,256]{4,3,2,1,0:T(8,128)S(1)}, f32[2,4,64,512]{3,2,1,0:T(8,128)S(1)}) custom-call(s32[9]{0:T(128)S(1)} %stack.84.at._, f32[5,4,2,64,256]{4,3,2,1,0:T(8,128)S(1)} %stage.1.own_ref.own, f32[8,4,2,64,256]{4,3,2,1,0:T(8,128)} %bitcast.13.other_ref.other, f32[2,2,64,256]{3,2,1,0:T(8,128)S(1)} %collective-permute-done.12.even, ...), custom_call_target="tpu_custom_call" | custom-call | flops 1073741824 | bytes 2097152 | tf_op jit(solution)/shard_map/last/pallas_call | solution.py:244
  61.5 3.9 %invert.1 = (f32[256,256]{1,0:T(8,128)S(1)}, f32[256,256]{1,0:T(8,128)S(1)}) custom-call(s32[9]{0:T(128)S(1)} %stack.84.at._, f32[256,256]{1,0:T(8,128)S(1)} %copy-done, f32[256,256]{1,0:T(8,128)S(1)} %copy-done.1), custom_call_target="tpu_custom_call" | custom-call | flops 4294967296 | bytes 1048576 | tf_op jit(solution)/shard_map/invert/pallas_call | solution.py:303
  67.4 2.0 %collective-permute-start.25 = (f32[2,24,256]{2,1,0:T(8,128)S(1)}, f32[2,24,256]{2,1,0:T(8,128)S(1)}, u32[]{:S(2)}, u32[]{:S(2)}) collective-permute-start(f32[2,24,256]{2,1,0:T(8,128)S(1)} %get-tuple-element.79), channel_id=1, source_target_pairs={{0,192},{1,65},{2,194},{3,67},{4,196},{5,69},{6,198},{7,71},{8,200... | collective-permute-start | bytes 147464 | tf_op jit(solution)/shard_map/ppermute | solution.py:29
  73.5 3.6 %collective-permute-done.27 = f32[2,24,256]{2,1,0:T(8,128)S(1)} collective-permute-done((f32[2,24,256]{2,1,0:T(8,128)S(1)}, f32[2,24,256]{2,1,0:T(8,128)S(1)}, u32[]{:S(2)}, u32[]{:S(2)}) %collective-permute-start.27) | collective-permute-done | bytes 49184 | tf_op jit(solution)/shard_map/ppermute | solution.py:29
  83.8 3.0 %collective-permute-start.32 = (f32[2,24,256]{2,1,0:T(8,128)S(1)}, f32[2,24,256]{2,1,0:T(8,128)S(1)}, u32[]{:S(2)}, u32[]{:S(2)}) collective-permute-start(f32[2,24,256]{2,1,0:T(8,128)S(1)} %add_add_fusion.1), channel_id=1, source_target_pairs={{0,32},{1,33},{2,34},{3,35},{4,36},{5,37},{6,38},{7,39},{8,40},{9,... | collective-permute-start | bytes 147464 | tf_op jit(solution)/shard_map/ppermute | solution.py:29
  88.1 2.2 %collective-permute-start.33 = (f32[2,24,256]{2,1,0:T(8,128)S(1)}, f32[2,24,256]{2,1,0:T(8,128)S(1)}, u32[]{:S(2)}, u32[]{:S(2)}) collective-permute-start(f32[2,24,256]{2,1,0:T(8,128)S(1)} %add_add_fusion.1), channel_id=1, source_target_pairs={{0,48},{1,17},{2,50},{3,19},{4,52},{5,21},{6,54},{7,23},{8,56},{9,... | collective-permute-start | bytes 147464 | tf_op jit(solution)/shard_map/ppermute | solution.py:29
  90.8 3.9 %collective-permute-start.24 = (f32[2,64,256]{2,1,0:T(8,128)S(1)}, f32[2,64,256]{2,1,0:T(8,128)S(1)}, u32[]{:S(2)}, u32[]{:S(2)}) collective-permute-start(f32[2,64,256]{2,1,0:T(8,128)S(1)} %pad_maximum_fusion.7), channel_id=1, source_target_pairs={{0,0},{1,1},{2,128},{3,129},{4,4},{5,5},{6,132},{7,133},{8,8},{9,9... | collective-permute-start | bytes 393224 | tf_op jit(solution)/shard_map/ppermute | solution.py:29
  94.8 1.9 %collective-permute-start.34 = (f32[2,24,256]{2,1,0:T(8,128)S(1)}, f32[2,24,256]{2,1,0:T(8,128)S(1)}, u32[]{:S(2)}, u32[]{:S(2)}) collective-permute-start(f32[2,24,256]{2,1,0:T(8,128)S(1)} %add_add_fusion), channel_id=1, source_target_pairs={{0,2},{1,7},{2,0},{3,5},{4,6},{5,3},{6,4},{7,1},{8,10},{9,15},{10,... | collective-permute-start | bytes 147464 | tf_op jit(solution)/shard_map/ppermute | solution.py:29
  100.4 3.8 %collective-permute-start.36 = (f32[2,24,256]{2,1,0:T(8,128)S(1)}, f32[2,24,256]{2,1,0:T(8,128)S(1)}, u32[]{:S(2)}, u32[]{:S(2)}) collective-permute-start(f32[2,24,256]{2,1,0:T(8,128)S(1)} %add_add_fusion), channel_id=1, source_target_pairs={{0,194},{1,71},{2,192},{3,69},{4,198},{5,67},{6,196},{7,65},{8,202... | collective-permute-start | bytes 147464 | tf_op jit(solution)/shard_map/ppermute | solution.py:29
  104.1 2.8 %collective-permute-done.36 = f32[2,24,256]{2,1,0:T(8,128)S(1)} collective-permute-done((f32[2,24,256]{2,1,0:T(8,128)S(1)}, f32[2,24,256]{2,1,0:T(8,128)S(1)}, u32[]{:S(2)}, u32[]{:S(2)}) %collective-permute-start.36) | collective-permute-done | bytes 49184 | tf_op jit(solution)/shard_map/ppermute | solution.py:29
  107.1 5.7 %collective-permute-done.37 = f32[2,2,2,24,256]{4,3,2,1,0:T(8,128)S(1)} collective-permute-done((f32[2,2,2,24,256]{4,3,2,1,0:T(8,128)S(1)}, f32[2,2,2,24,256]{4,3,2,1,0:T(8,128)S(1)}, u32[]{:S(2)}, u32[]{:S(2)}) %collective-permute-start.37) | collective-permute-done | bytes 196640 | tf_op jit(solution)/shard_map/ppermute | solution.py:29
  114.6 3.1 %finish.1 = (f32[256,256]{1,0:T(8,128)}, f32[256,256]{1,0:T(8,128)}, f32[256,256]{1,0:T(8,128)}) custom-call(s32[9]{0:T(128)S(1)} %stack.84.at._, f32[4,2,2,24,256]{4,3,2,1,0:T(8,128)S(1)} %pad_maximum_fusion.1.mine, f32[4,2,2,24,256]{4,3,2,1,0:T(8,128)S(1)} %collective-permute-done.38.other, bf16[1536,512]{1,0:T(8,128)(2,1)S(1)} %get-tuple-element.63.z_terms, ...), custom_call_target="tpu_custom_call" | custom-call | flops 268435456 | bytes 3145728 | tf_op jit(solution)/shard_map/finish/pallas_call | solution.py:425
  (109 shorter events, 43.6 us)
Async XLA Ops:
  1.6 7.4 %collective-permute-start.1 = (f32[1,2,64,256]{3,2,1,0:T(8,128)S(1)}, f32[1,2,64,256]{3,2,1,0:T(8,128)S(1)}, u32[]{:S(2)}, u32[]{:S(2)}) collective-permute-start(f32[1,2,64,256]{3,2,1,0:T(8,128)S(1)} %maximum_bitcast_fusion), channel_id=1, source_target_pairs={{0,4},{1,5},{2,6},{3,7},{4,0},{5,1},{6,2},{7,3},{8,12},{9,13},{10,... | collective-permute-start | bytes 393224 | tf_op jit(solution)/shard_map/ppermute | solution.py:29
  4.0 10.3 %collective-permute-start.3 = (f32[2,2,64,256]{3,2,1,0:T(8,128)S(1)}, f32[2,2,64,256]{3,2,1,0:T(8,128)S(1)}, u32[]{:S(2)}, u32[]{:S(2)}) collective-permute-start(f32[2,2,64,256]{3,2,1,0:T(8,128)S(1)} %pad_maximum_fusion.4), channel_id=1, source_target_pairs={{0,8},{1,57},{2,10},{3,59},{4,12},{5,61},{6,14},{7,63},{8,16},{9,1... | collective-permute-start | bytes 786440 | tf_op jit(solution)/shard_map/ppermute | solution.py:29
  14.3 20.4 %collective-permute-start.4 = (f32[4096,256]{1,0:T(8,128)}, f32[4096,256]{1,0:T(8,128)}, u32[]{:S(2)}, u32[]{:S(2)}) collective-permute-start(f32[4096,256]{1,0:T(8,128)} %param.6), channel_id=1, source_target_pairs={{0,1},{1,0},{2,3},{3,2},{4,5},{5,4},{6,7},{7,6},{8,9},{9,8},{10,11... | collective-permute-start | bytes 12582920 | tf_op jit(solution)/shard_map/ppermute | solution.py:29
  14.3 7.9 %collective-permute-start.6 = (f32[2,2,64,256]{3,2,1,0:T(8,128)}, f32[2,2,64,256]{3,2,1,0:T(8,128)}, u32[]{:S(2)}, u32[]{:S(2)}) collective-permute-start(f32[2,2,64,256]{3,2,1,0:T(8,128)} %constant_dynamic-update-slice_fusion), channel_id=1, source_target_pairs={{0,8},{1,57},{2,10},{3,59},{4,12},{5,61},{6,14},{7,63},{8,16},{9,1... | collective-permute-start | bytes 786440 | tf_op jit(solution)/shard_map/ppermute | solution.py:29
  14.3 7.9 %collective-permute-start.7 = (f32[2,2,64,256]{3,2,1,0:T(8,128)S(1)}, f32[2,2,64,256]{3,2,1,0:T(8,128)S(1)}, u32[]{:S(2)}, u32[]{:S(2)}) collective-permute-start(f32[2,2,64,256]{3,2,1,0:T(8,128)S(1)} %pad_maximum_fusion.3.even_ref), channel_id=1, source_target_pairs={{0,2},{1,7},{2,4},{3,1},{4,6},{5,3},{6,0},{7,5},{8,10},{9,15},{10,... | collective-permute-start | bytes 786440 | tf_op jit(solution)/shard_map/ppermute | solution.py:29
  14.9 10.1 %collective-permute-start.5 = (f32[2,2,64,256]{3,2,1,0:T(8,128)S(1)}, f32[2,2,64,256]{3,2,1,0:T(8,128)}, u32[]{:S(2)}, u32[]{:S(2)}) collective-permute-start(f32[2,2,64,256]{3,2,1,0:T(8,128)S(1)} %collective-permute-done.3), channel_id=1, source_target_pairs={{0,8},{1,57},{2,10},{3,59},{4,12},{5,61},{6,14},{7,63},{8,16},{9,1... | collective-permute-start | bytes 786440 | tf_op jit(solution)/shard_map/ppermute | solution.py:29
  22.2 8.1 %collective-permute-start.9 = (f32[2,2,64,256]{3,2,1,0:T(8,128)}, f32[2,2,64,256]{3,2,1,0:T(8,128)S(1)}, u32[]{:S(2)}, u32[]{:S(2)}) collective-permute-start(f32[2,2,64,256]{3,2,1,0:T(8,128)} %collective-permute-done.6), channel_id=1, source_target_pairs={{0,8},{1,57},{2,10},{3,59},{4,12},{5,61},{6,14},{7,63},{8,16},{9,1... | collective-permute-start | bytes 786440 | tf_op jit(solution)/shard_map/ppermute | solution.py:29
  25.0 8.3 %collective-permute-start.8 = (f32[2,2,64,256]{3,2,1,0:T(8,128)}, f32[2,2,64,256]{3,2,1,0:T(8,128)S(1)}, u32[]{:S(2)}, u32[]{:S(2)}) collective-permute-start(f32[2,2,64,256]{3,2,1,0:T(8,128)} %collective-permute-done.5), channel_id=1, source_target_pairs={{0,8},{1,57},{2,10},{3,59},{4,12},{5,61},{6,14},{7,63},{8,16},{9,1... | collective-permute-start | bytes 786440 | tf_op jit(solution)/shard_map/ppermute | solution.py:29
  25.1 11.9 %collective-permute-start.11 = (f32[2,2,64,256]{3,2,1,0:T(8,128)S(1)}, f32[2,2,64,256]{3,2,1,0:T(8,128)S(1)}, u32[]{:S(2)}, u32[]{:S(2)}) collective-permute-start(f32[2,2,64,256]{3,2,1,0:T(8,128)S(1)} %pad_maximum_fusion.2), channel_id=1, source_target_pairs={{0,128},{1,129},{2,130},{3,131},{4,132},{5,133},{6,134},{7,135},{8... | collective-permute-start | bytes 786440 | tf_op jit(solution)/shard_map/ppermute | solution.py:29
  29.2 12.0 %collective-permute-start.15 = (f32[4,2,64,256]{3,2,1,0:T(8,128)S(1)}, f32[4,2,64,256]{3,2,1,0:T(8,128)S(1)}, u32[]{:S(2)}, u32[]{:S(2)}) collective-permute-start(f32[4,2,64,256]{3,2,1,0:T(8,128)S(1)} %constant_dynamic-update-slice_fusion.4.even_ref), channel_id=1, source_target_pairs={{0,2},{1,7},{2,4},{3,1},{4,6},{5,3},{6,0},{7,5},{8,10},{9,15},{10,... | collective-permute-start | bytes 1572872 | tf_op jit(solution)/shard_map/ppermute | solution.py:29
  30.3 7.6 %collective-permute-start.10 = (f32[2,2,64,256]{3,2,1,0:T(8,128)S(1)}, f32[2,2,64,256]{3,2,1,0:T(8,128)S(1)}, u32[]{:S(2)}, u32[]{:S(2)}) collective-permute-start(f32[2,2,64,256]{3,2,1,0:T(8,128)S(1)} %collective-permute-done.9), channel_id=1, source_target_pairs={{0,8},{1,57},{2,10},{3,59},{4,12},{5,61},{6,14},{7,63},{8,16},{9,1... | collective-permute-start | bytes 786440 | tf_op jit(solution)/shard_map/ppermute | solution.py:29
  33.4 10.7 %collective-permute-start.14 = (f32[4,2,64,256]{3,2,1,0:T(8,128)S(1)}, f32[4,2,64,256]{3,2,1,0:T(8,128)S(1)}, u32[]{:S(2)}, u32[]{:S(2)}) collective-permute-start(f32[4,2,64,256]{3,2,1,0:T(8,128)S(1)} %constant_dynamic-update-slice_fusion.2.even_ref), channel_id=1, source_target_pairs={{0,2},{1,7},{2,4},{3,1},{4,6},{5,3},{6,0},{7,5},{8,10},{9,15},{10,... | collective-permute-start | bytes 1572872 | tf_op jit(solution)/shard_map/ppermute | solution.py:29
  37.9 7.7 %collective-permute-start.12 = (f32[2,2,64,256]{3,2,1,0:T(8,128)S(1)}, f32[2,2,64,256]{3,2,1,0:T(8,128)S(1)}, u32[]{:S(2)}, u32[]{:S(2)}) collective-permute-start(f32[2,2,64,256]{3,2,1,0:T(8,128)S(1)} %pad_maximum_fusion.5), channel_id=1, source_target_pairs={{0,8},{1,57},{2,10},{3,59},{4,12},{5,61},{6,14},{7,63},{8,16},{9,1... | collective-permute-start | bytes 786440 | tf_op jit(solution)/shard_map/ppermute | solution.py:29
  38.9 7.4 %collective-permute-start.13 = (f32[2,2,64,256]{3,2,1,0:T(8,128)S(1)}, f32[2,2,64,256]{3,2,1,0:T(8,128)S(1)}, u32[]{:S(2)}, u32[]{:S(2)}) collective-permute-start(f32[2,2,64,256]{3,2,1,0:T(8,128)S(1)} %broadcast_select_fusion), channel_id=1, source_target_pairs={{0,64},{1,65},{2,66},{3,67},{4,68},{5,69},{6,70},{7,71},{8,72},{9,... | collective-permute-start | bytes 786440 | tf_op jit(solution)/shard_map/ppermute | solution.py:29
  39.6 10.8 %collective-permute-start.17 = (f32[4,2,64,256]{3,2,1,0:T(8,128)S(1)}, f32[4,2,64,256]{3,2,1,0:T(8,128)S(1)}, u32[]{:S(2)}, u32[]{:S(2)}) collective-permute-start(f32[4,2,64,256]{3,2,1,0:T(8,128)S(1)} %constant_dynamic-update-slice_fusion.6.even_ref), channel_id=1, source_target_pairs={{0,2},{1,7},{2,4},{3,1},{4,6},{5,3},{6,0},{7,5},{8,10},{9,15},{10,... | collective-permute-start | bytes 1572872 | tf_op jit(solution)/shard_map/ppermute | solution.py:29
  46.3 6.8 %collective-permute-start.18 = (f32[4,2,64,256]{3,2,1,0:T(8,128)S(1)}, f32[4,2,64,256]{3,2,1,0:T(8,128)S(1)}, u32[]{:S(2)}, u32[]{:S(2)}) collective-permute-start(f32[4,2,64,256]{3,2,1,0:T(8,128)S(1)} %pad_maximum_fusion.mine), channel_id=1, source_target_pairs={{0,1},{1,0},{2,3},{3,2},{4,5},{5,4},{6,7},{7,6},{8,9},{9,8},{10,11... | collective-permute-start | bytes 1572872 | tf_op jit(solution)/shard_map/ppermute | solution.py:29
  46.4 7.7 %collective-permute-start.16 = (f32[2,2,64,256]{3,2,1,0:T(8,128)S(1)}, f32[2,2,64,256]{3,2,1,0:T(8,128)S(1)}, u32[]{:S(2)}, u32[]{:S(2)}) collective-permute-start(f32[2,2,64,256]{3,2,1,0:T(8,128)S(1)} %collective-permute-done.12.even), channel_id=1, source_target_pairs={{0,2},{1,7},{2,4},{3,1},{4,6},{5,3},{6,0},{7,5},{8,10},{9,15},{10,... | collective-permute-start | bytes 786440 | tf_op jit(solution)/shard_map/ppermute | solution.py:29
  65.6 13.2 %collective-permute-start.20 = (f32[2,64,512]{2,1,0:T(8,128)S(1)}, f32[2,64,512]{2,1,0:T(8,128)S(1)}, u32[]{:S(2)}, u32[]{:S(2)}) collective-permute-start(f32[2,64,512]{2,1,0:T(8,128)S(1)} %slice.81), channel_id=1, source_target_pairs={{0,64},{1,193},{2,66},{3,195},{4,68},{5,197},{6,70},{7,199},{8,72}... | collective-permute-start | bytes 786440 | tf_op jit(solution)/shard_map/ppermute | solution.py:29
  80.7 7.4 %collective-permute-start.21 = (f32[64,512]{1,0:T(8,128)S(1)}, f32[64,512]{1,0:T(8,128)S(1)}, u32[]{:S(2)}, u32[]{:S(2)}) collective-permute-start(f32[64,512]{1,0:T(8,128)S(1)} %get-tuple-element.75), channel_id=1, source_target_pairs={{0,192},{1,65},{2,194},{3,67},{4,196},{5,69},{6,198},{7,71},{8,200... | collective-permute-start | bytes 393224 | tf_op jit(solution)/shard_map/ppermute | solution.py:29
  83.8 10.9 %collective-permute-start.32 = (f32[2,24,256]{2,1,0:T(8,128)S(1)}, f32[2,24,256]{2,1,0:T(8,128)S(1)}, u32[]{:S(2)}, u32[]{:S(2)}) collective-permute-start(f32[2,24,256]{2,1,0:T(8,128)S(1)} %add_add_fusion.1), channel_id=1, source_target_pairs={{0,32},{1,33},{2,34},{3,35},{4,36},{5,37},{6,38},{7,39},{8,40},{9,... | collective-permute-start | bytes 147464 | tf_op jit(solution)/shard_map/ppermute | solution.py:29
  86.8 7.9 %collective-permute-start.31 = (f32[2,24,256]{2,1,0:T(8,128)S(1)}, f32[2,24,256]{2,1,0:T(8,128)S(1)}, u32[]{:S(2)}, u32[]{:S(2)}) collective-permute-start(f32[2,24,256]{2,1,0:T(8,128)S(1)} %add_add_fusion.1), channel_id=1, source_target_pairs={{0,16},{1,49},{2,18},{3,51},{4,20},{5,53},{6,22},{7,55},{8,24},{9,... | collective-permute-start | bytes 147464 | tf_op jit(solution)/shard_map/ppermute | solution.py:29
  90.8 9.6 %collective-permute-start.24 = (f32[2,64,256]{2,1,0:T(8,128)S(1)}, f32[2,64,256]{2,1,0:T(8,128)S(1)}, u32[]{:S(2)}, u32[]{:S(2)}) collective-permute-start(f32[2,64,256]{2,1,0:T(8,128)S(1)} %pad_maximum_fusion.7), channel_id=1, source_target_pairs={{0,0},{1,1},{2,128},{3,129},{4,4},{5,5},{6,132},{7,133},{8,8},{9,9... | collective-permute-start | bytes 393224 | tf_op jit(solution)/shard_map/ppermute | solution.py:29
  94.8 9.4 %collective-permute-start.34 = (f32[2,24,256]{2,1,0:T(8,128)S(1)}, f32[2,24,256]{2,1,0:T(8,128)S(1)}, u32[]{:S(2)}, u32[]{:S(2)}) collective-permute-start(f32[2,24,256]{2,1,0:T(8,128)S(1)} %add_add_fusion), channel_id=1, source_target_pairs={{0,2},{1,7},{2,0},{3,5},{4,6},{5,3},{6,4},{7,1},{8,10},{9,15},{10,... | collective-permute-start | bytes 147464 | tf_op jit(solution)/shard_map/ppermute | solution.py:29
  96.7 7.5 %collective-permute-start.35 = (f32[2,24,256]{2,1,0:T(8,128)S(1)}, f32[2,24,256]{2,1,0:T(8,128)S(1)}, u32[]{:S(2)}, u32[]{:S(2)}) collective-permute-start(f32[2,24,256]{2,1,0:T(8,128)S(1)} %add_add_fusion), channel_id=1, source_target_pairs={{0,192},{1,65},{2,194},{3,67},{4,196},{5,69},{6,198},{7,71},{8,200... | collective-permute-start | bytes 147464 | tf_op jit(solution)/shard_map/ppermute | solution.py:29
  (18 other events, 88.6 us)

commit v6 on v5

--- a/solution.py
+++ b/solution.py
@@ -116,11 +116,15 @@
     return jnp.dot(left, right, preferred_element_type=F32)
 
 
+def half_product(left, right, columns):
+    return sum(product(left[:B, n : n + B], right[n : n + B, columns]) for n in range(0, WIDE, 2 * B))
+
+
 def exact(left, right):
     return jnp.dot(left, right, precision=lax.Precision.HIGHEST, preferred_element_type=F32)
 
 
-def params(limit=16):
+def params(limit=10):
     return pltpu.CompilerParams(vmem_limit_bytes=limit * 1024 * 1024)
 
 
@@ -149,7 +153,7 @@
         out_specs=VMEM,
         out_shape=jax.ShapeDtypeStruct((5,) + SLAB, F32),
         scratch_shapes=[pltpu.SemaphoreType.DMA((5,))],
-        compiler_params=params(),
+        compiler_params=params(4),
         cost_estimate=cost(0, 5 << 20),
         name="stage",
     )(place, sigma)
@@ -205,7 +209,7 @@
         out_shape=jax.ShapeDtypeStruct((2, B, 2 * B), F32),
         scratch_shapes=slab_scratch(even),
         input_output_aliases={5: 0} if totals else {},
-        compiler_params=params(30),
+        compiler_params=params(12),
         cost_estimate=cost(3 << 28, 2 << 20),
         name="multiply",
     )(place, sigma, other, even, odd, *totals)
@@ -255,7 +259,7 @@
             pltpu.VMEM((WIDE, 2 * B), BF16),
         ]
         + slab_scratch(even),
-        compiler_params=params(30),
+        compiler_params=params(20),
         cost_estimate=cost(1 << 30, 2 << 20),
         name="last",
     )(place, sigma, other, even, odd, total, weights)
@@ -413,8 +417,9 @@
     fill_left(left, 0, B, crossed)
     fill_left(left, B, 0, crossed.T)
     fill_left(left, B, B, whole[2 * B :])
-    fill_right(right, 0, 0, product(left[...], z_terms[...]))
-    top = product(zt_terms[:B], right[...])
+    fill_right(right, 0, 0, half_product(left, z_terms, slice(0, B)))
+    fill_right(right, 0, B, product(left[...], z_terms[:, B:]))
+    top = half_product(zt_terms, right, slice(0, 2 * B))
     s11[...] = top[:, :B] + base[:B]
     s10[...] = top[:, B:] + base[B : 2 * B]
     s00[...] = product(zt_terms[B:], right[:, B:]) + base[2 * B :]

time: 120 us -> 120 us (level)
  no operation moved by 1% of the time
where the time goes in v6:
time: 120 us; the launch traced here: 118 us
  starting transfers between devices  54.9 us (46%)
  waiting for transfers between devices  30.4 us (25%)
  Pallas kernels  25.8 us (22%)
  local copies, waits for them, and re-layouts  4.25 us (4%)
  other arithmetic  1.35 us (1%)
    ppermute x39, starting transfers between devices, send(): return lax.ppermute(block, AXES, pairs)  54.9 us
    ppermute x39, waiting for transfers between devices, send(): return lax.ppermute(block, AXES, pairs)  30.4 us
    pallas_call x4, Pallas kernels, multiply(): pl.pallas_call(kernel, in_specs=[SMEM, VMEM, HBM] + [VMEM] * (2 + len(tot...  10.3 us
    pallas_call x1, Pallas kernels, invert(): pl.pallas_call(invert_kernel, in_specs=[SMEM, HBM, HBM], out_specs=[VMEM,...  3.94 us
    pallas_call x1, Pallas kernels, last(): pl.pallas_call(last_kernel, in_specs=[SMEM, VMEM, HBM] + [VMEM] * 4, out_...  3.55 us
    pallas_call x1, Pallas kernels, finish(): pl.pallas_call(finish_kernel, in_specs=[SMEM] + [VMEM] * 5, out_specs=[VM...  3.23 us
  transfers between devices with their start and end apart: 39, of which 17 were waited for; matrix products, arithmetic and copies ran while one was open for 4% of the time, Pallas kernels for 16%

profile of v6, /device:TPU:8, one launch (start us, length us, event | category | flops | bytes accessed | tf_op | source)
XLA Modules:
  0.0 117.9 jit_solution(14108550844471819066)
XLA Ops:
  1.6 2.4 %collective-permute-start.1 = (f32[1,2,64,256]{3,2,1,0:T(8,128)S(1)}, f32[1,2,64,256]{3,2,1,0:T(8,128)S(1)}, u32[]{:S(2)}, u32[]{:S(2)}) collective-permute-start(f32[1,2,64,256]{3,2,1,0:T(8,128)S(1)} %maximum_bitcast_fusion), channel_id=1, source_target_pairs={{0,4},{1,5},{2,6},{3,7},{4,0},{5,1},{6,2},{7,3},{8,12},{9,13},{10,... | collective-permute-start | bytes 393224 | tf_op jit(solution)/shard_map/ppermute | solution.py:29
  4.0 2.0 %collective-permute-start.3 = (f32[2,2,64,256]{3,2,1,0:T(8,128)S(1)}, f32[2,2,64,256]{3,2,1,0:T(8,128)S(1)}, u32[]{:S(2)}, u32[]{:S(2)}) collective-permute-start(f32[2,2,64,256]{3,2,1,0:T(8,128)S(1)} %pad_maximum_fusion.4), channel_id=1, source_target_pairs={{0,8},{1,57},{2,10},{3,59},{4,12},{5,61},{6,14},{7,63},{8,16},{9,1... | collective-permute-start | bytes 786440 | tf_op jit(solution)/shard_map/ppermute | solution.py:29
  6.1 2.3 %stage.1.own_ref.own = f32[5,4,2,64,256]{4,3,2,1,0:T(8,128)S(1)} custom-call(s32[9]{0:T(128)S(1)} %stack.84.at._, f32[8,4,2,64,256]{4,3,2,1,0:T(8,128)} %bitcast.12.ref), custom_call_target="tpu_custom_call" | custom-call | bytes 5242880 | tf_op jit(solution)/shard_map/stage/pallas_call | solution.py:150
  9.0 3.2 %collective-permute-start.2 = (f32[1,2,64,256]{3,2,1,0:T(8,128)S(1)}, f32[1,2,64,256]{3,2,1,0:T(8,128)S(1)}, u32[]{:S(2)}, u32[]{:S(2)}) collective-permute-start(f32[1,2,64,256]{3,2,1,0:T(8,128)S(1)} %collective-permute-done.1), channel_id=1, source_target_pairs={{0,1},{1,0},{2,3},{3,2},{4,5},{5,4},{6,7},{7,6},{8,9},{9,8},{10,11... | collective-permute-start | bytes 393224 | tf_op jit(solution)/shard_map/ppermute | solution.py:29
  16.7 5.5 %collective-permute-done.6 = f32[2,2,64,256]{3,2,1,0:T(8,128)} collective-permute-done((f32[2,2,64,256]{3,2,1,0:T(8,128)}, f32[2,2,64,256]{3,2,1,0:T(8,128)}, u32[]{:S(2)}, u32[]{:S(2)}) %collective-permute-start.6) | collective-permute-done | bytes 262176 | tf_op jit(solution)/shard_map/ppermute | solution.py:29
  22.2 2.8 %collective-permute-done.5 = f32[2,2,64,256]{3,2,1,0:T(8,128)} collective-permute-done((f32[2,2,64,256]{3,2,1,0:T(8,128)S(1)}, f32[2,2,64,256]{3,2,1,0:T(8,128)}, u32[]{:S(2)}, u32[]{:S(2)}) %collective-permute-start.5) | collective-permute-done | bytes 262176 | tf_op jit(solution)/shard_map/ppermute | solution.py:29
  25.1 3.1 %collective-permute-start.11 = (f32[2,2,64,256]{3,2,1,0:T(8,128)S(1)}, f32[2,2,64,256]{3,2,1,0:T(8,128)S(1)}, u32[]{:S(2)}, u32[]{:S(2)}) collective-permute-start(f32[2,2,64,256]{3,2,1,0:T(8,128)S(1)} %pad_maximum_fusion.2), channel_id=1, source_target_pairs={{0,128},{1,129},{2,130},{3,131},{4,132},{5,133},{6,134},{7,135},{8... | collective-permute-start | bytes 786440 | tf_op jit(solution)/shard_map/ppermute | solution.py:29
  30.3 2.0 %collective-permute-start.10 = (f32[2,2,64,256]{3,2,1,0:T(8,128)S(1)}, f32[2,2,64,256]{3,2,1,0:T(8,128)S(1)}, u32[]{:S(2)}, u32[]{:S(2)}) collective-permute-start(f32[2,2,64,256]{3,2,1,0:T(8,128)S(1)} %collective-permute-done.9), channel_id=1, source_target_pairs={{0,8},{1,57},{2,10},{3,59},{4,12},{5,61},{6,14},{7,63},{8,16},{9,1... | collective-permute-start | bytes 786440 | tf_op jit(solution)/shard_map/ppermute | solution.py:29
  34.7 2.2 %multiply.4.refs_0_ = f32[2,256,512]{2,1,0:T(8,128)S(1)} custom-call(s32[9]{0:T(128)S(1)} %stack.84.at._, f32[5,4,2,64,256]{4,3,2,1,0:T(8,128)S(1)} %stage.1.own_ref.own, f32[8,4,2,64,256]{4,3,2,1,0:T(8,128)} %bitcast.13.other_ref.other, f32[2,2,64,256]{3,2,1,0:T(8,128)S(1)} %pad_maximum_fusion.3.even_ref, f32[2,2,64,256]{3,2,1,0:T(8,128)S(1)} %collective-permute-done.7.odd_ref), custom_call_target="tpu_custom_call" | custom-call | flops 805306368 | bytes 2097152 | tf_op jit(solution)/shard_map/multiply/pallas_call | solution.py:205
  41.2 2.7 %multiply.5.refs_0_ = f32[2,256,512]{2,1,0:T(8,128)S(1)} custom-call(s32[9]{0:T(128)S(1)} %stack.84.at._, f32[5,4,2,64,256]{4,3,2,1,0:T(8,128)S(1)} %stage.1.own_ref.own, f32[8,4,2,64,256]{4,3,2,1,0:T(8,128)} %bitcast.13.other_ref.other, f32[4,2,64,256]{3,2,1,0:T(8,128)S(1)} %constant_dynamic-update-slice_fusion.4.even_ref, ...), custom_call_target="tpu_custom_call", output_to_operand_aliasing={{}: (5, {})} | custom-call | flops 805306368 | bytes 2097152 | tf_op jit(solution)/shard_map/multiply/pallas_call | solution.py:205
  47.7 2.7 %multiply.6.refs_0_ = f32[2,256,512]{2,1,0:T(8,128)S(1)} custom-call(s32[9]{0:T(128)S(1)} %stack.84.at._, f32[5,4,2,64,256]{4,3,2,1,0:T(8,128)S(1)} %stage.1.own_ref.own, f32[8,4,2,64,256]{4,3,2,1,0:T(8,128)} %bitcast.13.other_ref.other, f32[4,2,64,256]{3,2,1,0:T(8,128)S(1)} %constant_dynamic-update-slice_fusion.2.even_ref, ...), custom_call_target="tpu_custom_call", output_to_operand_aliasing={{}: (5, {})} | custom-call | flops 805306368 | bytes 2097152 | tf_op jit(solution)/shard_map/multiply/pallas_call | solution.py:205
  50.4 2.7 %multiply.7.total = f32[2,256,512]{2,1,0:T(8,128)S(1)} custom-call(s32[9]{0:T(128)S(1)} %stack.84.at._, f32[5,4,2,64,256]{4,3,2,1,0:T(8,128)S(1)} %stage.1.own_ref.own, f32[8,4,2,64,256]{4,3,2,1,0:T(8,128)} %bitcast.13.other_ref.other, f32[4,2,64,256]{3,2,1,0:T(8,128)S(1)} %constant_dynamic-update-slice_fusion.6.even_ref, ...), custom_call_target="tpu_custom_call", output_to_operand_aliasing={{}: (5, {})} | custom-call | flops 805306368 | bytes 2097152 | tf_op jit(solution)/shard_map/multiply/pallas_call | solution.py:205
  54.0 3.5 %last.1 = (f32[2,4,4,24,256]{4,3,2,1,0:T(8,128)S(1)}, f32[2,4,64,512]{3,2,1,0:T(8,128)S(1)}) custom-call(s32[9]{0:T(128)S(1)} %stack.84.at._, f32[5,4,2,64,256]{4,3,2,1,0:T(8,128)S(1)} %stage.1.own_ref.own, f32[8,4,2,64,256]{4,3,2,1,0:T(8,128)} %bitcast.13.other_ref.other, f32[2,2,64,256]{3,2,1,0:T(8,128)S(1)} %collective-permute-done.12.even, ...), custom_call_target="tpu_custom_call" | custom-call | flops 1073741824 | bytes 2097152 | tf_op jit(solution)/shard_map/last/pallas_call | solution.py:248
  61.5 3.9 %invert.1 = (f32[256,256]{1,0:T(8,128)S(1)}, f32[256,256]{1,0:T(8,128)S(1)}) custom-call(s32[9]{0:T(128)S(1)} %stack.84.at._, f32[256,256]{1,0:T(8,128)S(1)} %copy-done, f32[256,256]{1,0:T(8,128)S(1)} %copy-done.1), custom_call_target="tpu_custom_call" | custom-call | flops 4294967296 | bytes 1048576 | tf_op jit(solution)/shard_map/invert/pallas_call | solution.py:307
  67.4 2.0 %collective-permute-start.25 = (f32[2,24,256]{2,1,0:T(8,128)S(1)}, f32[2,24,256]{2,1,0:T(8,128)S(1)}, u32[]{:S(2)}, u32[]{:S(2)}) collective-permute-start(f32[2,24,256]{2,1,0:T(8,128)S(1)} %get-tuple-element.79), channel_id=1, source_target_pairs={{0,192},{1,65},{2,194},{3,67},{4,196},{5,69},{6,198},{7,71},{8,200... | collective-permute-start | bytes 147464 | tf_op jit(solution)/shard_map/ppermute | solution.py:29
  73.5 3.5 %collective-permute-done.27 = f32[2,24,256]{2,1,0:T(8,128)S(1)} collective-permute-done((f32[2,24,256]{2,1,0:T(8,128)S(1)}, f32[2,24,256]{2,1,0:T(8,128)S(1)}, u32[]{:S(2)}, u32[]{:S(2)}) %collective-permute-start.27) | collective-permute-done | bytes 49184 | tf_op jit(solution)/shard_map/ppermute | solution.py:29
  83.8 3.0 %collective-permute-start.32 = (f32[2,24,256]{2,1,0:T(8,128)S(1)}, f32[2,24,256]{2,1,0:T(8,128)S(1)}, u32[]{:S(2)}, u32[]{:S(2)}) collective-permute-start(f32[2,24,256]{2,1,0:T(8,128)S(1)} %add_add_fusion.1), channel_id=1, source_target_pairs={{0,32},{1,33},{2,34},{3,35},{4,36},{5,37},{6,38},{7,39},{8,40},{9,... | collective-permute-start | bytes 147464 | tf_op jit(solution)/shard_map/ppermute | solution.py:29
  88.1 2.2 %collective-permute-start.33 = (f32[2,24,256]{2,1,0:T(8,128)S(1)}, f32[2,24,256]{2,1,0:T(8,128)S(1)}, u32[]{:S(2)}, u32[]{:S(2)}) collective-permute-start(f32[2,24,256]{2,1,0:T(8,128)S(1)} %add_add_fusion.1), channel_id=1, source_target_pairs={{0,48},{1,17},{2,50},{3,19},{4,52},{5,21},{6,54},{7,23},{8,56},{9,... | collective-permute-start | bytes 147464 | tf_op jit(solution)/shard_map/ppermute | solution.py:29
  90.8 3.9 %collective-permute-start.24 = (f32[2,64,256]{2,1,0:T(8,128)S(1)}, f32[2,64,256]{2,1,0:T(8,128)S(1)}, u32[]{:S(2)}, u32[]{:S(2)}) collective-permute-start(f32[2,64,256]{2,1,0:T(8,128)S(1)} %pad_maximum_fusion.7), channel_id=1, source_target_pairs={{0,0},{1,1},{2,128},{3,129},{4,4},{5,5},{6,132},{7,133},{8,8},{9,9... | collective-permute-start | bytes 393224 | tf_op jit(solution)/shard_map/ppermute | solution.py:29
  94.8 1.9 %collective-permute-start.34 = (f32[2,24,256]{2,1,0:T(8,128)S(1)}, f32[2,24,256]{2,1,0:T(8,128)S(1)}, u32[]{:S(2)}, u32[]{:S(2)}) collective-permute-start(f32[2,24,256]{2,1,0:T(8,128)S(1)} %add_add_fusion), channel_id=1, source_target_pairs={{0,2},{1,7},{2,0},{3,5},{4,6},{5,3},{6,4},{7,1},{8,10},{9,15},{10,... | collective-permute-start | bytes 147464 | tf_op jit(solution)/shard_map/ppermute | solution.py:29
  100.4 3.8 %collective-permute-start.36 = (f32[2,24,256]{2,1,0:T(8,128)S(1)}, f32[2,24,256]{2,1,0:T(8,128)S(1)}, u32[]{:S(2)}, u32[]{:S(2)}) collective-permute-start(f32[2,24,256]{2,1,0:T(8,128)S(1)} %add_add_fusion), channel_id=1, source_target_pairs={{0,194},{1,71},{2,192},{3,69},{4,198},{5,67},{6,196},{7,65},{8,202... | collective-permute-start | bytes 147464 | tf_op jit(solution)/shard_map/ppermute | solution.py:29
  104.1 2.8 %collective-permute-done.36 = f32[2,24,256]{2,1,0:T(8,128)S(1)} collective-permute-done((f32[2,24,256]{2,1,0:T(8,128)S(1)}, f32[2,24,256]{2,1,0:T(8,128)S(1)}, u32[]{:S(2)}, u32[]{:S(2)}) %collective-permute-start.36) | collective-permute-done | bytes 49184 | tf_op jit(solution)/shard_map/ppermute | solution.py:29
  107.1 5.7 %collective-permute-done.37 = f32[2,2,2,24,256]{4,3,2,1,0:T(8,128)S(1)} collective-permute-done((f32[2,2,2,24,256]{4,3,2,1,0:T(8,128)S(1)}, f32[2,2,2,24,256]{4,3,2,1,0:T(8,128)S(1)}, u32[]{:S(2)}, u32[]{:S(2)}) %collective-permute-start.37) | collective-permute-done | bytes 196640 | tf_op jit(solution)/shard_map/ppermute | solution.py:29
  114.6 3.2 %finish.1 = (f32[256,256]{1,0:T(8,128)}, f32[256,256]{1,0:T(8,128)}, f32[256,256]{1,0:T(8,128)}) custom-call(s32[9]{0:T(128)S(1)} %stack.84.at._, f32[4,2,2,24,256]{4,3,2,1,0:T(8,128)S(1)} %pad_maximum_fusion.1.mine, f32[4,2,2,24,256]{4,3,2,1,0:T(8,128)S(1)} %collective-permute-done.38.other, bf16[1536,512]{1,0:T(8,128)(2,1)S(1)} %get-tuple-element.63.z_terms, ...), custom_call_target="tpu_custom_call" | custom-call | flops 268435456 | bytes 3145728 | tf_op jit(solution)/shard_map/finish/pallas_call | solution.py:430
  (109 shorter events, 43.6 us)
Async XLA Ops:
  1.6 7.4 %collective-permute-start.1 = (f32[1,2,64,256]{3,2,1,0:T(8,128)S(1)}, f32[1,2,64,256]{3,2,1,0:T(8,128)S(1)}, u32[]{:S(2)}, u32[]{:S(2)}) collective-permute-start(f32[1,2,64,256]{3,2,1,0:T(8,128)S(1)} %maximum_bitcast_fusion), channel_id=1, source_target_pairs={{0,4},{1,5},{2,6},{3,7},{4,0},{5,1},{6,2},{7,3},{8,12},{9,13},{10,... | collective-permute-start | bytes 393224 | tf_op jit(solution)/shard_map/ppermute | solution.py:29
  4.0 10.3 %collective-permute-start.3 = (f32[2,2,64,256]{3,2,1,0:T(8,128)S(1)}, f32[2,2,64,256]{3,2,1,0:T(8,128)S(1)}, u32[]{:S(2)}, u32[]{:S(2)}) collective-permute-start(f32[2,2,64,256]{3,2,1,0:T(8,128)S(1)} %pad_maximum_fusion.4), channel_id=1, source_target_pairs={{0,8},{1,57},{2,10},{3,59},{4,12},{5,61},{6,14},{7,63},{8,16},{9,1... | collective-permute-start | bytes 786440 | tf_op jit(solution)/shard_map/ppermute | solution.py:29
  14.3 20.4 %collective-permute-start.4 = (f32[4096,256]{1,0:T(8,128)}, f32[4096,256]{1,0:T(8,128)}, u32[]{:S(2)}, u32[]{:S(2)}) collective-permute-start(f32[4096,256]{1,0:T(8,128)} %param.6), channel_id=1, source_target_pairs={{0,1},{1,0},{2,3},{3,2},{4,5},{5,4},{6,7},{7,6},{8,9},{9,8},{10,11... | collective-permute-start | bytes 12582920 | tf_op jit(solution)/shard_map/ppermute | solution.py:29
  14.3 7.9 %collective-permute-start.6 = (f32[2,2,64,256]{3,2,1,0:T(8,128)}, f32[2,2,64,256]{3,2,1,0:T(8,128)}, u32[]{:S(2)}, u32[]{:S(2)}) collective-permute-start(f32[2,2,64,256]{3,2,1,0:T(8,128)} %constant_dynamic-update-slice_fusion), channel_id=1, source_target_pairs={{0,8},{1,57},{2,10},{3,59},{4,12},{5,61},{6,14},{7,63},{8,16},{9,1... | collective-permute-start | bytes 786440 | tf_op jit(solution)/shard_map/ppermute | solution.py:29
  14.3 7.9 %collective-permute-start.7 = (f32[2,2,64,256]{3,2,1,0:T(8,128)S(1)}, f32[2,2,64,256]{3,2,1,0:T(8,128)S(1)}, u32[]{:S(2)}, u32[]{:S(2)}) collective-permute-start(f32[2,2,64,256]{3,2,1,0:T(8,128)S(1)} %pad_maximum_fusion.3.even_ref), channel_id=1, source_target_pairs={{0,2},{1,7},{2,4},{3,1},{4,6},{5,3},{6,0},{7,5},{8,10},{9,15},{10,... | collective-permute-start | bytes 786440 | tf_op jit(solution)/shard_map/ppermute | solution.py:29
  14.9 10.1 %collective-permute-start.5 = (f32[2,2,64,256]{3,2,1,0:T(8,128)S(1)}, f32[2,2,64,256]{3,2,1,0:T(8,128)}, u32[]{:S(2)}, u32[]{:S(2)}) collective-permute-start(f32[2,2,64,256]{3,2,1,0:T(8,128)S(1)} %collective-permute-done.3), channel_id=1, source_target_pairs={{0,8},{1,57},{2,10},{3,59},{4,12},{5,61},{6,14},{7,63},{8,16},{9,1... | collective-permute-start | bytes 786440 | tf_op jit(solution)/shard_map/ppermute | solution.py:29
  22.2 8.1 %collective-permute-start.9 = (f32[2,2,64,256]{3,2,1,0:T(8,128)}, f32[2,2,64,256]{3,2,1,0:T(8,128)S(1)}, u32[]{:S(2)}, u32[]{:S(2)}) collective-permute-start(f32[2,2,64,256]{3,2,1,0:T(8,128)} %collective-permute-done.6), channel_id=1, source_target_pairs={{0,8},{1,57},{2,10},{3,59},{4,12},{5,61},{6,14},{7,63},{8,16},{9,1... | collective-permute-start | bytes 786440 | tf_op jit(solution)/shard_map/ppermute | solution.py:29
  25.0 8.3 %collective-permute-start.8 = (f32[2,2,64,256]{3,2,1,0:T(8,128)}, f32[2,2,64,256]{3,2,1,0:T(8,128)S(1)}, u32[]{:S(2)}, u32[]{:S(2)}) collective-permute-start(f32[2,2,64,256]{3,2,1,0:T(8,128)} %collective-permute-done.5), channel_id=1, source_target_pairs={{0,8},{1,57},{2,10},{3,59},{4,12},{5,61},{6,14},{7,63},{8,16},{9,1... | collective-permute-start | bytes 786440 | tf_op jit(solution)/shard_map/ppermute | solution.py:29
  25.1 11.9 %collective-permute-start.11 = (f32[2,2,64,256]{3,2,1,0:T(8,128)S(1)}, f32[2,2,64,256]{3,2,1,0:T(8,128)S(1)}, u32[]{:S(2)}, u32[]{:S(2)}) collective-permute-start(f32[2,2,64,256]{3,2,1,0:T(8,128)S(1)} %pad_maximum_fusion.2), channel_id=1, source_target_pairs={{0,128},{1,129},{2,130},{3,131},{4,132},{5,133},{6,134},{7,135},{8... | collective-permute-start | bytes 786440 | tf_op jit(solution)/shard_map/ppermute | solution.py:29
  29.2 12.0 %collective-permute-start.15 = (f32[4,2,64,256]{3,2,1,0:T(8,128)S(1)}, f32[4,2,64,256]{3,2,1,0:T(8,128)S(1)}, u32[]{:S(2)}, u32[]{:S(2)}) collective-permute-start(f32[4,2,64,256]{3,2,1,0:T(8,128)S(1)} %constant_dynamic-update-slice_fusion.4.even_ref), channel_id=1, source_target_pairs={{0,2},{1,7},{2,4},{3,1},{4,6},{5,3},{6,0},{7,5},{8,10},{9,15},{10,... | collective-permute-start | bytes 1572872 | tf_op jit(solution)/shard_map/ppermute | solution.py:29
  30.3 7.6 %collective-permute-start.10 = (f32[2,2,64,256]{3,2,1,0:T(8,128)S(1)}, f32[2,2,64,256]{3,2,1,0:T(8,128)S(1)}, u32[]{:S(2)}, u32[]{:S(2)}) collective-permute-start(f32[2,2,64,256]{3,2,1,0:T(8,128)S(1)} %collective-permute-done.9), channel_id=1, source_target_pairs={{0,8},{1,57},{2,10},{3,59},{4,12},{5,61},{6,14},{7,63},{8,16},{9,1... | collective-permute-start | bytes 786440 | tf_op jit(solution)/shard_map/ppermute | solution.py:29
  33.4 10.7 %collective-permute-start.14 = (f32[4,2,64,256]{3,2,1,0:T(8,128)S(1)}, f32[4,2,64,256]{3,2,1,0:T(8,128)S(1)}, u32[]{:S(2)}, u32[]{:S(2)}) collective-permute-start(f32[4,2,64,256]{3,2,1,0:T(8,128)S(1)} %constant_dynamic-update-slice_fusion.2.even_ref), channel_id=1, source_target_pairs={{0,2},{1,7},{2,4},{3,1},{4,6},{5,3},{6,0},{7,5},{8,10},{9,15},{10,... | collective-permute-start | bytes 1572872 | tf_op jit(solution)/shard_map/ppermute | solution.py:29
  37.9 7.7 %collective-permute-start.12 = (f32[2,2,64,256]{3,2,1,0:T(8,128)S(1)}, f32[2,2,64,256]{3,2,1,0:T(8,128)S(1)}, u32[]{:S(2)}, u32[]{:S(2)}) collective-permute-start(f32[2,2,64,256]{3,2,1,0:T(8,128)S(1)} %pad_maximum_fusion.5), channel_id=1, source_target_pairs={{0,8},{1,57},{2,10},{3,59},{4,12},{5,61},{6,14},{7,63},{8,16},{9,1... | collective-permute-start | bytes 786440 | tf_op jit(solution)/shard_map/ppermute | solution.py:29
  38.9 7.4 %collective-permute-start.13 = (f32[2,2,64,256]{3,2,1,0:T(8,128)S(1)}, f32[2,2,64,256]{3,2,1,0:T(8,128)S(1)}, u32[]{:S(2)}, u32[]{:S(2)}) collective-permute-start(f32[2,2,64,256]{3,2,1,0:T(8,128)S(1)} %broadcast_select_fusion), channel_id=1, source_target_pairs={{0,64},{1,65},{2,66},{3,67},{4,68},{5,69},{6,70},{7,71},{8,72},{9,... | collective-permute-start | bytes 786440 | tf_op jit(solution)/shard_map/ppermute | solution.py:29
  39.6 10.8 %collective-permute-start.17 = (f32[4,2,64,256]{3,2,1,0:T(8,128)S(1)}, f32[4,2,64,256]{3,2,1,0:T(8,128)S(1)}, u32[]{:S(2)}, u32[]{:S(2)}) collective-permute-start(f32[4,2,64,256]{3,2,1,0:T(8,128)S(1)} %constant_dynamic-update-slice_fusion.6.even_ref), channel_id=1, source_target_pairs={{0,2},{1,7},{2,4},{3,1},{4,6},{5,3},{6,0},{7,5},{8,10},{9,15},{10,... | collective-permute-start | bytes 1572872 | tf_op jit(solution)/shard_map/ppermute | solution.py:29
  46.3 6.8 %collective-permute-start.18 = (f32[4,2,64,256]{3,2,1,0:T(8,128)S(1)}, f32[4,2,64,256]{3,2,1,0:T(8,128)S(1)}, u32[]{:S(2)}, u32[]{:S(2)}) collective-permute-start(f32[4,2,64,256]{3,2,1,0:T(8,128)S(1)} %pad_maximum_fusion.mine), channel_id=1, source_target_pairs={{0,1},{1,0},{2,3},{3,2},{4,5},{5,4},{6,7},{7,6},{8,9},{9,8},{10,11... | collective-permute-start | bytes 1572872 | tf_op jit(solution)/shard_map/ppermute | solution.py:29
  46.4 7.7 %collective-permute-start.16 = (f32[2,2,64,256]{3,2,1,0:T(8,128)S(1)}, f32[2,2,64,256]{3,2,1,0:T(8,128)S(1)}, u32[]{:S(2)}, u32[]{:S(2)}) collective-permute-start(f32[2,2,64,256]{3,2,1,0:T(8,128)S(1)} %collective-permute-done.12.even), channel_id=1, source_target_pairs={{0,2},{1,7},{2,4},{3,1},{4,6},{5,3},{6,0},{7,5},{8,10},{9,15},{10,... | collective-permute-start | bytes 786440 | tf_op jit(solution)/shard_map/ppermute | solution.py:29
  65.6 13.2 %collective-permute-start.20 = (f32[2,64,512]{2,1,0:T(8,128)S(1)}, f32[2,64,512]{2,1,0:T(8,128)S(1)}, u32[]{:S(2)}, u32[]{:S(2)}) collective-permute-start(f32[2,64,512]{2,1,0:T(8,128)S(1)} %slice.81), channel_id=1, source_target_pairs={{0,64},{1,193},{2,66},{3,195},{4,68},{5,197},{6,70},{7,199},{8,72}... | collective-permute-start | bytes 786440 | tf_op jit(solution)/shard_map/ppermute | solution.py:29
  80.7 7.4 %collective-permute-start.21 = (f32[64,512]{1,0:T(8,128)S(1)}, f32[64,512]{1,0:T(8,128)S(1)}, u32[]{:S(2)}, u32[]{:S(2)}) collective-permute-start(f32[64,512]{1,0:T(8,128)S(1)} %get-tuple-element.75), channel_id=1, source_target_pairs={{0,192},{1,65},{2,194},{3,67},{4,196},{5,69},{6,198},{7,71},{8,200... | collective-permute-start | bytes 393224 | tf_op jit(solution)/shard_map/ppermute | solution.py:29
  83.8 10.9 %collective-permute-start.32 = (f32[2,24,256]{2,1,0:T(8,128)S(1)}, f32[2,24,256]{2,1,0:T(8,128)S(1)}, u32[]{:S(2)}, u32[]{:S(2)}) collective-permute-start(f32[2,24,256]{2,1,0:T(8,128)S(1)} %add_add_fusion.1), channel_id=1, source_target_pairs={{0,32},{1,33},{2,34},{3,35},{4,36},{5,37},{6,38},{7,39},{8,40},{9,... | collective-permute-start | bytes 147464 | tf_op jit(solution)/shard_map/ppermute | solution.py:29
  86.8 7.9 %collective-permute-start.31 = (f32[2,24,256]{2,1,0:T(8,128)S(1)}, f32[2,24,256]{2,1,0:T(8,128)S(1)}, u32[]{:S(2)}, u32[]{:S(2)}) collective-permute-start(f32[2,24,256]{2,1,0:T(8,128)S(1)} %add_add_fusion.1), channel_id=1, source_target_pairs={{0,16},{1,49},{2,18},{3,51},{4,20},{5,53},{6,22},{7,55},{8,24},{9,... | collective-permute-start | bytes 147464 | tf_op jit(solution)/shard_map/ppermute | solution.py:29
  90.8 9.6 %collective-permute-start.24 = (f32[2,64,256]{2,1,0:T(8,128)S(1)}, f32[2,64,256]{2,1,0:T(8,128)S(1)}, u32[]{:S(2)}, u32[]{:S(2)}) collective-permute-start(f32[2,64,256]{2,1,0:T(8,128)S(1)} %pad_maximum_fusion.7), channel_id=1, source_target_pairs={{0,0},{1,1},{2,128},{3,129},{4,4},{5,5},{6,132},{7,133},{8,8},{9,9... | collective-permute-start | bytes 393224 | tf_op jit(solution)/shard_map/ppermute | solution.py:29
  94.8 9.3 %collective-permute-start.34 = (f32[2,24,256]{2,1,0:T(8,128)S(1)}, f32[2,24,256]{2,1,0:T(8,128)S(1)}, u32[]{:S(2)}, u32[]{:S(2)}) collective-permute-start(f32[2,24,256]{2,1,0:T(8,128)S(1)} %add_add_fusion), channel_id=1, source_target_pairs={{0,2},{1,7},{2,0},{3,5},{4,6},{5,3},{6,4},{7,1},{8,10},{9,15},{10,... | collective-permute-start | bytes 147464 | tf_op jit(solution)/shard_map/ppermute | solution.py:29
  96.7 7.5 %collective-permute-start.35 = (f32[2,24,256]{2,1,0:T(8,128)S(1)}, f32[2,24,256]{2,1,0:T(8,128)S(1)}, u32[]{:S(2)}, u32[]{:S(2)}) collective-permute-start(f32[2,24,256]{2,1,0:T(8,128)S(1)} %add_add_fusion), channel_id=1, source_target_pairs={{0,192},{1,65},{2,194},{3,67},{4,196},{5,69},{6,198},{7,71},{8,200... | collective-permute-start | bytes 147464 | tf_op jit(solution)/shard_map/ppermute | solution.py:29
  (18 other events, 88.6 us)

commit v7 on v6

--- a/solution.py
+++ b/solution.py
@@ -139,45 +139,49 @@
 SLAB = (NY, 2, Q, B)
 
 
+DEPTHS = (B, 2 * B, 2 * B, 2 * B, B)
+
+
+def fill_slab(at, slab, left, row, depth):
+    y, s = at[1], at[3]
+    half = depth // 2
+    for n, first in enumerate((y, lax.rem(y + 3 + 2 * s, NY))):
+        blocks = [slab[lax.rem(first + 2 * d, NY), core] for d in range(2) for core in (s, 1 - s)[: half // 128]]
+        fill_left(left, row, n * half, jnp.concatenate(blocks, axis=0).T)
+
+
 def stage(place, sigma):
-    def kernel(at, ref, out, sems):
-        copies = [pltpu.make_async_copy(ref.at[at[4 + n]], out.at[n], sems.at[n]) for n in range(5)]
+    def kernel(at, ref, *refs):
+        outs, slabs, sems = refs[:5], refs[5], refs[6]
+        copies = [pltpu.make_async_copy(ref.at[at[4 + n]], slabs.at[n], sems.at[n]) for n in range(5)]
         for copy in copies:
             copy.start()
-        for copy in copies:
+        for n, copy in enumerate(copies):
             copy.wait()
+            fill_slab(at, slabs.at[n], outs[n], 0, DEPTHS[n])
 
     return pl.pallas_call(
         kernel,
         in_specs=[SMEM, HBM],
-        out_specs=VMEM,
-        out_shape=jax.ShapeDtypeStruct((5,) + SLAB, F32),
-        scratch_shapes=[pltpu.SemaphoreType.DMA((5,))],
-        compiler_params=params(4),
+        out_specs=[VMEM] * 5,
+        out_shape=[jax.ShapeDtypeStruct((B, 3 * depth), BF16) for depth in DEPTHS],
+        scratch_shapes=[pltpu.VMEM((5,) + SLAB, F32), pltpu.SemaphoreType.DMA((5,))],
+        compiler_params=params(12),
         cost_estimate=cost(0, 5 << 20),
         name="stage",
     )(place, sigma)
 
 
-def slab_product(at, step, own, other, even, odd, left, right, slabs, sems):
-    y, s, slab = at[1], at[3], at[4 + step]
-    copy = pltpu.make_async_copy(other.at[slab], slabs, sems.at[0])
+def slab_product(at, step, own, other, even, odd, left, right, slab, sems):
+    copy = pltpu.make_async_copy(other.at[at[4 + step]], slab, sems.at[0])
     copy.start()
     depth = even.shape[0] * Q
     for n, ref in enumerate((even, odd)):
         for panel in range(2):
             fill_right(right, n * depth, panel * B, ref[:, panel].reshape(depth, B))
-    near = lax.rem(y + 3 + 2 * s, NY)
-    for o in range(2):
-        if o == 1:
-            copy.wait()
-        for n, first in enumerate((y, near)):
-            blocks = [
-                (slabs if o else own.at[step])[lax.rem(first + 2 * d, NY), core]
-                for d in range(2)
-                for core in (s, 1 - s)[: depth // 128]
-            ]
-            fill_left(left, o * B, n * depth, jnp.concatenate(blocks, axis=0).T)
+    left[:B] = own[...]
+    copy.wait()
+    fill_slab(at, slab, left, B, 2 * depth)
     return product(left[...], right[...])
 
 
@@ -454,7 +458,7 @@
     y2 = send(own, lambda x, y, z, s: (x, y + 2, z, s))
     a1 = along_z(a)
     staged = stage(after(place, a), sigma.reshape(view))
-    y2 = after(y2, a, staged)
+    y2 = after(y2, a, *staged)
     b = jnp.concatenate([y2, to_core(y2)], axis=0)
     b1 = along_z(b)
     a2 = along_z(after(a1, b))
@@ -475,7 +479,7 @@
     z2 = jnp.concatenate([a2, b2], axis=0)
     e2 = along_y(z2)
     a3 = after(a3, b2)
-    total = multiply(place, 0, staged, sigma_other, even, odd)
+    total = multiply(place, 0, staged[0], sigma_other, even, odd)
 
     b3, crossed = after((b3, crossed), b3, crossed, a3, total)
     z4 = along_z(jnp.concatenate([a3[:1], b3[:1]], axis=0))
@@ -483,16 +487,16 @@
     e3 = along_y(z3)
     first = jnp.where(x // 2 == y % 2, pair, crossed)
     second = send(first, lambda x, y, z, s: (x ^ 1, y, z, s))
-    total = multiply(place, 1, staged, sigma_other, z1, e1, total)
+    total = multiply(place, 1, staged[1], sigma_other, z1, e1, total)
 
     z4, second, e2 = after((z4, second, e2), z4, second, e2, total)
     e4 = along_y(z4)
     mine = jnp.concatenate([first, second], axis=0)
     others = to_core(mine)
-    total = multiply(place, 2, staged, sigma_other, z2, e2, total)
+    total = multiply(place, 2, staged[2], sigma_other, z2, e2, total)
     weights = weigh(place, mine, others)
-    total = multiply(place, 3, staged, sigma_other, z3, e3, total)
-    corner, pieces = last(place, staged, sigma_other, z4, e4, total, weights)
+    total = multiply(place, 3, staged[3], sigma_other, z3, e3, total)
+    corner, pieces = last(place, staged[4], sigma_other, z4, e4, total, weights)
 
     part = corner[0] + to_core(corner[1])
     came = swap(part[2:], "x", 0)

time: 120 us -> 120 us (level)
  local copies, waits for them, and re-layouts: 4.25 us -> 5.67 us
    unnamed x10 -> x16, local copies, waits for them, and re-layouts: 1.69 us -> 3.11 us
  transfers between devices with their start and end apart: 39 -> 39, of which waited for: 17 -> 16; matrix products, arithmetic and copies ran while one was open for 4% -> 5% of each run, Pallas kernels for 16% -> 16%
where the time goes in v7:
time: 120 us; the launch traced here: 119 us
  starting transfers between devices  54.4 us (45%)
  waiting for transfers between devices  30.2 us (25%)
  Pallas kernels  25.8 us (22%)
  local copies, waits for them, and re-layouts  5.67 us (5%)
  other arithmetic  1.35 us (1%)
    ppermute x39, starting transfers between devices, send(): return lax.ppermute(block, AXES, pairs)  54.4 us
    ppermute x39, waiting for transfers between devices, send(): return lax.ppermute(block, AXES, pairs)  30.2 us
    pallas_call x4, Pallas kernels, multiply(): pl.pallas_call(kernel, in_specs=[SMEM, VMEM, HBM] + [VMEM] * (2 + len(tot...  9.98 us
    pallas_call x1, Pallas kernels, invert(): pl.pallas_call(invert_kernel, in_specs=[SMEM, HBM, HBM], out_specs=[VMEM,...  3.94 us
    pallas_call x1, Pallas kernels, last(): pl.pallas_call(last_kernel, in_specs=[SMEM, VMEM, HBM] + [VMEM] * 4, out_...  3.54 us
    pallas_call x1, Pallas kernels, finish(): pl.pallas_call(finish_kernel, in_specs=[SMEM] + [VMEM] * 5, out_specs=[VM...  3.23 us
    unnamed x16, local copies, waits for them, and re-layouts  3.11 us
    pallas_call x1, Pallas kernels, stage(): pl.pallas_call(kernel, in_specs=[SMEM, HBM], out_specs=[VMEM] * 5, out_sh...  2.57 us
  transfers between devices with their start and end apart: 39, of which 16 were waited for; matrix products, arithmetic and copies ran while one was open for 5% of the time, Pallas kernels for 16%

profile of v7, /device:TPU:8, one launch (start us, length us, event | category | flops | bytes accessed | tf_op | source)
XLA Modules:
  0.0 118.6 jit_solution(11150276019905225917)
XLA Ops:
  1.6 2.4 %collective-permute-start.1 = (f32[1,2,64,256]{3,2,1,0:T(8,128)S(1)}, f32[1,2,64,256]{3,2,1,0:T(8,128)S(1)}, u32[]{:S(2)}, u32[]{:S(2)}) collective-permute-start(f32[1,2,64,256]{3,2,1,0:T(8,128)S(1)} %maximum_bitcast_fusion), channel_id=1, source_target_pairs={{0,4},{1,5},{2,6},{3,7},{4,0},{5,1},{6,2},{7,3},{8,12},{9,13},{10,... | collective-permute-start | bytes 393224 | tf_op jit(solution)/shard_map/ppermute | solution.py:29
  6.1 2.6 %stage.1 = (bf16[256,768]{1,0:T(8,128)(2,1)S(1)}, bf16[256,1536]{1,0:T(8,128)(2,1)S(1)}, bf16[256,1536]{1,0:T(8,128)(2,1)S(1)}, bf16[256,1536]{1,0:T(8,128)(2,1)S(1)}, bf16[256,768]{1,0:T(8,128)(2,1)S(1)}) custom-call(s32[9]{0:T(128)S(1)} %stack.84.at._, f32[8,4,2,64,256]{4,3,2,1,0:T(8,128)} %bitcast.12.ref), custom_call_target="tpu_custom_call" | custom-call | bytes 5242880 | tf_op jit(solution)/shard_map/stage/pallas_call | solution.py:163
  9.0 3.6 %collective-permute-start.2 = (f32[1,2,64,256]{3,2,1,0:T(8,128)S(1)}, f32[1,2,64,256]{3,2,1,0:T(8,128)S(1)}, u32[]{:S(2)}, u32[]{:S(2)}) collective-permute-start(f32[1,2,64,256]{3,2,1,0:T(8,128)S(1)} %collective-permute-done.1), channel_id=1, source_target_pairs={{0,1},{1,0},{2,3},{3,2},{4,5},{5,4},{6,7},{7,6},{8,9},{9,8},{10,11... | collective-permute-start | bytes 393224 | tf_op jit(solution)/shard_map/ppermute | solution.py:29
  18.3 4.6 %collective-permute-done.6 = f32[2,2,64,256]{3,2,1,0:T(8,128)} collective-permute-done((f32[2,2,64,256]{3,2,1,0:T(8,128)}, f32[2,2,64,256]{3,2,1,0:T(8,128)}, u32[]{:S(2)}, u32[]{:S(2)}) %collective-permute-start.6) | collective-permute-done | bytes 262176 | tf_op jit(solution)/shard_map/ppermute | solution.py:29
  22.9 2.8 %collective-permute-done.5 = f32[2,2,64,256]{3,2,1,0:T(8,128)} collective-permute-done((f32[2,2,64,256]{3,2,1,0:T(8,128)}, f32[2,2,64,256]{3,2,1,0:T(8,128)}, u32[]{:S(2)}, u32[]{:S(2)}) %collective-permute-start.5) | collective-permute-done | bytes 262176 | tf_op jit(solution)/shard_map/ppermute | solution.py:29
  25.8 3.1 %collective-permute-start.11 = (f32[2,2,64,256]{3,2,1,0:T(8,128)S(1)}, f32[2,2,64,256]{3,2,1,0:T(8,128)S(1)}, u32[]{:S(2)}, u32[]{:S(2)}) collective-permute-start(f32[2,2,64,256]{3,2,1,0:T(8,128)S(1)} %pad_maximum_fusion.2), channel_id=1, source_target_pairs={{0,128},{1,129},{2,130},{3,131},{4,132},{5,133},{6,134},{7,135},{8... | collective-permute-start | bytes 786440 | tf_op jit(solution)/shard_map/ppermute | solution.py:29
  30.9 2.0 %collective-permute-start.10 = (f32[2,2,64,256]{3,2,1,0:T(8,128)S(1)}, f32[2,2,64,256]{3,2,1,0:T(8,128)S(1)}, u32[]{:S(2)}, u32[]{:S(2)}) collective-permute-start(f32[2,2,64,256]{3,2,1,0:T(8,128)S(1)} %collective-permute-done.9), channel_id=1, source_target_pairs={{0,8},{1,57},{2,10},{3,59},{4,12},{5,61},{6,14},{7,63},{8,16},{9,1... | collective-permute-start | bytes 786440 | tf_op jit(solution)/shard_map/ppermute | solution.py:29
  35.3 2.2 %multiply.4.refs_0_ = f32[2,256,512]{2,1,0:T(8,128)S(1)} custom-call(s32[9]{0:T(128)S(1)} %stack.84.at._, bf16[256,768]{1,0:T(8,128)(2,1)S(1)} %copy-done.1, f32[8,4,2,64,256]{4,3,2,1,0:T(8,128)} %bitcast.13.other_ref.other, f32[2,2,64,256]{3,2,1,0:T(8,128)S(1)} %pad_maximum_fusion.3.even_ref, f32[2,2,64,256]{3,2,1,0:T(8,128)S(1)} %collective-permute-done.7.odd_ref), custom_call_target="tpu_custom_call" | custom-call | flops 805306368 | bytes 2097152 | tf_op jit(solution)/shard_map/multiply/pallas_call | solution.py:209
  41.9 2.6 %multiply.5.refs_0_ = f32[2,256,512]{2,1,0:T(8,128)S(1)} custom-call(s32[9]{0:T(128)S(1)} %stack.84.at._, bf16[256,1536]{1,0:T(8,128)(2,1)S(1)} %get-tuple-element.48.own_ref, f32[8,4,2,64,256]{4,3,2,1,0:T(8,128)} %bitcast.13.other_ref.other, f32[4,2,64,256]{3,2,1,0:T(8,128)S(1)} %constant_dynamic-update-slice_fusion.4.even_ref, ...), custom_call_target="tpu_custom_call", output_to_operand_aliasing={{}: (5, {})} | custom-call | flops 805306368 | bytes 2097152 | tf_op jit(solution)/shard_map/multiply/pallas_call | solution.py:209
  45.8 2.0 %collective-permute-done.12.even = f32[2,2,64,256]{3,2,1,0:T(8,128)S(1)} collective-permute-done((f32[2,2,64,256]{3,2,1,0:T(8,128)S(1)}, f32[2,2,64,256]{3,2,1,0:T(8,128)S(1)}, u32[]{:S(2)}, u32[]{:S(2)}) %collective-permute-start.12) | collective-permute-done | bytes 262176 | tf_op jit(solution)/shard_map/ppermute | solution.py:29
  49.3 2.6 %multiply.6.refs_0_ = f32[2,256,512]{2,1,0:T(8,128)S(1)} custom-call(s32[9]{0:T(128)S(1)} %stack.84.at._, bf16[256,1536]{1,0:T(8,128)(2,1)S(1)} %get-tuple-element.49.own_ref, f32[8,4,2,64,256]{4,3,2,1,0:T(8,128)} %bitcast.13.other_ref.other, f32[4,2,64,256]{3,2,1,0:T(8,128)S(1)} %constant_dynamic-update-slice_fusion.2.even_ref, ...), custom_call_target="tpu_custom_call", output_to_operand_aliasing={{}: (5, {})} | custom-call | flops 805306368 | bytes 2097152 | tf_op jit(solution)/shard_map/multiply/pallas_call | solution.py:209
  51.9 2.6 %multiply.7.total = f32[2,256,512]{2,1,0:T(8,128)S(1)} custom-call(s32[9]{0:T(128)S(1)} %stack.84.at._, bf16[256,1536]{1,0:T(8,128)(2,1)S(1)} %get-tuple-element.50.own_ref, f32[8,4,2,64,256]{4,3,2,1,0:T(8,128)} %bitcast.13.other_ref.other, f32[4,2,64,256]{3,2,1,0:T(8,128)S(1)} %constant_dynamic-update-slice_fusion.6.even_ref, ...), custom_call_target="tpu_custom_call", output_to_operand_aliasing={{}: (5, {})} | custom-call | flops 805306368 | bytes 2097152 | tf_op jit(solution)/shard_map/multiply/pallas_call | solution.py:209
  55.5 3.5 %last.1 = (f32[2,4,4,24,256]{4,3,2,1,0:T(8,128)S(1)}, f32[2,4,64,512]{3,2,1,0:T(8,128)S(1)}) custom-call(s32[9]{0:T(128)S(1)} %stack.84.at._, bf16[256,768]{1,0:T(8,128)(2,1)S(1)} %get-tuple-element.46.own, f32[8,4,2,64,256]{4,3,2,1,0:T(8,128)} %bitcast.13.other_ref.other, f32[2,2,64,256]{3,2,1,0:T(8,128)S(1)} %collective-permute-done.12.even, ...), custom_call_target="tpu_custom_call" | custom-call | flops 1073741824 | bytes 2097152 | tf_op jit(solution)/shard_map/last/pallas_call | solution.py:252
  62.7 3.9 %invert.1 = (f32[256,256]{1,0:T(8,128)S(1)}, f32[256,256]{1,0:T(8,128)S(1)}) custom-call(s32[9]{0:T(128)S(1)} %stack.84.at._, f32[256,256]{1,0:T(8,128)S(1)} %copy-done.2, f32[256,256]{1,0:T(8,128)S(1)} %copy-done.3), custom_call_target="tpu_custom_call" | custom-call | flops 4294967296 | bytes 1048576 | tf_op jit(solution)/shard_map/invert/pallas_call | solution.py:311
  73.6 3.7 %collective-permute-done.27 = f32[2,24,256]{2,1,0:T(8,128)S(1)} collective-permute-done((f32[2,24,256]{2,1,0:T(8,128)S(1)}, f32[2,24,256]{2,1,0:T(8,128)S(1)}, u32[]{:S(2)}, u32[]{:S(2)}) %collective-permute-start.27) | collective-permute-done | bytes 49184 | tf_op jit(solution)/shard_map/ppermute | solution.py:29
  84.4 2.7 %collective-permute-start.31 = (f32[2,24,256]{2,1,0:T(8,128)S(1)}, f32[2,24,256]{2,1,0:T(8,128)S(1)}, u32[]{:S(2)}, u32[]{:S(2)}) collective-permute-start(f32[2,24,256]{2,1,0:T(8,128)S(1)} %add_add_fusion.1), channel_id=1, source_target_pairs={{0,16},{1,49},{2,18},{3,51},{4,20},{5,53},{6,22},{7,55},{8,24},{9,... | collective-permute-start | bytes 147464 | tf_op jit(solution)/shard_map/ppermute | solution.py:29
  88.5 2.5 %collective-permute-start.33 = (f32[2,24,256]{2,1,0:T(8,128)S(1)}, f32[2,24,256]{2,1,0:T(8,128)S(1)}, u32[]{:S(2)}, u32[]{:S(2)}) collective-permute-start(f32[2,24,256]{2,1,0:T(8,128)S(1)} %add_add_fusion.1), channel_id=1, source_target_pairs={{0,48},{1,17},{2,50},{3,19},{4,52},{5,21},{6,54},{7,23},{8,56},{9,... | collective-permute-start | bytes 147464 | tf_op jit(solution)/shard_map/ppermute | solution.py:29
  91.4 3.9 %collective-permute-start.24 = (f32[2,64,256]{2,1,0:T(8,128)S(1)}, f32[2,64,256]{2,1,0:T(8,128)S(1)}, u32[]{:S(2)}, u32[]{:S(2)}) collective-permute-start(f32[2,64,256]{2,1,0:T(8,128)S(1)} %pad_maximum_fusion.7), channel_id=1, source_target_pairs={{0,0},{1,1},{2,128},{3,129},{4,4},{5,5},{6,132},{7,133},{8,8},{9,9... | collective-permute-start | bytes 393224 | tf_op jit(solution)/shard_map/ppermute | solution.py:29
  95.4 2.1 %collective-permute-start.34 = (f32[2,24,256]{2,1,0:T(8,128)S(1)}, f32[2,24,256]{2,1,0:T(8,128)S(1)}, u32[]{:S(2)}, u32[]{:S(2)}) collective-permute-start(f32[2,24,256]{2,1,0:T(8,128)S(1)} %add_add_fusion), channel_id=1, source_target_pairs={{0,2},{1,7},{2,0},{3,5},{4,6},{5,3},{6,4},{7,1},{8,10},{9,15},{10,... | collective-permute-start | bytes 147464 | tf_op jit(solution)/shard_map/ppermute | solution.py:29
  97.4 2.0 %collective-permute-start.35 = (f32[2,24,256]{2,1,0:T(8,128)S(1)}, f32[2,24,256]{2,1,0:T(8,128)S(1)}, u32[]{:S(2)}, u32[]{:S(2)}) collective-permute-start(f32[2,24,256]{2,1,0:T(8,128)S(1)} %add_add_fusion), channel_id=1, source_target_pairs={{0,192},{1,65},{2,194},{3,67},{4,196},{5,69},{6,198},{7,71},{8,200... | collective-permute-start | bytes 147464 | tf_op jit(solution)/shard_map/ppermute | solution.py:29
  101.1 3.4 %collective-permute-start.36 = (f32[2,24,256]{2,1,0:T(8,128)S(1)}, f32[2,24,256]{2,1,0:T(8,128)S(1)}, u32[]{:S(2)}, u32[]{:S(2)}) collective-permute-start(f32[2,24,256]{2,1,0:T(8,128)S(1)} %add_add_fusion), channel_id=1, source_target_pairs={{0,194},{1,71},{2,192},{3,69},{4,198},{5,67},{6,196},{7,65},{8,202... | collective-permute-start | bytes 147464 | tf_op jit(solution)/shard_map/ppermute | solution.py:29
  104.5 3.2 %collective-permute-done.36 = f32[2,24,256]{2,1,0:T(8,128)S(1)} collective-permute-done((f32[2,24,256]{2,1,0:T(8,128)S(1)}, f32[2,24,256]{2,1,0:T(8,128)S(1)}, u32[]{:S(2)}, u32[]{:S(2)}) %collective-permute-start.36) | collective-permute-done | bytes 49184 | tf_op jit(solution)/shard_map/ppermute | solution.py:29
  107.9 5.7 %collective-permute-done.37 = f32[2,2,2,24,256]{4,3,2,1,0:T(8,128)S(1)} collective-permute-done((f32[2,2,2,24,256]{4,3,2,1,0:T(8,128)S(1)}, f32[2,2,2,24,256]{4,3,2,1,0:T(8,128)S(1)}, u32[]{:S(2)}, u32[]{:S(2)}) %collective-permute-start.37) | collective-permute-done | bytes 196640 | tf_op jit(solution)/shard_map/ppermute | solution.py:29
  115.4 3.2 %finish.1 = (f32[256,256]{1,0:T(8,128)}, f32[256,256]{1,0:T(8,128)}, f32[256,256]{1,0:T(8,128)}) custom-call(s32[9]{0:T(128)S(1)} %stack.84.at._, f32[4,2,2,24,256]{4,3,2,1,0:T(8,128)S(1)} %pad_maximum_fusion.1.mine, f32[4,2,2,24,256]{4,3,2,1,0:T(8,128)S(1)} %collective-permute-done.38.other, bf16[1536,512]{1,0:T(8,128)(2,1)S(1)} %get-tuple-element.73.z_terms, ...), custom_call_target="tpu_custom_call" | custom-call | flops 268435456 | bytes 3145728 | tf_op jit(solution)/shard_map/finish/pallas_call | solution.py:434
  (115 shorter events, 44.5 us)
Async XLA Ops:
  1.6 7.4 %collective-permute-start.1 = (f32[1,2,64,256]{3,2,1,0:T(8,128)S(1)}, f32[1,2,64,256]{3,2,1,0:T(8,128)S(1)}, u32[]{:S(2)}, u32[]{:S(2)}) collective-permute-start(f32[1,2,64,256]{3,2,1,0:T(8,128)S(1)} %maximum_bitcast_fusion), channel_id=1, source_target_pairs={{0,4},{1,5},{2,6},{3,7},{4,0},{5,1},{6,2},{7,3},{8,12},{9,13},{10,... | collective-permute-start | bytes 393224 | tf_op jit(solution)/shard_map/ppermute | solution.py:29
  4.0 10.3 %collective-permute-start.3 = (f32[2,2,64,256]{3,2,1,0:T(8,128)S(1)}, f32[2,2,64,256]{3,2,1,0:T(8,128)S(1)}, u32[]{:S(2)}, u32[]{:S(2)}) collective-permute-start(f32[2,2,64,256]{3,2,1,0:T(8,128)S(1)} %pad_maximum_fusion.4), channel_id=1, source_target_pairs={{0,8},{1,57},{2,10},{3,59},{4,12},{5,61},{6,14},{7,63},{8,16},{9,1... | collective-permute-start | bytes 786440 | tf_op jit(solution)/shard_map/ppermute | solution.py:29
  14.3 21.0 %collective-permute-start.4 = (f32[4096,256]{1,0:T(8,128)}, f32[4096,256]{1,0:T(8,128)}, u32[]{:S(2)}, u32[]{:S(2)}) collective-permute-start(f32[4096,256]{1,0:T(8,128)} %param.6), channel_id=1, source_target_pairs={{0,1},{1,0},{2,3},{3,2},{4,5},{5,4},{6,7},{7,6},{8,9},{9,8},{10,11... | collective-permute-start | bytes 12582920 | tf_op jit(solution)/shard_map/ppermute | solution.py:29
  15.0 7.9 %collective-permute-start.6 = (f32[2,2,64,256]{3,2,1,0:T(8,128)}, f32[2,2,64,256]{3,2,1,0:T(8,128)}, u32[]{:S(2)}, u32[]{:S(2)}) collective-permute-start(f32[2,2,64,256]{3,2,1,0:T(8,128)} %constant_dynamic-update-slice_fusion), channel_id=1, source_target_pairs={{0,8},{1,57},{2,10},{3,59},{4,12},{5,61},{6,14},{7,63},{8,16},{9,1... | collective-permute-start | bytes 786440 | tf_op jit(solution)/shard_map/ppermute | solution.py:29
  15.0 7.9 %collective-permute-start.7 = (f32[2,2,64,256]{3,2,1,0:T(8,128)S(1)}, f32[2,2,64,256]{3,2,1,0:T(8,128)S(1)}, u32[]{:S(2)}, u32[]{:S(2)}) collective-permute-start(f32[2,2,64,256]{3,2,1,0:T(8,128)S(1)} %pad_maximum_fusion.3.even_ref), channel_id=1, source_target_pairs={{0,2},{1,7},{2,4},{3,1},{4,6},{5,3},{6,0},{7,5},{8,10},{9,15},{10,... | collective-permute-start | bytes 786440 | tf_op jit(solution)/shard_map/ppermute | solution.py:29
  15.6 10.1 %collective-permute-start.5 = (f32[2,2,64,256]{3,2,1,0:T(8,128)}, f32[2,2,64,256]{3,2,1,0:T(8,128)}, u32[]{:S(2)}, u32[]{:S(2)}) collective-permute-start(f32[2,2,64,256]{3,2,1,0:T(8,128)} %copy-done.5), channel_id=1, source_target_pairs={{0,8},{1,57},{2,10},{3,59},{4,12},{5,61},{6,14},{7,63},{8,16},{9,1... | collective-permute-start | bytes 786440 | tf_op jit(solution)/shard_map/ppermute | solution.py:29
  22.9 8.0 %collective-permute-start.9 = (f32[2,2,64,256]{3,2,1,0:T(8,128)}, f32[2,2,64,256]{3,2,1,0:T(8,128)S(1)}, u32[]{:S(2)}, u32[]{:S(2)}) collective-permute-start(f32[2,2,64,256]{3,2,1,0:T(8,128)} %collective-permute-done.6), channel_id=1, source_target_pairs={{0,8},{1,57},{2,10},{3,59},{4,12},{5,61},{6,14},{7,63},{8,16},{9,1... | collective-permute-start | bytes 786440 | tf_op jit(solution)/shard_map/ppermute | solution.py:29
  25.7 8.2 %collective-permute-start.8 = (f32[2,2,64,256]{3,2,1,0:T(8,128)}, f32[2,2,64,256]{3,2,1,0:T(8,128)S(1)}, u32[]{:S(2)}, u32[]{:S(2)}) collective-permute-start(f32[2,2,64,256]{3,2,1,0:T(8,128)} %collective-permute-done.5), channel_id=1, source_target_pairs={{0,8},{1,57},{2,10},{3,59},{4,12},{5,61},{6,14},{7,63},{8,16},{9,1... | collective-permute-start | bytes 786440 | tf_op jit(solution)/shard_map/ppermute | solution.py:29
  25.8 11.7 %collective-permute-start.11 = (f32[2,2,64,256]{3,2,1,0:T(8,128)S(1)}, f32[2,2,64,256]{3,2,1,0:T(8,128)S(1)}, u32[]{:S(2)}, u32[]{:S(2)}) collective-permute-start(f32[2,2,64,256]{3,2,1,0:T(8,128)S(1)} %pad_maximum_fusion.2), channel_id=1, source_target_pairs={{0,128},{1,129},{2,130},{3,131},{4,132},{5,133},{6,134},{7,135},{8... | collective-permute-start | bytes 786440 | tf_op jit(solution)/shard_map/ppermute | solution.py:29
  29.9 12.0 %collective-permute-start.15 = (f32[4,2,64,256]{3,2,1,0:T(8,128)S(1)}, f32[4,2,64,256]{3,2,1,0:T(8,128)S(1)}, u32[]{:S(2)}, u32[]{:S(2)}) collective-permute-start(f32[4,2,64,256]{3,2,1,0:T(8,128)S(1)} %constant_dynamic-update-slice_fusion.4.even_ref), channel_id=1, source_target_pairs={{0,2},{1,7},{2,4},{3,1},{4,6},{5,3},{6,0},{7,5},{8,10},{9,15},{10,... | collective-permute-start | bytes 1572872 | tf_op jit(solution)/shard_map/ppermute | solution.py:29
  30.9 7.6 %collective-permute-start.10 = (f32[2,2,64,256]{3,2,1,0:T(8,128)S(1)}, f32[2,2,64,256]{3,2,1,0:T(8,128)S(1)}, u32[]{:S(2)}, u32[]{:S(2)}) collective-permute-start(f32[2,2,64,256]{3,2,1,0:T(8,128)S(1)} %collective-permute-done.9), channel_id=1, source_target_pairs={{0,8},{1,57},{2,10},{3,59},{4,12},{5,61},{6,14},{7,63},{8,16},{9,1... | collective-permute-start | bytes 786440 | tf_op jit(solution)/shard_map/ppermute | solution.py:29
  33.9 10.8 %collective-permute-start.14 = (f32[4,2,64,256]{3,2,1,0:T(8,128)S(1)}, f32[4,2,64,256]{3,2,1,0:T(8,128)S(1)}, u32[]{:S(2)}, u32[]{:S(2)}) collective-permute-start(f32[4,2,64,256]{3,2,1,0:T(8,128)S(1)} %constant_dynamic-update-slice_fusion.2.even_ref), channel_id=1, source_target_pairs={{0,2},{1,7},{2,4},{3,1},{4,6},{5,3},{6,0},{7,5},{8,10},{9,15},{10,... | collective-permute-start | bytes 1572872 | tf_op jit(solution)/shard_map/ppermute | solution.py:29
  38.5 7.2 %collective-permute-start.13 = (f32[2,2,64,256]{3,2,1,0:T(8,128)S(1)}, f32[2,2,64,256]{3,2,1,0:T(8,128)S(1)}, u32[]{:S(2)}, u32[]{:S(2)}) collective-permute-start(f32[2,2,64,256]{3,2,1,0:T(8,128)S(1)} %broadcast_select_fusion), channel_id=1, source_target_pairs={{0,64},{1,65},{2,66},{3,67},{4,68},{5,69},{6,70},{7,71},{8,72},{9,... | collective-permute-start | bytes 786440 | tf_op jit(solution)/shard_map/ppermute | solution.py:29
  39.9 7.8 %collective-permute-start.12 = (f32[2,2,64,256]{3,2,1,0:T(8,128)S(1)}, f32[2,2,64,256]{3,2,1,0:T(8,128)S(1)}, u32[]{:S(2)}, u32[]{:S(2)}) collective-permute-start(f32[2,2,64,256]{3,2,1,0:T(8,128)S(1)} %pad_maximum_fusion.5), channel_id=1, source_target_pairs={{0,8},{1,57},{2,10},{3,59},{4,12},{5,61},{6,14},{7,63},{8,16},{9,1... | collective-permute-start | bytes 786440 | tf_op jit(solution)/shard_map/ppermute | solution.py:29
  40.7 11.3 %collective-permute-start.17 = (f32[4,2,64,256]{3,2,1,0:T(8,128)S(1)}, f32[4,2,64,256]{3,2,1,0:T(8,128)S(1)}, u32[]{:S(2)}, u32[]{:S(2)}) collective-permute-start(f32[4,2,64,256]{3,2,1,0:T(8,128)S(1)} %constant_dynamic-update-slice_fusion.6.even_ref), channel_id=1, source_target_pairs={{0,2},{1,7},{2,4},{3,1},{4,6},{5,3},{6,0},{7,5},{8,10},{9,15},{10,... | collective-permute-start | bytes 1572872 | tf_op jit(solution)/shard_map/ppermute | solution.py:29
  47.9 7.5 %collective-permute-start.16 = (f32[2,2,64,256]{3,2,1,0:T(8,128)S(1)}, f32[2,2,64,256]{3,2,1,0:T(8,128)S(1)}, u32[]{:S(2)}, u32[]{:S(2)}) collective-permute-start(f32[2,2,64,256]{3,2,1,0:T(8,128)S(1)} %collective-permute-done.12.even), channel_id=1, source_target_pairs={{0,2},{1,7},{2,4},{3,1},{4,6},{5,3},{6,0},{7,5},{8,10},{9,15},{10,... | collective-permute-start | bytes 786440 | tf_op jit(solution)/shard_map/ppermute | solution.py:29
  59.4 7.3 %collective-permute-start.19 = (f32[4,64,512]{2,1,0:T(8,128)S(1)}, f32[4,64,512]{2,1,0:T(8,128)S(1)}, u32[]{:S(2)}, u32[]{:S(2)}) collective-permute-start(f32[4,64,512]{2,1,0:T(8,128)S(1)} %slice_bitcast_fusion), channel_id=1, source_target_pairs={{0,1},{1,0},{2,3},{3,2},{4,5},{5,4},{6,7},{7,6},{8,9},{9,8},{10,11... | collective-permute-start | bytes 1572872 | tf_op jit(solution)/shard_map/ppermute | solution.py:29
  66.8 12.6 %collective-permute-start.20 = (f32[2,64,512]{2,1,0:T(8,128)S(1)}, f32[2,64,512]{2,1,0:T(8,128)S(1)}, u32[]{:S(2)}, u32[]{:S(2)}) collective-permute-start(f32[2,64,512]{2,1,0:T(8,128)S(1)} %slice.81), channel_id=1, source_target_pairs={{0,64},{1,193},{2,66},{3,195},{4,68},{5,197},{6,70},{7,199},{8,72}... | collective-permute-start | bytes 786440 | tf_op jit(solution)/shard_map/ppermute | solution.py:29
  81.0 7.4 %collective-permute-start.21 = (f32[64,512]{1,0:T(8,128)S(1)}, f32[64,512]{1,0:T(8,128)S(1)}, u32[]{:S(2)}, u32[]{:S(2)}) collective-permute-start(f32[64,512]{1,0:T(8,128)S(1)} %get-tuple-element.85), channel_id=1, source_target_pairs={{0,192},{1,65},{2,194},{3,67},{4,196},{5,69},{6,198},{7,71},{8,200... | collective-permute-start | bytes 393224 | tf_op jit(solution)/shard_map/ppermute | solution.py:29
  84.4 10.9 %collective-permute-start.31 = (f32[2,24,256]{2,1,0:T(8,128)S(1)}, f32[2,24,256]{2,1,0:T(8,128)S(1)}, u32[]{:S(2)}, u32[]{:S(2)}) collective-permute-start(f32[2,24,256]{2,1,0:T(8,128)S(1)} %add_add_fusion.1), channel_id=1, source_target_pairs={{0,16},{1,49},{2,18},{3,51},{4,20},{5,53},{6,22},{7,55},{8,24},{9,... | collective-permute-start | bytes 147464 | tf_op jit(solution)/shard_map/ppermute | solution.py:29
  87.1 8.2 %collective-permute-start.32 = (f32[2,24,256]{2,1,0:T(8,128)S(1)}, f32[2,24,256]{2,1,0:T(8,128)S(1)}, u32[]{:S(2)}, u32[]{:S(2)}) collective-permute-start(f32[2,24,256]{2,1,0:T(8,128)S(1)} %add_add_fusion.1), channel_id=1, source_target_pairs={{0,32},{1,33},{2,34},{3,35},{4,36},{5,37},{6,38},{7,39},{8,40},{9,... | collective-permute-start | bytes 147464 | tf_op jit(solution)/shard_map/ppermute | solution.py:29
  91.4 9.7 %collective-permute-start.24 = (f32[2,64,256]{2,1,0:T(8,128)S(1)}, f32[2,64,256]{2,1,0:T(8,128)S(1)}, u32[]{:S(2)}, u32[]{:S(2)}) collective-permute-start(f32[2,64,256]{2,1,0:T(8,128)S(1)} %pad_maximum_fusion.7), channel_id=1, source_target_pairs={{0,0},{1,1},{2,128},{3,129},{4,4},{5,5},{6,132},{7,133},{8,8},{9,9... | collective-permute-start | bytes 393224 | tf_op jit(solution)/shard_map/ppermute | solution.py:29
  95.4 9.1 %collective-permute-start.34 = (f32[2,24,256]{2,1,0:T(8,128)S(1)}, f32[2,24,256]{2,1,0:T(8,128)S(1)}, u32[]{:S(2)}, u32[]{:S(2)}) collective-permute-start(f32[2,24,256]{2,1,0:T(8,128)S(1)} %add_add_fusion), channel_id=1, source_target_pairs={{0,2},{1,7},{2,0},{3,5},{4,6},{5,3},{6,4},{7,1},{8,10},{9,15},{10,... | collective-permute-start | bytes 147464 | tf_op jit(solution)/shard_map/ppermute | solution.py:29
  97.4 7.0 %collective-permute-start.35 = (f32[2,24,256]{2,1,0:T(8,128)S(1)}, f32[2,24,256]{2,1,0:T(8,128)S(1)}, u32[]{:S(2)}, u32[]{:S(2)}) collective-permute-start(f32[2,24,256]{2,1,0:T(8,128)S(1)} %add_add_fusion), channel_id=1, source_target_pairs={{0,192},{1,65},{2,194},{3,67},{4,196},{5,69},{6,198},{7,71},{8,200... | collective-permute-start | bytes 147464 | tf_op jit(solution)/shard_map/ppermute | solution.py:29
  (21 other events, 112.6 us)

commit v8 on v5

--- a/solution.py
+++ b/solution.py
@@ -457,7 +457,8 @@
     sigma_other = to_core(after(sigma, b, a1)).reshape(view)
     even = jnp.concatenate([own, after(y2, a1)], axis=0)
     odd = along_y(even)
-    b1, odd = after((b1, odd), b1, odd)
+    x1, x0 = invert(after(place, b, a1), diag_one, diag_zero)
+    b1, odd = after((b1, odd), b1, odd, x1, x0)
     b2 = along_z(b1)
     z1 = jnp.concatenate([a1, b1], axis=0)
     e1 = along_y(z1)
@@ -492,8 +493,7 @@
     part = corner[0] + to_core(corner[1])
     came = swap(part[2:], "x", 0)
     q = pieces[0] + to_core(pieces[1])
-    x1, x0 = invert(after(place, part), diag_one, diag_zero)
-    part = part[:2] + after(came, x1, x0, q)
+    part = part[:2] + after(came, q)
     part = part.reshape(2, 2, 2, N, B)
     a, b, c = to_second_x(part[1, 0]), to_first_y(part[0, 1]), to_both(part[1, 1])
     z_terms, zt_terms, base = constants(x1, x0, after(link, part))

time: 120 us -> 119 us (level)
  local copies, waits for them, and re-layouts: 4.25 us -> 2.72 us
  transfers between devices with their start and end apart: 39 -> 39, of which waited for: 17 -> 19; matrix products, arithmetic and copies ran while one was open for 4% -> 3% of each run, Pallas kernels for 16% -> 16%
where the time goes in v8:
time: 119 us; the launch traced here: 118 us
  starting transfers between devices  54.3 us (46%)
  waiting for transfers between devices  31.6 us (27%)
  Pallas kernels  25.8 us (22%)
  local copies, waits for them, and re-layouts  2.72 us (2%)
  other arithmetic  2.05 us (2%)
    ppermute x39, starting transfers between devices, send(): return lax.ppermute(block, AXES, pairs)  54.3 us
    ppermute x39, waiting for transfers between devices, send(): return lax.ppermute(block, AXES, pairs)  31.6 us
    pallas_call x4, Pallas kernels, multiply(): pl.pallas_call(kernel, in_specs=[SMEM, VMEM, HBM] + [VMEM] * (2 + len(tot...  10.3 us
    pallas_call x1, Pallas kernels, invert(): pl.pallas_call(invert_kernel, in_specs=[SMEM, HBM, HBM], out_specs=[VMEM,...  3.94 us
    pallas_call x1, Pallas kernels, last(): pl.pallas_call(last_kernel, in_specs=[SMEM, VMEM, HBM] + [VMEM] * 4, out_...  3.57 us
    pallas_call x1, Pallas kernels, finish(): pl.pallas_call(finish_kernel, in_specs=[SMEM] + [VMEM] * 5, out_specs=[VM...  3.14 us
  transfers between devices with their start and end apart: 39, of which 19 were waited for; matrix products, arithmetic and copies ran while one was open for 3% of the time, Pallas kernels for 16%

profile of v8, /device:TPU:8, one launch (start us, length us, event | category | flops | bytes accessed | tf_op | source)
XLA Modules:
  0.0 117.6 jit_solution(17740407962036536028)
XLA Ops:
  1.6 2.4 %collective-permute-start.1 = (f32[1,2,64,256]{3,2,1,0:T(8,128)S(1)}, f32[1,2,64,256]{3,2,1,0:T(8,128)S(1)}, u32[]{:S(2)}, u32[]{:S(2)}) collective-permute-start(f32[1,2,64,256]{3,2,1,0:T(8,128)S(1)} %maximum_bitcast_fusion), channel_id=1, source_target_pairs={{0,4},{1,5},{2,6},{3,7},{4,0},{5,1},{6,2},{7,3},{8,12},{9,13},{10,... | collective-permute-start | bytes 393224 | tf_op jit(solution)/shard_map/ppermute | solution.py:29
  6.7 2.3 %stage.1.own_ref.own = f32[5,4,2,64,256]{4,3,2,1,0:T(8,128)S(1)} custom-call(s32[9]{0:T(128)S(1)} %stack.84.at._, f32[8,4,2,64,256]{4,3,2,1,0:T(8,128)} %bitcast.12.ref), custom_call_target="tpu_custom_call" | custom-call | bytes 5242880 | tf_op jit(solution)/shard_map/stage/pallas_call | solution.py:146
  9.0 3.9 %collective-permute-start.2 = (f32[1,2,64,256]{3,2,1,0:T(8,128)S(1)}, f32[1,2,64,256]{3,2,1,0:T(8,128)S(1)}, u32[]{:S(2)}, u32[]{:S(2)}) collective-permute-start(f32[1,2,64,256]{3,2,1,0:T(8,128)S(1)} %collective-permute-done.1), channel_id=1, source_target_pairs={{0,1},{1,0},{2,3},{3,2},{4,5},{5,4},{6,7},{7,6},{8,9},{9,8},{10,11... | collective-permute-start | bytes 393224 | tf_op jit(solution)/shard_map/ppermute | solution.py:29
  17.8 3.9 %invert.1 = (f32[256,256]{1,0:T(8,128)S(1)}, f32[256,256]{1,0:T(8,128)S(1)}) custom-call(s32[9]{0:T(128)S(1)} %stack.84.at._, f32[256,256]{1,0:T(8,128)S(1)} %copy-done, f32[256,256]{1,0:T(8,128)S(1)} %copy-done.1), custom_call_target="tpu_custom_call" | custom-call | flops 4294967296 | bytes 1048576 | tf_op jit(solution)/shard_map/invert/pallas_call | solution.py:303
  27.3 3.1 %collective-permute-start.11 = (f32[2,2,64,256]{3,2,1,0:T(8,128)S(1)}, f32[2,2,64,256]{3,2,1,0:T(8,128)S(1)}, u32[]{:S(2)}, u32[]{:S(2)}) collective-permute-start(f32[2,2,64,256]{3,2,1,0:T(8,128)S(1)} %pad_maximum_fusion.2), channel_id=1, source_target_pairs={{0,128},{1,129},{2,130},{3,131},{4,132},{5,133},{6,134},{7,135},{8... | collective-permute-start | bytes 786440 | tf_op jit(solution)/shard_map/ppermute | solution.py:29
  34.2 2.2 %multiply.4.refs_0_ = f32[2,256,512]{2,1,0:T(8,128)S(1)} custom-call(s32[9]{0:T(128)S(1)} %stack.84.at._, f32[5,4,2,64,256]{4,3,2,1,0:T(8,128)S(1)} %stage.1.own_ref.own, f32[8,4,2,64,256]{4,3,2,1,0:T(8,128)} %bitcast.13.other_ref.other, f32[2,2,64,256]{3,2,1,0:T(8,128)S(1)} %pad_maximum_fusion.3.even_ref, f32[2,2,64,256]{3,2,1,0:T(8,128)S(1)} %collective-permute-done.7.odd_ref), custom_call_target="tpu_custom_call" | custom-call | flops 805306368 | bytes 2097152 | tf_op jit(solution)/shard_map/multiply/pallas_call | solution.py:201
  37.0 2.3 %collective-permute-done.10 = f32[2,2,64,256]{3,2,1,0:T(8,128)S(1)} collective-permute-done((f32[2,2,64,256]{3,2,1,0:T(8,128)S(1)}, f32[2,2,64,256]{3,2,1,0:T(8,128)S(1)}, u32[]{:S(2)}, u32[]{:S(2)}) %collective-permute-start.10) | collective-permute-done | bytes 262176 | tf_op jit(solution)/shard_map/ppermute | solution.py:29
  40.2 2.2 %collective-permute-start.17 = (f32[4,2,64,256]{3,2,1,0:T(8,128)S(1)}, f32[4,2,64,256]{3,2,1,0:T(8,128)S(1)}, u32[]{:S(2)}, u32[]{:S(2)}) collective-permute-start(f32[4,2,64,256]{3,2,1,0:T(8,128)S(1)} %constant_dynamic-update-slice_fusion.6.even_ref), channel_id=1, source_target_pairs={{0,2},{1,7},{2,4},{3,1},{4,6},{5,3},{6,0},{7,5},{8,10},{9,15},{10,... | collective-permute-start | bytes 1572872 | tf_op jit(solution)/shard_map/ppermute | solution.py:29
  42.5 2.7 %multiply.5.refs_0_ = f32[2,256,512]{2,1,0:T(8,128)S(1)} custom-call(s32[9]{0:T(128)S(1)} %stack.84.at._, f32[5,4,2,64,256]{4,3,2,1,0:T(8,128)S(1)} %stage.1.own_ref.own, f32[8,4,2,64,256]{4,3,2,1,0:T(8,128)} %bitcast.13.other_ref.other, f32[4,2,64,256]{3,2,1,0:T(8,128)S(1)} %constant_dynamic-update-slice_fusion.4.even_ref, ...), custom_call_target="tpu_custom_call", output_to_operand_aliasing={{}: (5, {})} | custom-call | flops 805306368 | bytes 2097152 | tf_op jit(solution)/shard_map/multiply/pallas_call | solution.py:201
  47.2 2.2 %collective-permute-start.16 = (f32[2,2,64,256]{3,2,1,0:T(8,128)S(1)}, f32[2,2,64,256]{3,2,1,0:T(8,128)S(1)}, u32[]{:S(2)}, u32[]{:S(2)}) collective-permute-start(f32[2,2,64,256]{3,2,1,0:T(8,128)S(1)} %collective-permute-done.12.even), channel_id=1, source_target_pairs={{0,2},{1,7},{2,4},{3,1},{4,6},{5,3},{6,0},{7,5},{8,10},{9,15},{10,... | collective-permute-start | bytes 786440 | tf_op jit(solution)/shard_map/ppermute | solution.py:29
  49.4 2.7 %multiply.6.refs_0_ = f32[2,256,512]{2,1,0:T(8,128)S(1)} custom-call(s32[9]{0:T(128)S(1)} %stack.84.at._, f32[5,4,2,64,256]{4,3,2,1,0:T(8,128)S(1)} %stage.1.own_ref.own, f32[8,4,2,64,256]{4,3,2,1,0:T(8,128)} %bitcast.13.other_ref.other, f32[4,2,64,256]{3,2,1,0:T(8,128)S(1)} %constant_dynamic-update-slice_fusion.2.even_ref, ...), custom_call_target="tpu_custom_call", output_to_operand_aliasing={{}: (5, {})} | custom-call | flops 805306368 | bytes 2097152 | tf_op jit(solution)/shard_map/multiply/pallas_call | solution.py:201
  52.2 2.7 %multiply.7.total = f32[2,256,512]{2,1,0:T(8,128)S(1)} custom-call(s32[9]{0:T(128)S(1)} %stack.84.at._, f32[5,4,2,64,256]{4,3,2,1,0:T(8,128)S(1)} %stage.1.own_ref.own, f32[8,4,2,64,256]{4,3,2,1,0:T(8,128)} %bitcast.13.other_ref.other, f32[4,2,64,256]{3,2,1,0:T(8,128)S(1)} %constant_dynamic-update-slice_fusion.6.even_ref, ...), custom_call_target="tpu_custom_call", output_to_operand_aliasing={{}: (5, {})} | custom-call | flops 805306368 | bytes 2097152 | tf_op jit(solution)/shard_map/multiply/pallas_call | solution.py:201
  55.8 3.6 %last.1 = (f32[2,4,4,24,256]{4,3,2,1,0:T(8,128)S(1)}, f32[2,4,64,512]{3,2,1,0:T(8,128)S(1)}) custom-call(s32[9]{0:T(128)S(1)} %stack.84.at._, f32[5,4,2,64,256]{4,3,2,1,0:T(8,128)S(1)} %stage.1.own_ref.own, f32[8,4,2,64,256]{4,3,2,1,0:T(8,128)} %bitcast.13.other_ref.other, f32[2,2,64,256]{3,2,1,0:T(8,128)S(1)} %collective-permute-done.12.even, ...), custom_call_target="tpu_custom_call" | custom-call | flops 1073741824 | bytes 2097152 | tf_op jit(solution)/shard_map/last/pallas_call | solution.py:244
  63.8 3.2 %collective-permute-done.23 = f32[2,4,24,256]{3,2,1,0:T(8,128)S(1)} collective-permute-done((f32[2,4,24,256]{3,2,1,0:T(8,128)S(1)}, f32[2,4,24,256]{3,2,1,0:T(8,128)S(1)}, u32[]{:S(2)}, u32[]{:S(2)}) %collective-permute-start.23) | collective-permute-done | bytes 196640 | tf_op jit(solution)/shard_map/ppermute | solution.py:29
  73.2 3.6 %collective-permute-done.27 = f32[2,24,256]{2,1,0:T(8,128)S(1)} collective-permute-done((f32[2,24,256]{2,1,0:T(8,128)S(1)}, f32[2,24,256]{2,1,0:T(8,128)S(1)}, u32[]{:S(2)}, u32[]{:S(2)}) %collective-permute-start.27) | collective-permute-done | bytes 49184 | tf_op jit(solution)/shard_map/ppermute | solution.py:29
  83.4 3.3 %collective-permute-start.32 = (f32[2,24,256]{2,1,0:T(8,128)S(1)}, f32[2,24,256]{2,1,0:T(8,128)S(1)}, u32[]{:S(2)}, u32[]{:S(2)}) collective-permute-start(f32[2,24,256]{2,1,0:T(8,128)S(1)} %add_add_fusion.1), channel_id=1, source_target_pairs={{0,32},{1,33},{2,34},{3,35},{4,36},{5,37},{6,38},{7,39},{8,40},{9,... | collective-permute-start | bytes 147464 | tf_op jit(solution)/shard_map/ppermute | solution.py:29
  88.0 2.2 %collective-permute-start.33 = (f32[2,24,256]{2,1,0:T(8,128)S(1)}, f32[2,24,256]{2,1,0:T(8,128)S(1)}, u32[]{:S(2)}, u32[]{:S(2)}) collective-permute-start(f32[2,24,256]{2,1,0:T(8,128)S(1)} %add_add_fusion.1), channel_id=1, source_target_pairs={{0,48},{1,17},{2,50},{3,19},{4,52},{5,21},{6,54},{7,23},{8,56},{9,... | collective-permute-start | bytes 147464 | tf_op jit(solution)/shard_map/ppermute | solution.py:29
  90.6 3.2 %collective-permute-start.24 = (f32[2,64,256]{2,1,0:T(8,128)S(1)}, f32[2,64,256]{2,1,0:T(8,128)S(1)}, u32[]{:S(2)}, u32[]{:S(2)}) collective-permute-start(f32[2,64,256]{2,1,0:T(8,128)S(1)} %pad_maximum_fusion.7), channel_id=1, source_target_pairs={{0,0},{1,1},{2,128},{3,129},{4,4},{5,5},{6,132},{7,133},{8,8},{9,9... | collective-permute-start | bytes 393224 | tf_op jit(solution)/shard_map/ppermute | solution.py:29
  94.3 2.3 %collective-permute-start.34 = (f32[2,24,256]{2,1,0:T(8,128)S(1)}, f32[2,24,256]{2,1,0:T(8,128)S(1)}, u32[]{:S(2)}, u32[]{:S(2)}) collective-permute-start(f32[2,24,256]{2,1,0:T(8,128)S(1)} %add_add_fusion), channel_id=1, source_target_pairs={{0,2},{1,7},{2,0},{3,5},{4,6},{5,3},{6,4},{7,1},{8,10},{9,15},{10,... | collective-permute-start | bytes 147464 | tf_op jit(solution)/shard_map/ppermute | solution.py:29
  96.6 2.3 %collective-permute-start.35 = (f32[2,24,256]{2,1,0:T(8,128)S(1)}, f32[2,24,256]{2,1,0:T(8,128)S(1)}, u32[]{:S(2)}, u32[]{:S(2)}) collective-permute-start(f32[2,24,256]{2,1,0:T(8,128)S(1)} %add_add_fusion), channel_id=1, source_target_pairs={{0,192},{1,65},{2,194},{3,67},{4,196},{5,69},{6,198},{7,71},{8,200... | collective-permute-start | bytes 147464 | tf_op jit(solution)/shard_map/ppermute | solution.py:29
  100.0 3.4 %collective-permute-start.36 = (f32[2,24,256]{2,1,0:T(8,128)S(1)}, f32[2,24,256]{2,1,0:T(8,128)S(1)}, u32[]{:S(2)}, u32[]{:S(2)}) collective-permute-start(f32[2,24,256]{2,1,0:T(8,128)S(1)} %add_add_fusion), channel_id=1, source_target_pairs={{0,194},{1,71},{2,192},{3,69},{4,198},{5,67},{6,196},{7,65},{8,202... | collective-permute-start | bytes 147464 | tf_op jit(solution)/shard_map/ppermute | solution.py:29
  103.5 3.3 %collective-permute-done.36 = f32[2,24,256]{2,1,0:T(8,128)S(1)} collective-permute-done((f32[2,24,256]{2,1,0:T(8,128)S(1)}, f32[2,24,256]{2,1,0:T(8,128)S(1)}, u32[]{:S(2)}, u32[]{:S(2)}) %collective-permute-start.36) | collective-permute-done | bytes 49184 | tf_op jit(solution)/shard_map/ppermute | solution.py:29
  106.9 5.7 %collective-permute-done.37 = f32[2,2,2,24,256]{4,3,2,1,0:T(8,128)S(1)} collective-permute-done((f32[2,2,2,24,256]{4,3,2,1,0:T(8,128)S(1)}, f32[2,2,2,24,256]{4,3,2,1,0:T(8,128)S(1)}, u32[]{:S(2)}, u32[]{:S(2)}) %collective-permute-start.37) | collective-permute-done | bytes 196640 | tf_op jit(solution)/shard_map/ppermute | solution.py:29
  114.4 3.1 %finish.1 = (f32[256,256]{1,0:T(8,128)}, f32[256,256]{1,0:T(8,128)}, f32[256,256]{1,0:T(8,128)}) custom-call(s32[9]{0:T(128)S(1)} %stack.84.at._, f32[4,2,2,24,256]{4,3,2,1,0:T(8,128)S(1)} %pad_maximum_fusion.1.mine, f32[4,2,2,24,256]{4,3,2,1,0:T(8,128)S(1)} %collective-permute-done.38.other, bf16[1536,512]{1,0:T(8,128)(2,1)S(1)} %get-tuple-element.63.z_terms, ...), custom_call_target="tpu_custom_call" | custom-call | flops 268435456 | bytes 3145728 | tf_op jit(solution)/shard_map/finish/pallas_call | solution.py:425
  (111 shorter events, 44.5 us)
Async XLA Ops:
  1.6 7.4 %collective-permute-start.1 = (f32[1,2,64,256]{3,2,1,0:T(8,128)S(1)}, f32[1,2,64,256]{3,2,1,0:T(8,128)S(1)}, u32[]{:S(2)}, u32[]{:S(2)}) collective-permute-start(f32[1,2,64,256]{3,2,1,0:T(8,128)S(1)} %maximum_bitcast_fusion), channel_id=1, source_target_pairs={{0,4},{1,5},{2,6},{3,7},{4,0},{5,1},{6,2},{7,3},{8,12},{9,13},{10,... | collective-permute-start | bytes 393224 | tf_op jit(solution)/shard_map/ppermute | solution.py:29
  4.7 10.5 %collective-permute-start.3 = (f32[2,2,64,256]{3,2,1,0:T(8,128)}, f32[2,2,64,256]{3,2,1,0:T(8,128)}, u32[]{:S(2)}, u32[]{:S(2)}) collective-permute-start(f32[2,2,64,256]{3,2,1,0:T(8,128)} %pad_maximum_fusion.4), channel_id=1, source_target_pairs={{0,8},{1,57},{2,10},{3,59},{4,12},{5,61},{6,14},{7,63},{8,16},{9,1... | collective-permute-start | bytes 786440 | tf_op jit(solution)/shard_map/ppermute | solution.py:29
  15.2 18.9 %collective-permute-start.4 = (f32[4096,256]{1,0:T(8,128)}, f32[4096,256]{1,0:T(8,128)}, u32[]{:S(2)}, u32[]{:S(2)}) collective-permute-start(f32[4096,256]{1,0:T(8,128)} %param.6), channel_id=1, source_target_pairs={{0,1},{1,0},{2,3},{3,2},{4,5},{5,4},{6,7},{7,6},{8,9},{9,8},{10,11... | collective-permute-start | bytes 12582920 | tf_op jit(solution)/shard_map/ppermute | solution.py:29
  15.2 7.8 %collective-permute-start.6 = (f32[2,2,64,256]{3,2,1,0:T(8,128)}, f32[2,2,64,256]{3,2,1,0:T(8,128)S(1)}, u32[]{:S(2)}, u32[]{:S(2)}) collective-permute-start(f32[2,2,64,256]{3,2,1,0:T(8,128)} %copy-done.3), channel_id=1, source_target_pairs={{0,8},{1,57},{2,10},{3,59},{4,12},{5,61},{6,14},{7,63},{8,16},{9,1... | collective-permute-start | bytes 786440 | tf_op jit(solution)/shard_map/ppermute | solution.py:29
  15.3 7.8 %collective-permute-start.7 = (f32[2,2,64,256]{3,2,1,0:T(8,128)S(1)}, f32[2,2,64,256]{3,2,1,0:T(8,128)S(1)}, u32[]{:S(2)}, u32[]{:S(2)}) collective-permute-start(f32[2,2,64,256]{3,2,1,0:T(8,128)S(1)} %pad_maximum_fusion.3.even_ref), channel_id=1, source_target_pairs={{0,2},{1,7},{2,4},{3,1},{4,6},{5,3},{6,0},{7,5},{8,10},{9,15},{10,... | collective-permute-start | bytes 786440 | tf_op jit(solution)/shard_map/ppermute | solution.py:29
  15.9 10.0 %collective-permute-start.5 = (f32[2,2,64,256]{3,2,1,0:T(8,128)}, f32[2,2,64,256]{3,2,1,0:T(8,128)S(1)}, u32[]{:S(2)}, u32[]{:S(2)}) collective-permute-start(f32[2,2,64,256]{3,2,1,0:T(8,128)} %collective-permute-done.3), channel_id=1, source_target_pairs={{0,8},{1,57},{2,10},{3,59},{4,12},{5,61},{6,14},{7,63},{8,16},{9,1... | collective-permute-start | bytes 786440 | tf_op jit(solution)/shard_map/ppermute | solution.py:29
  23.0 8.7 %collective-permute-start.9 = (f32[2,2,64,256]{3,2,1,0:T(8,128)S(1)}, f32[2,2,64,256]{3,2,1,0:T(8,128)S(1)}, u32[]{:S(2)}, u32[]{:S(2)}) collective-permute-start(f32[2,2,64,256]{3,2,1,0:T(8,128)S(1)} %collective-permute-done.6), channel_id=1, source_target_pairs={{0,8},{1,57},{2,10},{3,59},{4,12},{5,61},{6,14},{7,63},{8,16},{9,1... | collective-permute-start | bytes 786440 | tf_op jit(solution)/shard_map/ppermute | solution.py:29
  25.9 7.6 %collective-permute-start.8 = (f32[2,2,64,256]{3,2,1,0:T(8,128)S(1)}, f32[2,2,64,256]{3,2,1,0:T(8,128)S(1)}, u32[]{:S(2)}, u32[]{:S(2)}) collective-permute-start(f32[2,2,64,256]{3,2,1,0:T(8,128)S(1)} %collective-permute-done.5), channel_id=1, source_target_pairs={{0,8},{1,57},{2,10},{3,59},{4,12},{5,61},{6,14},{7,63},{8,16},{9,1... | collective-permute-start | bytes 786440 | tf_op jit(solution)/shard_map/ppermute | solution.py:29
  27.3 9.7 %collective-permute-start.11 = (f32[2,2,64,256]{3,2,1,0:T(8,128)S(1)}, f32[2,2,64,256]{3,2,1,0:T(8,128)S(1)}, u32[]{:S(2)}, u32[]{:S(2)}) collective-permute-start(f32[2,2,64,256]{3,2,1,0:T(8,128)S(1)} %pad_maximum_fusion.2), channel_id=1, source_target_pairs={{0,128},{1,129},{2,130},{3,131},{4,132},{5,133},{6,134},{7,135},{8... | collective-permute-start | bytes 786440 | tf_op jit(solution)/shard_map/ppermute | solution.py:29
  30.4 12.1 %collective-permute-start.15 = (f32[4,2,64,256]{3,2,1,0:T(8,128)S(1)}, f32[4,2,64,256]{3,2,1,0:T(8,128)S(1)}, u32[]{:S(2)}, u32[]{:S(2)}) collective-permute-start(f32[4,2,64,256]{3,2,1,0:T(8,128)S(1)} %constant_dynamic-update-slice_fusion.4.even_ref), channel_id=1, source_target_pairs={{0,2},{1,7},{2,4},{3,1},{4,6},{5,3},{6,0},{7,5},{8,10},{9,15},{10,... | collective-permute-start | bytes 1572872 | tf_op jit(solution)/shard_map/ppermute | solution.py:29
  31.8 7.6 %collective-permute-start.10 = (f32[2,2,64,256]{3,2,1,0:T(8,128)S(1)}, f32[2,2,64,256]{3,2,1,0:T(8,128)S(1)}, u32[]{:S(2)}, u32[]{:S(2)}) collective-permute-start(f32[2,2,64,256]{3,2,1,0:T(8,128)S(1)} %collective-permute-done.9), channel_id=1, source_target_pairs={{0,8},{1,57},{2,10},{3,59},{4,12},{5,61},{6,14},{7,63},{8,16},{9,1... | collective-permute-start | bytes 786440 | tf_op jit(solution)/shard_map/ppermute | solution.py:29
  33.5 11.8 %collective-permute-start.14 = (f32[4,2,64,256]{3,2,1,0:T(8,128)S(1)}, f32[4,2,64,256]{3,2,1,0:T(8,128)S(1)}, u32[]{:S(2)}, u32[]{:S(2)}) collective-permute-start(f32[4,2,64,256]{3,2,1,0:T(8,128)S(1)} %constant_dynamic-update-slice_fusion.2.even_ref), channel_id=1, source_target_pairs={{0,2},{1,7},{2,4},{3,1},{4,6},{5,3},{6,0},{7,5},{8,10},{9,15},{10,... | collective-permute-start | bytes 1572872 | tf_op jit(solution)/shard_map/ppermute | solution.py:29
  39.4 7.7 %collective-permute-start.12 = (f32[2,2,64,256]{3,2,1,0:T(8,128)S(1)}, f32[2,2,64,256]{3,2,1,0:T(8,128)S(1)}, u32[]{:S(2)}, u32[]{:S(2)}) collective-permute-start(f32[2,2,64,256]{3,2,1,0:T(8,128)S(1)} %pad_maximum_fusion.5), channel_id=1, source_target_pairs={{0,8},{1,57},{2,10},{3,59},{4,12},{5,61},{6,14},{7,63},{8,16},{9,1... | collective-permute-start | bytes 786440 | tf_op jit(solution)/shard_map/ppermute | solution.py:29
  39.5 7.6 %collective-permute-start.13 = (f32[2,2,64,256]{3,2,1,0:T(8,128)S(1)}, f32[2,2,64,256]{3,2,1,0:T(8,128)S(1)}, u32[]{:S(2)}, u32[]{:S(2)}) collective-permute-start(f32[2,2,64,256]{3,2,1,0:T(8,128)S(1)} %broadcast_select_fusion), channel_id=1, source_target_pairs={{0,64},{1,65},{2,66},{3,67},{4,68},{5,69},{6,70},{7,71},{8,72},{9,... | collective-permute-start | bytes 786440 | tf_op jit(solution)/shard_map/ppermute | solution.py:29
  40.2 11.9 %collective-permute-start.17 = (f32[4,2,64,256]{3,2,1,0:T(8,128)S(1)}, f32[4,2,64,256]{3,2,1,0:T(8,128)S(1)}, u32[]{:S(2)}, u32[]{:S(2)}) collective-permute-start(f32[4,2,64,256]{3,2,1,0:T(8,128)S(1)} %constant_dynamic-update-slice_fusion.6.even_ref), channel_id=1, source_target_pairs={{0,2},{1,7},{2,4},{3,1},{4,6},{5,3},{6,0},{7,5},{8,10},{9,15},{10,... | collective-permute-start | bytes 1572872 | tf_op jit(solution)/shard_map/ppermute | solution.py:29
  47.1 7.8 %collective-permute-start.18 = (f32[4,2,64,256]{3,2,1,0:T(8,128)S(1)}, f32[4,2,64,256]{3,2,1,0:T(8,128)S(1)}, u32[]{:S(2)}, u32[]{:S(2)}) collective-permute-start(f32[4,2,64,256]{3,2,1,0:T(8,128)S(1)} %pad_maximum_fusion.mine), channel_id=1, source_target_pairs={{0,1},{1,0},{2,3},{3,2},{4,5},{5,4},{6,7},{7,6},{8,9},{9,8},{10,11... | collective-permute-start | bytes 1572872 | tf_op jit(solution)/shard_map/ppermute | solution.py:29
  47.2 8.6 %collective-permute-start.16 = (f32[2,2,64,256]{3,2,1,0:T(8,128)S(1)}, f32[2,2,64,256]{3,2,1,0:T(8,128)S(1)}, u32[]{:S(2)}, u32[]{:S(2)}) collective-permute-start(f32[2,2,64,256]{3,2,1,0:T(8,128)S(1)} %collective-permute-done.12.even), channel_id=1, source_target_pairs={{0,2},{1,7},{2,4},{3,1},{4,6},{5,3},{6,0},{7,5},{8,10},{9,15},{10,... | collective-permute-start | bytes 786440 | tf_op jit(solution)/shard_map/ppermute | solution.py:29
  62.2 16.2 %collective-permute-start.20 = (f32[2,64,512]{2,1,0:T(8,128)S(1)}, f32[2,64,512]{2,1,0:T(8,128)S(1)}, u32[]{:S(2)}, u32[]{:S(2)}) collective-permute-start(f32[2,64,512]{2,1,0:T(8,128)S(1)} %slice.81), channel_id=1, source_target_pairs={{0,64},{1,193},{2,66},{3,195},{4,68},{5,197},{6,70},{7,199},{8,72}... | collective-permute-start | bytes 786440 | tf_op jit(solution)/shard_map/ppermute | solution.py:29
  80.4 7.6 %collective-permute-start.21 = (f32[64,512]{1,0:T(8,128)S(1)}, f32[64,512]{1,0:T(8,128)S(1)}, u32[]{:S(2)}, u32[]{:S(2)}) collective-permute-start(f32[64,512]{1,0:T(8,128)S(1)} %get-tuple-element.75), channel_id=1, source_target_pairs={{0,192},{1,65},{2,194},{3,67},{4,196},{5,69},{6,198},{7,71},{8,200... | collective-permute-start | bytes 393224 | tf_op jit(solution)/shard_map/ppermute | solution.py:29
  83.4 10.4 %collective-permute-start.32 = (f32[2,24,256]{2,1,0:T(8,128)S(1)}, f32[2,24,256]{2,1,0:T(8,128)S(1)}, u32[]{:S(2)}, u32[]{:S(2)}) collective-permute-start(f32[2,24,256]{2,1,0:T(8,128)S(1)} %add_add_fusion.1), channel_id=1, source_target_pairs={{0,32},{1,33},{2,34},{3,35},{4,36},{5,37},{6,38},{7,39},{8,40},{9,... | collective-permute-start | bytes 147464 | tf_op jit(solution)/shard_map/ppermute | solution.py:29
  86.7 7.1 %collective-permute-start.31 = (f32[2,24,256]{2,1,0:T(8,128)S(1)}, f32[2,24,256]{2,1,0:T(8,128)S(1)}, u32[]{:S(2)}, u32[]{:S(2)}) collective-permute-start(f32[2,24,256]{2,1,0:T(8,128)S(1)} %add_add_fusion.1), channel_id=1, source_target_pairs={{0,16},{1,49},{2,18},{3,51},{4,20},{5,53},{6,22},{7,55},{8,24},{9,... | collective-permute-start | bytes 147464 | tf_op jit(solution)/shard_map/ppermute | solution.py:29
  90.6 9.4 %collective-permute-start.24 = (f32[2,64,256]{2,1,0:T(8,128)S(1)}, f32[2,64,256]{2,1,0:T(8,128)S(1)}, u32[]{:S(2)}, u32[]{:S(2)}) collective-permute-start(f32[2,64,256]{2,1,0:T(8,128)S(1)} %pad_maximum_fusion.7), channel_id=1, source_target_pairs={{0,0},{1,1},{2,128},{3,129},{4,4},{5,5},{6,132},{7,133},{8,8},{9,9... | collective-permute-start | bytes 393224 | tf_op jit(solution)/shard_map/ppermute | solution.py:29
  94.3 9.1 %collective-permute-start.34 = (f32[2,24,256]{2,1,0:T(8,128)S(1)}, f32[2,24,256]{2,1,0:T(8,128)S(1)}, u32[]{:S(2)}, u32[]{:S(2)}) collective-permute-start(f32[2,24,256]{2,1,0:T(8,128)S(1)} %add_add_fusion), channel_id=1, source_target_pairs={{0,2},{1,7},{2,0},{3,5},{4,6},{5,3},{6,4},{7,1},{8,10},{9,15},{10,... | collective-permute-start | bytes 147464 | tf_op jit(solution)/shard_map/ppermute | solution.py:29
  96.6 6.9 %collective-permute-start.35 = (f32[2,24,256]{2,1,0:T(8,128)S(1)}, f32[2,24,256]{2,1,0:T(8,128)S(1)}, u32[]{:S(2)}, u32[]{:S(2)}) collective-permute-start(f32[2,24,256]{2,1,0:T(8,128)S(1)} %add_add_fusion), channel_id=1, source_target_pairs={{0,192},{1,65},{2,194},{3,67},{4,196},{5,69},{6,198},{7,71},{8,200... | collective-permute-start | bytes 147464 | tf_op jit(solution)/shard_map/ppermute | solution.py:29
  (19 other events, 103.7 us)
